TPU v7x, 32 devices: a whole 2x2x4 slice. The times are simulated.
32 devices in a mesh: ctx: 8 (over z, y), wt: 4 (over x, core).
Axes of the slice: x: 2, y: 2, z: 4, core: 2. Of those that a mesh axis runs over, the one named last changes fastest.
Arguments:
- residual_in: bfloat16 [4, 3072, 768], P('wt', 'ctx')
- cotangent: bfloat16 [4, 3072, 768], P('wt', 'ctx'), may hold values from -6 to 6
- block_order: int32 [8], replicated, may hold values from 0 to 7, each once
- doc_starts: int32 [4, 3], P('wt'), may hold values from 0 to 3071, as said below
- gain_attn: bfloat16 [768], P('wt'), may hold values from 0.5 to 1.5
- w_query: bfloat16 [768, 768], P('wt'), may hold values from -0.21875 to 0.21875
- w_key: bfloat16 [768, 768], P('wt'), may hold values from -0.21875 to 0.21875
- w_value: bfloat16 [768, 768], P('wt'), may hold values from -0.21875 to 0.21875
- mix_logit: bfloat16 [12, 12], P('wt'), may hold values from -3.5 to 3.5
- mix_weight: bfloat16 [12, 12], P('wt'), may hold values from -1.75 to 1.75
- w_output: bfloat16 [768, 768], P('wt'), may hold values from -1.5 to 1.5
- gain_ffn: bfloat16 [768], P('wt'), may hold values from 0.5 to 1.5
- w_in: bfloat16 [768, 3072], P('wt'), may hold values from -0.21875 to 0.21875
- w_out: bfloat16 [3072, 768], P('wt'), may hold values from -0.109375 to 0.109375
Outputs:
- output: bfloat16 [4, 3072, 768], P('wt', 'ctx')
- input_grad: bfloat16 [4, 3072, 768], P('wt', 'ctx')
- rms_values: float32 [3], replicated
- grad_gain_attn: float32 [768], P('wt')
- grad_w_query: float32 [768, 768], P('wt')
- grad_w_key: float32 [768, 768], P('wt')
- grad_w_value: float32 [768, 768], P('wt')
- grad_mix_logit: float32 [12, 12], P('wt')
- grad_mix_weight: float32 [12, 12], P('wt')
- grad_w_output: float32 [768, 768], P('wt')
- grad_gain_ffn: float32 [768], P('wt')
- grad_w_in: float32 [768, 3072], P('wt')
- grad_w_out: float32 [3072, 768], P('wt')
Inputs may be any that keep to these rules, and one draw needn't show every extreme that they name: `block_order`: each number once. `doc_starts`: each row rises: 0, then a start below 384, then one above 2688.
All inputs are finite; a program needn't handle non-finite values.
Results may differ from a plain program's by a relative error of at most 0.02.
Values may be sent and summed in bfloat16 or wider, within the bound.
No kernel may reach another device: no remote copies, remote signals or barrier semaphores. Data moves between devices by JAX's collectives and lax.ppermute only.
A program may use at most 256 MiB of HBM per device.

v0:
```python
import jax
import jax.numpy as jnp
from jax import lax
from jax.sharding import PartitionSpec as P

NEG = -1e30
EPS = 1e-06
HIGH = lax.Precision.HIGHEST


def shifted(value, axis, steps):
    count = lax.axis_size(axis)
    pairs = [(source, (source + steps) % count) for source in range(count)]
    return lax.ppermute(value, axis, pairs)


def rms_norm(values, gain):
    return values * lax.rsqrt(jnp.mean(values * values, axis=-1, keepdims=True) + EPS) * gain


def gelu_tanh(values):
    return jax.nn.gelu(values, approximate=True)


def block_size(total):
    largest = 1
    for divisor in range(1, min(total, 768) + 1):
        if total % divisor == 0:
            largest = divisor
    return largest


def key_places(first, length, tok_rows, order, starts):
    row_index = first + jnp.arange(length, dtype=jnp.int32)
    owner_dev = row_index // tok_rows
    device_ids = jnp.arange(order.shape[0], dtype=jnp.int32)
    blocks = jnp.sum(
        jnp.where(owner_dev[:, None] == device_ids[None, :], order[None, :], 0), axis=1
    )
    places = blocks * tok_rows + row_index % tok_rows
    doc_ids = (places >= starts[1]).astype(jnp.int32) + (places >= starts[2]).astype(jnp.int32)
    return (places, doc_ids)


def sweep(step, carry, arrays, first):
    length = arrays[0].shape[0]
    size_block = block_size(length)
    number = length // size_block
    pieces = tuple((member.reshape((number, size_block) + member.shape[1:]) for member in arrays))
    offsets = first + size_block * jnp.arange(number, dtype=jnp.int32)

    def advance(running, scan_entry):
        return step(running, scan_entry[0], scan_entry[1])

    return lax.scan(advance, carry, (pieces, offsets))


def shards(
    residual_in,
    cotangent,
    block_order,
    doc_starts,
    gain_attn,
    w_query,
    w_key,
    w_value,
    mix_logit,
    mix_weight,
    w_output,
    gain_ffn,
    w_in,
    w_out,
):
    (
        gain_one,
        query_mat,
        key_mat,
        value_mat,
        logit_mix,
        weight_mix,
        output_mat,
        gain_two,
        inner_mat,
        outer_mat,
    ) = (
        lax.all_gather(gain_attn, "wt", axis=0, tiled=True),
        lax.all_gather(w_query, "wt", axis=0, tiled=True),
        lax.all_gather(w_key, "wt", axis=0, tiled=True),
        lax.all_gather(w_value, "wt", axis=0, tiled=True),
        lax.all_gather(mix_logit, "wt", axis=0, tiled=True),
        lax.all_gather(mix_weight, "wt", axis=0, tiled=True),
        lax.all_gather(w_output, "wt", axis=0, tiled=True),
        lax.all_gather(gain_ffn, "wt", axis=0, tiled=True),
        lax.all_gather(w_in, "wt", axis=0, tiled=True),
        lax.all_gather(w_out, "wt", axis=0, tiled=True),
    )
    tok_rows = residual_in.shape[1]
    model_width = residual_in.shape[2]
    head_count = logit_mix.shape[0]
    head_size = model_width // head_count
    score_scale = head_size ** (-0.5)
    cycle_size = lax.axis_size("ctx")
    my_index = lax.axis_index("ctx")
    starts = doc_starts[0]
    logit_mix_f = logit_mix.astype(jnp.float32)
    weight_mix_f = weight_mix.astype(jnp.float32)
    query_places, query_docs = key_places(
        my_index * tok_rows, tok_rows, tok_rows, block_order, starts
    )
    inputs = residual_in[0].astype(jnp.float32)
    normed, norm_back = jax.vjp(rms_norm, inputs, gain_one.astype(jnp.float32))
    normed_low = normed.astype(jnp.bfloat16)
    queries = jnp.dot(normed_low, query_mat, preferred_element_type=jnp.float32).astype(
        jnp.bfloat16
    )
    keys = jnp.dot(normed_low, key_mat, preferred_element_type=jnp.float32).astype(jnp.bfloat16)
    values = jnp.dot(normed_low, value_mat, preferred_element_type=jnp.float32).astype(jnp.bfloat16)
    query_heads = queries.reshape(tok_rows, head_count, head_size)
    key_value = jnp.stack([keys, values])

    def visibility(first, length):
        key_pos, key_doc = key_places(first, length, tok_rows, block_order, starts)
        return (key_pos[None, :] <= query_places[:, None]) & (
            key_doc[None, :] == query_docs[:, None]
        )

    def logits_for(key_heads, visible):
        scores = (
            jnp.einsum("qhd,khd->hqk", query_heads, key_heads, preferred_element_type=jnp.float32)
            * score_scale
        )
        logits = jnp.einsum("hqk,hg->gqk", scores, logit_mix_f, precision=HIGH)
        return (scores, jnp.where(visible[None], logits, NEG))

    def stats_step(running, members, first):
        key_heads = members[0].reshape(members[0].shape[0], head_count, head_size)
        visible = visibility(first, members[0].shape[0])

        def stats_compute(current):
            scores, logits = logits_for(key_heads, visible)
            top_new = jnp.maximum(current[0], jnp.max(logits, axis=-1))
            terms = jnp.where(visible[None], jnp.exp(logits - top_new[:, :, None]), 0.0)
            return (top_new, current[1] * jnp.exp(current[0] - top_new) + jnp.sum(terms, axis=-1))

        return (lax.cond(jnp.any(visible), stats_compute, lambda current: current, running), None)

    start_stats = (
        jnp.full((head_count, tok_rows), NEG, jnp.float32),
        jnp.zeros((head_count, tok_rows), jnp.float32),
    )
    top_all, total_all = sweep(
        stats_step, start_stats, (lax.all_gather(keys, "ctx", axis=0, tiled=True),), jnp.int32(0)
    )[0]
    log_total = top_all + jnp.log(total_all)

    def probabilities(key_heads, visible):
        scores, logits = logits_for(key_heads, visible)
        return (scores, jnp.exp(logits - log_total[:, :, None]))

    def value_step(running, members, first):
        length = members[0].shape[0]
        key_heads = members[0].reshape(length, head_count, head_size)
        value_heads = members[1].reshape(length, head_count, head_size)
        visible = visibility(first, length)

        def value_compute(current):
            scores, probability = probabilities(key_heads, visible)
            mixed_w = jnp.einsum("gqk,gh->hqk", probability, weight_mix_f, precision=HIGH).astype(
                jnp.bfloat16
            )
            attended = current[0] + jnp.einsum(
                "hqk,khd->qhd", mixed_w, value_heads, preferred_element_type=jnp.float32
            )
            pair_sum = current[1]
            return (attended, pair_sum)

        return (lax.cond(jnp.any(visible), value_compute, lambda current: current, running), None)

    pair_start = jnp.zeros((1,), jnp.float32)
    piece = lax.all_gather(key_value, "ctx", axis=1, tiled=True)
    attended, pair_sum = sweep(
        value_step,
        (jnp.zeros((tok_rows, head_count, head_size), jnp.float32), pair_start),
        (piece[0], piece[1]),
        jnp.int32(0),
    )[0]
    attended_low = attended.reshape(tok_rows, model_width).astype(jnp.bfloat16)
    branch = jnp.dot(attended_low, output_mat, preferred_element_type=jnp.float32)
    middle = inputs + branch
    normed_two, norm_two_back = jax.vjp(rms_norm, middle, gain_two.astype(jnp.float32))
    normed_two_low = normed_two.astype(jnp.bfloat16)
    hidden = jnp.dot(normed_two_low, inner_mat, preferred_element_type=jnp.float32)
    active, gelu_back = jax.vjp(gelu_tanh, hidden)
    active_low = active.astype(jnp.bfloat16)
    feed = jnp.dot(active_low, outer_mat, preferred_element_type=jnp.float32)
    output = middle + feed
    sums = lax.psum(
        jnp.stack([jnp.sum(output * output), jnp.sum(branch * branch), jnp.sum(feed * feed)]),
        ("ctx", "wt"),
    )
    entries = float(tok_rows * model_width * cycle_size * lax.axis_size("wt"))
    rms_values = jnp.sqrt(sums / entries)
    grad_out = cotangent[0].astype(jnp.float32)
    grad_feed_low = cotangent[0]
    grad_outer = jnp.einsum(
        "ti,to->io", active_low, grad_feed_low, preferred_element_type=jnp.float32
    )
    grad_active = jnp.einsum(
        "to,io->ti", grad_feed_low, outer_mat, preferred_element_type=jnp.float32
    )
    grad_hidden_low = gelu_back(grad_active)[0].astype(jnp.bfloat16)
    grad_inner = jnp.einsum(
        "ti,tf->if", normed_two_low, grad_hidden_low, preferred_element_type=jnp.float32
    )
    grad_normed_two = jnp.einsum(
        "tf,if->ti", grad_hidden_low, inner_mat, preferred_element_type=jnp.float32
    )
    grad_mid_norm, grad_gain_two = norm_two_back(grad_normed_two)
    grad_middle = grad_out + grad_mid_norm
    grad_branch_low = grad_middle.astype(jnp.bfloat16)
    grad_output_mat = jnp.einsum(
        "ti,to->io", attended_low, grad_branch_low, preferred_element_type=jnp.float32
    )
    grad_attended_low = jnp.einsum(
        "to,io->ti", grad_branch_low, output_mat, preferred_element_type=jnp.float32
    ).astype(jnp.bfloat16)
    grad_heads = grad_attended_low.reshape(tok_rows, head_count, head_size)

    def delta_step(running, members, first):
        length = members[0].shape[0]
        key_heads = members[0].reshape(length, head_count, head_size)
        value_heads = members[1].reshape(length, head_count, head_size)
        visible = visibility(first, length)

        def delta_compute(current):
            scores, probability = probabilities(key_heads, visible)
            grad_mixed = jnp.einsum(
                "qhd,khd->hqk", grad_heads, value_heads, preferred_element_type=jnp.float32
            )
            grad_probs = jnp.einsum("hqk,gh->gqk", grad_mixed, weight_mix_f, precision=HIGH)
            return current + jnp.sum(probability * grad_probs, axis=-1)

        return (lax.cond(jnp.any(visible), delta_compute, lambda current: current, running), None)

    piece = lax.all_gather(key_value, "ctx", axis=1, tiled=True)
    delta = sweep(
        delta_step,
        jnp.zeros((head_count, tok_rows), jnp.float32),
        (piece[0], piece[1]),
        jnp.int32(0),
    )[0]

    def back_step(running, members, first):
        length = members[0].shape[0]
        key_heads = members[0].reshape(length, head_count, head_size)
        value_heads = members[1].reshape(length, head_count, head_size)
        visible = visibility(first, length)

        def back_compute(current):
            scores, probability = probabilities(key_heads, visible)
            mixed_w = jnp.einsum("gqk,gh->hqk", probability, weight_mix_f, precision=HIGH).astype(
                jnp.bfloat16
            )
            grad_mixed = jnp.einsum(
                "qhd,khd->hqk", grad_heads, value_heads, preferred_element_type=jnp.float32
            )
            grad_probs = jnp.einsum("hqk,gh->gqk", grad_mixed, weight_mix_f, precision=HIGH)
            grad_logits = probability * (grad_probs - delta[:, :, None])
            grad_scores = jnp.einsum(
                "gqk,hg->hqk", grad_logits, logit_mix_f, precision=HIGH
            ).astype(jnp.bfloat16)
            grad_query = current[0] + score_scale * jnp.einsum(
                "hqk,khd->qhd", grad_scores, key_heads, preferred_element_type=jnp.float32
            )
            grad_lmix = current[1] + jnp.einsum("hqk,gqk->hg", scores, grad_logits, precision=HIGH)
            grad_wmix = current[2] + jnp.einsum(
                "gqk,hqk->gh", probability, grad_mixed, precision=HIGH
            )
            grad_key = score_scale * jnp.einsum(
                "hqk,qhd->khd", grad_scores, query_heads, preferred_element_type=jnp.float32
            )
            grad_value = jnp.einsum(
                "hqk,qhd->khd", mixed_w, grad_heads, preferred_element_type=jnp.float32
            )
            return (
                (grad_query, grad_lmix, grad_wmix),
                (grad_key.reshape(length, model_width), grad_value.reshape(length, model_width)),
            )

        def skip(current):
            empty = jnp.zeros((length, model_width), jnp.float32)
            return (current, (empty, empty))

        return lax.cond(jnp.any(visible), back_compute, skip, running)

    def cycle_turn(turn_index, cycle_state):
        moving, grad_moving, grad_query, grad_lmix, grad_wmix = cycle_state
        anchor = jnp.mod(my_index - turn_index, cycle_size)
        (grad_query, grad_lmix, grad_wmix), (grad_key, grad_value) = sweep(
            back_step, (grad_query, grad_lmix, grad_wmix), (moving[0], moving[1]), anchor * tok_rows
        )
        grad_moving = grad_moving + jnp.stack(
            [grad_key.reshape(tok_rows, model_width), grad_value.reshape(tok_rows, model_width)]
        )
        moving = shifted(moving, "ctx", 1)
        grad_moving = shifted(grad_moving.astype(jnp.bfloat16), "ctx", 1).astype(grad_moving.dtype)
        return (moving, grad_moving, grad_query, grad_lmix, grad_wmix)

    cycle_start = (
        key_value,
        jnp.zeros((2, tok_rows, model_width), jnp.float32),
        jnp.zeros((tok_rows, head_count, head_size), jnp.float32),
        jnp.zeros((head_count, head_count), jnp.float32),
        jnp.zeros((head_count, head_count), jnp.float32),
    )
    cycle_end = lax.fori_loop(0, cycle_size, cycle_turn, cycle_start)
    grad_moving, grad_query, grad_lmix, grad_wmix = (
        cycle_end[1],
        cycle_end[2],
        cycle_end[3],
        cycle_end[4],
    )
    grad_query_low = grad_query.reshape(tok_rows, model_width).astype(jnp.bfloat16)
    grad_key_low = grad_moving[0].astype(jnp.bfloat16)
    grad_value_low = grad_moving[1].astype(jnp.bfloat16)
    grad_query_mat = jnp.einsum(
        "ti,to->io", normed_low, grad_query_low, preferred_element_type=jnp.float32
    )
    grad_key_mat = jnp.einsum(
        "ti,to->io", normed_low, grad_key_low, preferred_element_type=jnp.float32
    )
    grad_value_mat = jnp.einsum(
        "ti,to->io", normed_low, grad_value_low, preferred_element_type=jnp.float32
    )
    grad_normed = jnp.einsum(
        "to,io->ti", grad_query_low, query_mat, preferred_element_type=jnp.float32
    )
    grad_normed = grad_normed + jnp.einsum(
        "to,io->ti", grad_key_low, key_mat, preferred_element_type=jnp.float32
    )
    grad_normed = grad_normed + jnp.einsum(
        "to,io->ti", grad_value_low, value_mat, preferred_element_type=jnp.float32
    )
    grad_in_norm, grad_gain_one = norm_back(grad_normed)
    grad_input = (grad_middle + grad_in_norm).astype(jnp.bfloat16)
    shares = (
        lax.psum_scatter(
            grad_gain_one.astype(jnp.bfloat16), "wt", scatter_dimension=0, tiled=True
        ).astype(jnp.float32),
        lax.psum_scatter(
            grad_query_mat.astype(jnp.bfloat16), "wt", scatter_dimension=0, tiled=True
        ).astype(jnp.float32),
        lax.psum_scatter(
            grad_key_mat.astype(jnp.bfloat16), "wt", scatter_dimension=0, tiled=True
        ).astype(jnp.float32),
        lax.psum_scatter(
            grad_value_mat.astype(jnp.bfloat16), "wt", scatter_dimension=0, tiled=True
        ).astype(jnp.float32),
        lax.psum_scatter(
            grad_lmix.astype(jnp.bfloat16), "wt", scatter_dimension=0, tiled=True
        ).astype(jnp.float32),
        lax.psum_scatter(
            grad_wmix.astype(jnp.bfloat16), "wt", scatter_dimension=0, tiled=True
        ).astype(jnp.float32),
        lax.psum_scatter(
            grad_output_mat.astype(jnp.bfloat16), "wt", scatter_dimension=0, tiled=True
        ).astype(jnp.float32),
        lax.psum_scatter(
            grad_gain_two.astype(jnp.bfloat16), "wt", scatter_dimension=0, tiled=True
        ).astype(jnp.float32),
        lax.psum_scatter(
            grad_inner.astype(jnp.bfloat16), "wt", scatter_dimension=0, tiled=True
        ).astype(jnp.float32),
        lax.psum_scatter(
            grad_outer.astype(jnp.bfloat16), "wt", scatter_dimension=0, tiled=True
        ).astype(jnp.float32),
    )
    totals = (
        lax.psum(shares[0].astype(jnp.bfloat16), "ctx").astype(jnp.float32),
        lax.psum(shares[1].astype(jnp.bfloat16), "ctx").astype(jnp.float32),
        lax.psum(shares[2].astype(jnp.bfloat16), "ctx").astype(jnp.float32),
        lax.psum(shares[3].astype(jnp.bfloat16), "ctx").astype(jnp.float32),
        lax.psum(shares[4].astype(jnp.bfloat16), "ctx").astype(jnp.float32),
        lax.psum(shares[5].astype(jnp.bfloat16), "ctx").astype(jnp.float32),
        lax.psum(shares[6].astype(jnp.bfloat16), "ctx").astype(jnp.float32),
        lax.psum(shares[7].astype(jnp.bfloat16), "ctx").astype(jnp.float32),
        lax.psum(shares[8].astype(jnp.bfloat16), "ctx").astype(jnp.float32),
        lax.psum(shares[9].astype(jnp.bfloat16), "ctx").astype(jnp.float32),
    )
    return (
        output.astype(jnp.bfloat16)[None],
        grad_input[None],
        rms_values,
        totals[0],
        totals[1],
        totals[2],
        totals[3],
        totals[4],
        totals[5],
        totals[6],
        totals[7],
        totals[8],
        totals[9],
    )


def solution(mesh):
    return jax.shard_map(
        shards,
        mesh=mesh,
        in_specs=(
            P("wt", "ctx", None),
            P("wt", "ctx", None),
            P(),
            P("wt", None),
            P("wt"),
            P("wt", None),
            P("wt", None),
            P("wt", None),
            P("wt", None),
            P("wt", None),
            P("wt", None),
            P("wt"),
            P("wt", None),
            P("wt", None),
        ),
        out_specs=(
            P("wt", "ctx", None),
            P("wt", "ctx", None),
            P(),
            P("wt"),
            P("wt", None),
            P("wt", None),
            P("wt", None),
            P("wt", None),
            P("wt", None),
            P("wt", None),
            P("wt"),
            P("wt", None),
            P("wt", None),
        ),
        check_vma=False,
    )
```

profile of v0, /device:TPU:0, one launch (start us, length us, event | category | flops | bytes accessed | tf_op | source)
XLA Modules:
  0.0 2984.4 jit_solution(9208938649344471737)
XLA Ops:
  71.9 78.5 %all-gather.19.cloned.1.call-done = bf16[3072,768]{1,0:T(8,128)(2,1)} async-done(((bf16[384,768]{1,0:T(8,128)(2,1)}), bf16[3072,768]{1,0:T(8,128)(2,1)}) %all-gather.19.cloned.1.call-update) | async-done | bytes 4718608 | tf_op jit(solution)/shard_map/all_gather | solution.py:152
  157.2 261.0 %while.89 = (s32[]{:T(128)}, f32[12,384]{0,1:T(8,128)S(1)}, f32[12,384]{0,1:T(8,128)S(1)}, s32[4]{0:T(128)S(1)}, s32[8]{0:T(128)S(1)}, /*index=5*/s32[384]{0:T(5...) while((s32[]{:T(128)}, f32[12,384]{0,1:T(8,128)S(1)}, ...), condition=%wide.region_9.10_spmd, body=%wide.region_2.9_spmd.sunk | while | flops 988589568 | bytes 90216296 | solution.py:55
  163.1 59.7 %conditional.9 = ((f32[12,384]{0,1:T(8,128)S(1)}, f32[12,384]{0,1:T(8,128)S(1)})) conditional(s32[]{:T(128)} %convert_element_type.527, (f32[12,384]{0,1:T(8,128)S(1)}, f32[12,384]{0,1:T(8,128)S(1)}) %tuple.230, (pred[384,768]{1,0:T(8,128)(4,1)S(1)}, bf16[4,768,768]{1,2,0:T(8,128)(2,1)}, s32[]{:T(128)}, bf16[384,12,64]{0,2,1:T(8,128)(2,1)S(1)}, ...), branch_computations={%region_5.5_spmd, %region_6.8_spmd} | conditional | flops 987374592 | bytes 89893464 | solution.py:145
  293.3 59.7 %conditional.9 = ((f32[12,384]{0,1:T(8,128)S(1)}, f32[12,384]{0,1:T(8,128)S(1)})) conditional(s32[]{:T(128)} %convert_element_type.527, (f32[12,384]{0,1:T(8,128)S(1)}, f32[12,384]{0,1:T(8,128)S(1)}) %tuple.230, (pred[384,768]{1,0:T(8,128)(4,1)S(1)}, bf16[4,768,768]{1,2,0:T(8,128)(2,1)}, s32[]{:T(128)}, bf16[384,12,64]{0,2,1:T(8,128)(2,1)S(1)}, ...), branch_computations={%region_5.5_spmd, %region_6.8_spmd} | conditional | flops 987374592 | bytes 89893464 | solution.py:145
  358.6 59.6 %conditional.9 = ((f32[12,384]{0,1:T(8,128)S(1)}, f32[12,384]{0,1:T(8,128)S(1)})) conditional(s32[]{:T(128)} %convert_element_type.527, (f32[12,384]{0,1:T(8,128)S(1)}, f32[12,384]{0,1:T(8,128)S(1)}) %tuple.230, (pred[384,768]{1,0:T(8,128)(4,1)S(1)}, bf16[4,768,768]{1,2,0:T(8,128)(2,1)}, s32[]{:T(128)}, bf16[384,12,64]{0,2,1:T(8,128)(2,1)S(1)}, ...), branch_computations={%region_5.5_spmd, %region_6.8_spmd} | conditional | flops 987374592 | bytes 89893464 | solution.py:145
  440.8 357.1 %while.90 = (s32[]{:T(128)}, f32[384,12,64]{0,2,1:T(8,128)}, s32[4]{0:T(128)S(1)}, s32[8]{0:T(128)S(1)}, s32[384]{0:T(512)S(1)}, /*index=5*/s32[3]{0:T(128)S(1)}...) while((s32[]{:T(128)}, f32[384,12,64]{0,2,1:T(8,128)}, ...), condition=%wide.region_15.16_spmd, body=%wide.region_10.15_spmd.sunk | while | flops 1940851200 | bytes 109754792 | solution.py:55
  458.6 80.6 %conditional.10 = (f32[384,12,64]{0,2,1:T(8,128)}) conditional(s32[]{:T(128)} %convert_element_type.530, f32[384,12,64]{0,2,1:T(8,128)} %get-tuple-element.2262, (pred[384,768]{1,0:T(8,128)(4,1)S(1)}, bf16[4,768,768]{1,2,0:T(8,128)(2,1)}, s32[]{:T(128)}, bf16[384,12,64]{0,2,1:T(8,128)(2,1)S(1)}, f32[12,12]{0,1:T(8,128)}, ...), branch_computations={%region_13.13_spmd, %region_14.14_spmd} | conditional | flops 1939636224 | bytes 109431944 | solution.py:177
  544.7 80.6 %conditional.10 = (f32[384,12,64]{0,2,1:T(8,128)}) conditional(s32[]{:T(128)} %convert_element_type.530, f32[384,12,64]{0,2,1:T(8,128)} %get-tuple-element.2262, (pred[384,768]{1,0:T(8,128)(4,1)S(1)}, bf16[4,768,768]{1,2,0:T(8,128)(2,1)}, s32[]{:T(128)}, bf16[384,12,64]{0,2,1:T(8,128)(2,1)S(1)}, f32[12,12]{0,1:T(8,128)}, ...), branch_computations={%region_13.13_spmd, %region_14.14_spmd} | conditional | flops 1939636224 | bytes 109431944 | solution.py:177
  630.8 80.6 %conditional.10 = (f32[384,12,64]{0,2,1:T(8,128)}) conditional(s32[]{:T(128)} %convert_element_type.530, f32[384,12,64]{0,2,1:T(8,128)} %get-tuple-element.2262, (pred[384,768]{1,0:T(8,128)(4,1)S(1)}, bf16[4,768,768]{1,2,0:T(8,128)(2,1)}, s32[]{:T(128)}, bf16[384,12,64]{0,2,1:T(8,128)(2,1)S(1)}, f32[12,12]{0,1:T(8,128)}, ...), branch_computations={%region_13.13_spmd, %region_14.14_spmd} | conditional | flops 1939636224 | bytes 109431944 | solution.py:177
  716.9 80.6 %conditional.10 = (f32[384,12,64]{0,2,1:T(8,128)}) conditional(s32[]{:T(128)} %convert_element_type.530, f32[384,12,64]{0,2,1:T(8,128)} %get-tuple-element.2262, (pred[384,768]{1,0:T(8,128)(4,1)S(1)}, bf16[4,768,768]{1,2,0:T(8,128)(2,1)}, s32[]{:T(128)}, bf16[384,12,64]{0,2,1:T(8,128)(2,1)S(1)}, f32[12,12]{0,1:T(8,128)}, ...), branch_computations={%region_13.13_spmd, %region_14.14_spmd} | conditional | flops 1939636224 | bytes 109431944 | solution.py:177
  833.6 420.1 %while.91 = (s32[]{:T(128)}, f32[12,384]{0,1:T(8,128)}, s32[4]{0:T(128)S(1)}, s32[8]{0:T(128)S(1)}, s32[384]{0:T(512)S(1)}, /*index=5*/s32[3]{0:T(128)S(1)}, s32...) while((s32[]{:T(128)}, f32[12,384]{0,1:T(8,128)}, ...), condition=%wide.region_24.25_spmd, body=%wide.region_18.24_spmd.sunk | while | flops 1944095232 | bytes 150526384 | solution.py:55
  839.2 99.8 %conditional.11 = (f32[12,384]{0,1:T(8,128)}) conditional(s32[]{:T(128)} %convert_element_type.533, f32[12,384]{0,1:T(8,128)} %get-tuple-element.2305, (pred[384,768]{1,0:T(8,128)(4,1)S(1)}, bf16[4,768,768]{1,2,0:T(8,128)(2,1)}, s32[]{:T(128)}, bf16[384,12,64]{0,2,1:T(8,128)(2,1)S(1)}, f32[12,12]{0,1:T(8,128)}, ...), branch_computations={%region_21.21_spmd, %region_22.23_spmd} | conditional | flops 1942880256 | bytes 150203520 | solution.py:243
  944.3 99.5 %conditional.11 = (f32[12,384]{0,1:T(8,128)}) conditional(s32[]{:T(128)} %convert_element_type.533, f32[12,384]{0,1:T(8,128)} %get-tuple-element.2305, (pred[384,768]{1,0:T(8,128)(4,1)S(1)}, bf16[4,768,768]{1,2,0:T(8,128)(2,1)}, s32[]{:T(128)}, bf16[384,12,64]{0,2,1:T(8,128)(2,1)S(1)}, f32[12,12]{0,1:T(8,128)}, ...), branch_computations={%region_21.21_spmd, %region_22.23_spmd} | conditional | flops 1942880256 | bytes 150203520 | solution.py:243
  1049.2 99.5 %conditional.11 = (f32[12,384]{0,1:T(8,128)}) conditional(s32[]{:T(128)} %convert_element_type.533, f32[12,384]{0,1:T(8,128)} %get-tuple-element.2305, (pred[384,768]{1,0:T(8,128)(4,1)S(1)}, bf16[4,768,768]{1,2,0:T(8,128)(2,1)}, s32[]{:T(128)}, bf16[384,12,64]{0,2,1:T(8,128)(2,1)S(1)}, f32[12,12]{0,1:T(8,128)}, ...), branch_computations={%region_21.21_spmd, %region_22.23_spmd} | conditional | flops 1942880256 | bytes 150203520 | solution.py:243
  1154.2 99.5 %conditional.11 = (f32[12,384]{0,1:T(8,128)}) conditional(s32[]{:T(128)} %convert_element_type.533, f32[12,384]{0,1:T(8,128)} %get-tuple-element.2305, (pred[384,768]{1,0:T(8,128)(4,1)S(1)}, bf16[4,768,768]{1,2,0:T(8,128)(2,1)}, s32[]{:T(128)}, bf16[384,12,64]{0,2,1:T(8,128)(2,1)S(1)}, f32[12,12]{0,1:T(8,128)}, ...), branch_computations={%region_21.21_spmd, %region_22.23_spmd} | conditional | flops 1942880256 | bytes 150203520 | solution.py:243
  1254.8 1373.1 %while.92 = (s32[]{:T(128)}, bf16[2,384,768]{1,2,0:T(8,128)(2,1)}, f32[2,384,768]{1,2,0:T(8,128)}, f32[384,12,64]{0,2,1:T(8,128)}, f32[12,12]{1,0:T(8,128)S(1)},...) while((s32[]{:T(128)}, bf16[2,384,768]{1,2,0:T(8,128)(2,1)}, ...), condition=%wide.region_30.31_spmd.clone, body=%wide.region_25.30_spmd.clone.sunk | while | flops 2685191680 | bytes 208892160 | solution.py:316
  1260.0 103.8 %conditional.12 = (f32[384,12,64]{0,2,1:T(8,128)}, f32[12,12]{1,0:T(8,128)S(1)}, f32[12,12]{1,0:T(8,128)S(1)}, f32[1,384,768]{1,2,0:T(8,128)}, f32[1,384,768]{1,2,0:T(8,128)}) conditional(s32[]{:T(128)} %convert_element_type.537, (f32[384,12,64]{0,2,1:T(8,128)}, f32[12,12]{1,0:T(8,128)S(1)}, f32[12,12]{1,0:T(8,128)S(1)}) %tuple.246, ...), branch_computations={%region_28.28_spmd, %region_29.29_spmd} | conditional | flops 2681635072 | bytes 187495072 | solution.py:294
  1427.2 114.0 %conditional.12 = (f32[384,12,64]{0,2,1:T(8,128)}, f32[12,12]{1,0:T(8,128)S(1)}, f32[12,12]{1,0:T(8,128)S(1)}, f32[1,384,768]{1,2,0:T(8,128)}, f32[1,384,768]{1,2,0:T(8,128)}) conditional(s32[]{:T(128)} %convert_element_type.537, (f32[384,12,64]{0,2,1:T(8,128)}, f32[12,12]{1,0:T(8,128)S(1)}, f32[12,12]{1,0:T(8,128)S(1)}) %tuple.246, ...), branch_computations={%region_28.28_spmd, %region_29.29_spmd} | conditional | flops 2681635072 | bytes 187495072 | solution.py:294
  1674.3 78.8 %collective-permute-start.1 = (bf16[2,384,768]{1,2,0:T(8,128)(2,1)}, bf16[2,384,768]{1,2,0:T(8,128)(2,1)}, u32[]{:S(2)}, u32[]{:S(2)}) collective-permute-start(bf16[2,384,768]{1,2,0:T(8,128)(2,1)} %fusion.252), channel_id=1, source_target_pairs={{0,4},{4,8},{8,12},{12,16},{16,20},{20,24},{24,28},{28,0},{1,5},{5... | collective-permute-start | bytes 3538952 | tf_op jit(solution)/shard_map/while/body/eval_jaxpr/ppermute | solution.py:14
  1753.1 127.7 %collective-permute-start = (bf16[2,384,768]{1,2,0:T(8,128)(2,1)S(1)}, bf16[2,384,768]{1,2,0:T(8,128)(2,1)}, u32[]{:S(2)}, u32[]{:S(2)}) collective-permute-start(bf16[2,384,768]{1,2,0:T(8,128)(2,1)S(1)} %copy.217), channel_id=1, source_target_pairs={{0,4},{4,8},{8,12},{12,16},{16,20},{20,24},{24,28},{28,0},{1,5},{5... | collective-permute-start | bytes 3538952 | tf_op jit(solution)/shard_map/while/body/eval_jaxpr/ppermute | solution.py:14
  1936.8 114.0 %conditional.12 = (f32[384,12,64]{0,2,1:T(8,128)}, f32[12,12]{1,0:T(8,128)S(1)}, f32[12,12]{1,0:T(8,128)S(1)}, f32[1,384,768]{1,2,0:T(8,128)}, f32[1,384,768]{1,2,0:T(8,128)}) conditional(s32[]{:T(128)} %convert_element_type.537, (f32[384,12,64]{0,2,1:T(8,128)}, f32[12,12]{1,0:T(8,128)S(1)}, f32[12,12]{1,0:T(8,128)S(1)}) %tuple.246, ...), branch_computations={%region_28.28_spmd, %region_29.29_spmd} | conditional | flops 2681635072 | bytes 187495072 | solution.py:294
  2175.0 114.0 %conditional.12 = (f32[384,12,64]{0,2,1:T(8,128)}, f32[12,12]{1,0:T(8,128)S(1)}, f32[12,12]{1,0:T(8,128)S(1)}, f32[1,384,768]{1,2,0:T(8,128)}, f32[1,384,768]{1,2,0:T(8,128)}) conditional(s32[]{:T(128)} %convert_element_type.537, (f32[384,12,64]{0,2,1:T(8,128)}, f32[12,12]{1,0:T(8,128)S(1)}, f32[12,12]{1,0:T(8,128)S(1)}) %tuple.246, ...), branch_computations={%region_28.28_spmd, %region_29.29_spmd} | conditional | flops 2681635072 | bytes 187495072 | solution.py:294
  2292.7 133.9 %collective-permute-done.1 = bf16[2,384,768]{1,2,0:T(8,128)(2,1)} collective-permute-done((bf16[2,384,768]{1,2,0:T(8,128)(2,1)}, bf16[2,384,768]{1,2,0:T(8,128)(2,1)}, u32[]{:S(2)}, u32[]{:S(2)}) %collective-permute-start.1) | collective-permute-done | bytes 1179680 | tf_op jit(solution)/shard_map/while/body/eval_jaxpr/ppermute | solution.py:14
  2450.8 114.0 %conditional.12 = (f32[384,12,64]{0,2,1:T(8,128)}, f32[12,12]{1,0:T(8,128)S(1)}, f32[12,12]{1,0:T(8,128)S(1)}, f32[1,384,768]{1,2,0:T(8,128)}, f32[1,384,768]{1,2,0:T(8,128)}) conditional(s32[]{:T(128)} %convert_element_type.537, (f32[384,12,64]{0,2,1:T(8,128)}, f32[12,12]{1,0:T(8,128)S(1)}, f32[12,12]{1,0:T(8,128)S(1)}) %tuple.246, ...), branch_computations={%region_28.28_spmd, %region_29.29_spmd} | conditional | flops 2681635072 | bytes 187495072 | solution.py:294
  (578 shorter events, 2575.4 us)
Async XLA Ops:
  7.9 40.9 %all-gather.13.cloned.1.call-start = ((), (), s32[]{:S(2)}) async-start(), calls=%async_computation.7 | async-start | bytes 1474560 | tf_op jit(solution)/shard_map/all_gather | solution.py:89
  8.7 61.0 %all-gather.17.cloned.1.call-start = ((), (), s32[]{:S(2)}) async-start(), calls=%async_computation.9 | async-start | bytes 1474560 | tf_op jit(solution)/shard_map/all_gather | solution.py:87
  9.4 141.0 %all-gather.19.cloned.1.call-start = ((), (), s32[]{:S(2)}) async-start(), calls=%async_computation.10 | async-start | bytes 5308416 | tf_op jit(solution)/shard_map/all_gather | solution.py:152
  32.7 385.5 %all-gather.15.cloned.1.call-start = ((), (), s32[]{:S(2)}) async-start(), calls=%async_computation.8 | async-start | bytes 10616832 | tf_op jit(solution)/shard_map/all_gather | solution.py:180
  51.9 747.4 %all-gather.21.cloned.1.call-start = ((), (), s32[]{:S(2)}) async-start(), calls=%async_computation.11 | async-start | bytes 1474560 | tf_op jit(solution)/shard_map/all_gather | solution.py:92
  52.5 750.6 %all-gather.23.cloned.1.call-start = ((), (), s32[]{:S(2)}) async-start(), calls=%async_computation.12 | async-start | bytes 5898240 | tf_op jit(solution)/shard_map/all_gather | solution.py:94
  53.3 756.9 %all-gather.25.cloned.1.call-start = ((), (), s32[]{:S(2)}) async-start(), calls=%async_computation.13 | async-start | bytes 5898240 | tf_op jit(solution)/shard_map/all_gather | solution.py:95
  54.0 2599.7 %reduce-scatter.13.cloned.1.call-start = ((), (), s32[]{:S(2)}) async-start(), calls=%async_computation.17 | async-start | bytes 1474560 | tf_op jit(solution)/shard_map/reduce_scatter | solution.py:365
  830.6 1834.2 %reduce-scatter.7.cloned.1.call-start = ((), (), s32[]{:S(2)}) async-start(), calls=%async_computation.14 | async-start | bytes 1474560 | tf_op jit(solution)/shard_map/reduce_scatter | solution.py:350
  1366.8 55.3 %collective-permute-start = (bf16[2,384,768]{1,2,0:T(8,128)(2,1)S(1)}, bf16[2,384,768]{1,2,0:T(8,128)(2,1)}, u32[]{:S(2)}, u32[]{:S(2)}) collective-permute-start(bf16[2,384,768]{1,2,0:T(8,128)(2,1)S(1)} %copy.217), channel_id=1, source_target_pairs={{0,4},{4,8},{8,12},{12,16},{16,20},{20,24},{24,28},{28,0},{1,5},{5... | collective-permute-start | bytes 3538952 | tf_op jit(solution)/shard_map/while/body/eval_jaxpr/ppermute | solution.py:14
  1544.9 54.3 %collective-permute-start = (bf16[2,384,768]{1,2,0:T(8,128)(2,1)S(1)}, bf16[2,384,768]{1,2,0:T(8,128)(2,1)}, u32[]{:S(2)}, u32[]{:S(2)}) collective-permute-start(bf16[2,384,768]{1,2,0:T(8,128)(2,1)S(1)} %copy.217), channel_id=1, source_target_pairs={{0,4},{4,8},{8,12},{12,16},{16,20},{20,24},{24,28},{28,0},{1,5},{5... | collective-permute-start | bytes 3538952 | tf_op jit(solution)/shard_map/while/body/eval_jaxpr/ppermute | solution.py:14
  1610.5 53.1 %collective-permute-start = (bf16[2,384,768]{1,2,0:T(8,128)(2,1)S(1)}, bf16[2,384,768]{1,2,0:T(8,128)(2,1)}, u32[]{:S(2)}, u32[]{:S(2)}) collective-permute-start(bf16[2,384,768]{1,2,0:T(8,128)(2,1)S(1)} %copy.217), channel_id=1, source_target_pairs={{0,4},{4,8},{8,12},{12,16},{16,20},{20,24},{24,28},{28,0},{1,5},{5... | collective-permute-start | bytes 3538952 | tf_op jit(solution)/shard_map/while/body/eval_jaxpr/ppermute | solution.py:14
  1674.3 235.9 %collective-permute-start.1 = (bf16[2,384,768]{1,2,0:T(8,128)(2,1)}, bf16[2,384,768]{1,2,0:T(8,128)(2,1)}, u32[]{:S(2)}, u32[]{:S(2)}) collective-permute-start(bf16[2,384,768]{1,2,0:T(8,128)(2,1)} %fusion.252), channel_id=1, source_target_pairs={{0,4},{4,8},{8,12},{12,16},{16,20},{20,24},{24,28},{28,0},{1,5},{5... | collective-permute-start | bytes 3538952 | tf_op jit(solution)/shard_map/while/body/eval_jaxpr/ppermute | solution.py:14
  1753.1 178.9 %collective-permute-start = (bf16[2,384,768]{1,2,0:T(8,128)(2,1)S(1)}, bf16[2,384,768]{1,2,0:T(8,128)(2,1)}, u32[]{:S(2)}, u32[]{:S(2)}) collective-permute-start(bf16[2,384,768]{1,2,0:T(8,128)(2,1)S(1)} %copy.217), channel_id=1, source_target_pairs={{0,4},{4,8},{8,12},{12,16},{16,20},{20,24},{24,28},{28,0},{1,5},{5... | collective-permute-start | bytes 3538952 | tf_op jit(solution)/shard_map/while/body/eval_jaxpr/ppermute | solution.py:14
  2054.5 52.8 %collective-permute-start = (bf16[2,384,768]{1,2,0:T(8,128)(2,1)S(1)}, bf16[2,384,768]{1,2,0:T(8,128)(2,1)}, u32[]{:S(2)}, u32[]{:S(2)}) collective-permute-start(bf16[2,384,768]{1,2,0:T(8,128)(2,1)S(1)} %copy.217), channel_id=1, source_target_pairs={{0,4},{4,8},{8,12},{12,16},{16,20},{20,24},{24,28},{28,0},{1,5},{5... | collective-permute-start | bytes 3538952 | tf_op jit(solution)/shard_map/while/body/eval_jaxpr/ppermute | solution.py:14
  2118.4 51.9 %collective-permute-start = (bf16[2,384,768]{1,2,0:T(8,128)(2,1)S(1)}, bf16[2,384,768]{1,2,0:T(8,128)(2,1)}, u32[]{:S(2)}, u32[]{:S(2)}) collective-permute-start(bf16[2,384,768]{1,2,0:T(8,128)(2,1)S(1)} %copy.217), channel_id=1, source_target_pairs={{0,4},{4,8},{8,12},{12,16},{16,20},{20,24},{24,28},{28,0},{1,5},{5... | collective-permute-start | bytes 3538952 | tf_op jit(solution)/shard_map/while/body/eval_jaxpr/ppermute | solution.py:14
  2292.7 133.9 %collective-permute-start.1 = (bf16[2,384,768]{1,2,0:T(8,128)(2,1)}, bf16[2,384,768]{1,2,0:T(8,128)(2,1)}, u32[]{:S(2)}, u32[]{:S(2)}) collective-permute-start(bf16[2,384,768]{1,2,0:T(8,128)(2,1)} %fusion.252), channel_id=1, source_target_pairs={{0,4},{4,8},{8,12},{12,16},{16,20},{20,24},{24,28},{28,0},{1,5},{5... | collective-permute-start | bytes 3538952 | tf_op jit(solution)/shard_map/while/body/eval_jaxpr/ppermute | solution.py:14
  2292.7 153.0 %collective-permute-start = (bf16[2,384,768]{1,2,0:T(8,128)(2,1)S(1)}, bf16[2,384,768]{1,2,0:T(8,128)(2,1)}, u32[]{:S(2)}, u32[]{:S(2)}) collective-permute-start(bf16[2,384,768]{1,2,0:T(8,128)(2,1)S(1)} %copy.217), channel_id=1, source_target_pairs={{0,4},{4,8},{8,12},{12,16},{16,20},{20,24},{24,28},{28,0},{1,5},{5... | collective-permute-start | bytes 3538952 | tf_op jit(solution)/shard_map/while/body/eval_jaxpr/ppermute | solution.py:14
  2568.5 50.1 %collective-permute-start = (bf16[2,384,768]{1,2,0:T(8,128)(2,1)S(1)}, bf16[2,384,768]{1,2,0:T(8,128)(2,1)}, u32[]{:S(2)}, u32[]{:S(2)}) collective-permute-start(bf16[2,384,768]{1,2,0:T(8,128)(2,1)S(1)} %copy.217), channel_id=1, source_target_pairs={{0,4},{4,8},{8,12},{12,16},{16,20},{20,24},{24,28},{28,0},{1,5},{5... | collective-permute-start | bytes 3538952 | tf_op jit(solution)/shard_map/while/body/eval_jaxpr/ppermute | solution.py:14
  2632.5 60.6 %reduce-scatter.11.cloned.1.call-start = ((), (), s32[]{:S(2)}) async-start(), calls=%async_computation.16 | async-start | bytes 1474560 | tf_op jit(solution)/shard_map/reduce_scatter | solution.py:356
  2635.3 86.8 %reduce-scatter.9.cloned.1.call-start = ((), (), s32[]{:S(2)}) async-start(), calls=%async_computation.15 | async-start | bytes 1474560 | tf_op jit(solution)/shard_map/reduce_scatter | solution.py:353
  2638.0 134.5 %reduce-scatter.15.cloned.1.call-start = ((), (), s32[]{:S(2)}) async-start(), calls=%async_computation.18 | async-start | bytes 5898240 | tf_op jit(solution)/shard_map/reduce_scatter | solution.py:371
  2644.9 178.0 %reduce-scatter.17.cloned.1.call-start = ((), (), s32[]{:S(2)}) async-start(), calls=%async_computation.19 | async-start | bytes 5898240 | tf_op jit(solution)/shard_map/reduce_scatter | solution.py:374
  2653.7 315.9 %all-reduce.12.cloned.1.call-start = ((), (), s32[]{:S(2)}) async-start(), calls=%async_computation.20 | async-start | bytes 7077888 | tf_op jit(solution)/shard_map/psum | solution.py:380
  (71 other events, 2092.2 us)
Sparse Core Ops, SparseCore 0:
  9.6 20.1 all-gather.10
  31.3 17.4 all-gather.12
  50.4 17.4 all-gather.16
  70.5 79.8 all-gather.18
  153.0 136.1 all-gather.14
  290.7 15.6 all-gather.20
  307.9 37.4 all-gather.22
  347.0 37.4 all-gather.24
  830.7 24.8 reduce-scatter.12
  2632.6 32.1 reduce-scatter.6
  2667.4 25.7 reduce-scatter.10
  2696.3 25.7 reduce-scatter.8
  2724.6 47.8 reduce-scatter.14
  2775.0 47.8 reduce-scatter.16
  2827.1 142.5 all-reduce.11
where the time goes:
time: 3000 us; the launch traced here: 2980 us
  matrix products  1230 us (41%)
  waiting for transfers between devices  820 us (27%)
  local copies, waits for them, and re-layouts  380 us (13%)
  starting transfers between devices  215 us (7%)
  other arithmetic  187 us (6%)
  blocking collectives  93.7 us (3%)
  loops' own time  39.7 us (1%)
    ppermute x16, waiting for transfers between devices, shifted(): return lax.ppermute(value, axis, pairs)  491 us
    dot_general x17, matrix products, logits_for(): logits = jnp.einsum('hqk,hg->gqk', scores, logit_mix_f, precision=HIGH)  402 us
    ppermute x16, starting transfers between devices, shifted(): return lax.ppermute(value, axis, pairs)  215 us
    mul x12, local copies, waits for them, and re-layouts, logits_for(): jnp.einsum('qhd,khd->hqk', query_heads, key_heads, preferred_element_type...  208 us
    dot_general x5, matrix products, back_compute(): jnp.einsum('hqk,gh->gqk', grad_mixed, weight_mix_f, precision=HIGH)  119 us
    dot_general x5, matrix products, back_compute(): jnp.einsum('gqk,hqk->gh', probability, grad_mixed, precision=HIGH)  96 us
    dot_general x4, matrix products, value_compute(): jnp.einsum('gqk,gh->hqk', probability, weight_mix_f, precision=HIGH)  92.4 us
    dot_general x4, matrix products, delta_compute(): jnp.einsum('hqk,gh->gqk', grad_mixed, weight_mix_f, precision=HIGH)  90 us
  transfers between devices with their start and end apart: 31, of which 25 were waited for; matrix products, arithmetic and copies ran while one was open for 59% of the time, Pallas kernels for 0%

commit v1 on v0

v1 whole, which is shorter than its diff:
```python
import functools
import math

import jax
import jax.numpy as jnp
from jax import lax
from jax.experimental import pallas as pl
from jax.experimental.pallas import tpu as pltpu
from jax.sharding import PartitionSpec as P

NEG = -1e30
EPS = 1e-06
LOG2E = 1.4426950408889634
LN2 = 0.6931471805599453
F32 = jnp.float32
BF16 = jnp.bfloat16
NT = (((1,), (1,)), ((), ()))
VMEM_BYTES = 60 * 1024 * 1024


def dot(left, right):
    return jnp.dot(left, right, preferred_element_type=F32)


def dot_nt(left, right):
    return lax.dot_general(left, right, NT, preferred_element_type=F32)


def rms_norm(values, gain):
    return values * lax.rsqrt(jnp.mean(values * values, axis=-1, keepdims=True) + EPS) * gain


def gelu_tanh(values):
    return jax.nn.gelu(values, approximate=True)


def params(flops, moved, dims=1):
    return dict(
        compiler_params=pltpu.CompilerParams(
            dimension_semantics=("arbitrary",) * dims, vmem_limit_bytes=VMEM_BYTES
        ),
        cost_estimate=pl.CostEstimate(flops=flops, bytes_accessed=moved, transcendentals=0),
    )


HEAD = 5


def project_kernel(sc, x_ref, gain_ref, wk_ref, wv_ref, k_ref, v_ref, kt_ref, vt_ref, nt_ref):
    x = x_ref[0].astype(F32)
    normed = rms_norm(x, gain_ref[...]).astype(BF16)
    nt_ref[0] = normed.T
    k = dot(normed, wk_ref[...]).astype(BF16)
    k_ref[0] = k
    kt_ref[0] = k.T
    v = dot(normed, wv_ref[...]).astype(BF16)
    v_ref[0] = v
    vt_ref[0] = v.T


def project(scalars, x_rel, gain, wk, wv):
    count, rows, width = x_rel.shape
    place = lambda j, sc: (sc[HEAD + 2 * count + j], 0, 0)
    fixed = lambda j, sc: (0, 0)
    tall = jax.ShapeDtypeStruct((count, rows, width), BF16)
    wide = jax.ShapeDtypeStruct((count, width, rows), BF16)
    return pl.pallas_call(
        project_kernel,
        grid_spec=pltpu.PrefetchScalarGridSpec(
            num_scalar_prefetch=1,
            grid=(count,),
            in_specs=[
                pl.BlockSpec((1, rows, width), lambda j, sc: (j, 0, 0)),
                pl.BlockSpec((1, width), fixed),
                pl.BlockSpec((width, width), fixed),
                pl.BlockSpec((width, width), fixed),
            ],
            out_specs=[
                pl.BlockSpec((1, rows, width), place),
                pl.BlockSpec((1, rows, width), place),
                pl.BlockSpec((1, width, rows), place),
                pl.BlockSpec((1, width, rows), place),
                pl.BlockSpec((1, width, rows), place),
            ],
        ),
        out_shape=[tall, tall, wide, wide, wide],
        **params(4 * count * rows * width * width, 12 * count * rows * width),
    )(scalars, x_rel, gain, wk, wv)


def bias_of(sc, key_place, query_place, rows, half):
    key_pos = key_place + lax.broadcasted_iota(jnp.int32, (rows, 2 * half), 0)
    lane = lax.broadcasted_iota(jnp.int32, (rows, 2 * half), 1)
    query_pos = query_place + jnp.where(lane >= half, lane - half, lane)
    key_doc = (key_pos >= sc[3]).astype(jnp.int32) + (key_pos >= sc[4]).astype(jnp.int32)
    query_doc = (query_pos >= sc[3]).astype(jnp.int32) + (query_pos >= sc[4]).astype(jnp.int32)
    return jnp.where((key_pos <= query_pos) & (key_doc == query_doc), 0.0, NEG)


def fold(target, lead, source, mix_ref, heads, half):
    values = source.astype(F32)
    for g in range(heads):
        piece = (values * mix_ref[g : g + 1, :]).astype(BF16)
        if lead is None:
            target[g * half : (g + 1) * half, :] = piece
        else:
            target[lead, g * half : (g + 1) * half, :] = piece


def attend_kernel(
    count, heads, group, sc, q_ref, k_ref, vt_ref, mix_ref, back_ref,
    att_ref, t_ref, lse_ref, folded, total, top, norm, bias_s,
):
    half, width = q_ref.shape[1], q_ref.shape[2]
    rows = k_ref.shape[1]
    step = pl.program_id(0)
    own = sc[0]
    first_half = step <= own
    tile = jnp.where(first_half, step, step - own - 1)
    query_place = jnp.where(first_half, own * rows, (count - 1 - own) * rows + half)

    @pl.when((step == 0) | (step == own + 1))
    def start():
        fold(folded, None, q_ref[0], mix_ref, heads, half)
        top[...] = jnp.full(top.shape, NEG, F32)
        norm[...] = jnp.zeros(norm.shape, F32)
        total[...] = jnp.zeros(total.shape, F32)

    bias_s[...] = bias_of(sc, tile * rows, query_place, rows, half)
    span = group * half
    for c in range(heads // group):
        cols = slice(c * span, (c + 1) * span)
        logits = dot_nt(k_ref[0], folded[cols, :])
        logits = logits + jnp.concatenate([bias_s[...]] * (group // 2), axis=1)
        before = top[:, cols]
        after = jnp.maximum(before, jnp.max(logits, axis=0, keepdims=True))
        shrink = jnp.exp2(before - after)
        weights = jnp.exp2(logits - after)
        top[:, cols] = after
        norm[:, cols] = norm[:, cols] * shrink + jnp.sum(weights, axis=0, keepdims=True)
        total[:, cols] = total[:, cols] * shrink + dot(vt_ref[0], weights.astype(BF16))

    @pl.when((step == own) | (step == count))
    def finish():
        lse_ref[0] = top[...] + jnp.log2(norm[...])
        inverse = 1.0 / norm[...]
        attended = jnp.zeros((width, half), F32)
        for p in range(heads // 2):
            cols = slice(2 * p * half, (2 * p + 2) * half)
            scaled = total[:, cols] * inverse[:, cols]
            t_ref[0, :, cols] = scaled.astype(BF16)
            attended += back_ref[:, 2 * p : 2 * p + 1] * scaled[:, :half]
            attended += back_ref[:, 2 * p + 1 : 2 * p + 2] * scaled[:, half:]
        att_ref[0] = attended.T.astype(BF16)


def attend(scalars, q, k, vt, mix_rows, weight_cols, heads):
    count, rows, width = k.shape
    half = q.shape[1]
    span = heads * half
    which = lambda s, sc: (jnp.where(s <= sc[0], 0, 1), 0, 0)
    tile = lambda s, sc: (sc[HEAD + jnp.where(s <= sc[0], s, s - sc[0] - 1)], 0, 0)
    fixed = lambda s, sc: (0, 0)
    group = math.gcd(heads, 4)
    return pl.pallas_call(
        functools.partial(attend_kernel, count, heads, group),
        grid_spec=pltpu.PrefetchScalarGridSpec(
            num_scalar_prefetch=1,
            grid=(count + 1,),
            in_specs=[
                pl.BlockSpec((1, half, width), which),
                pl.BlockSpec((1, rows, width), tile),
                pl.BlockSpec((1, width, rows), tile),
                pl.BlockSpec((heads, width), fixed),
                pl.BlockSpec((width, heads), fixed),
            ],
            out_specs=[
                pl.BlockSpec((1, half, width), which),
                pl.BlockSpec((1, width, span), which),
                pl.BlockSpec((1, 1, span), which),
            ],
            scratch_shapes=[
                pltpu.VMEM((span, width), BF16),
                pltpu.VMEM((width, span), F32),
                pltpu.VMEM((1, span), F32),
                pltpu.VMEM((1, span), F32),
                pltpu.VMEM((rows, 2 * half), F32),
            ],
        ),
        out_shape=[
            jax.ShapeDtypeStruct((2, half, width), BF16),
            jax.ShapeDtypeStruct((2, width, span), BF16),
            jax.ShapeDtypeStruct((2, 1, span), F32),
        ],
        **params(4 * (count + 1) * rows * span * width, 6 * count * rows * width),
    )(scalars, q, k, vt, mix_rows, weight_cols)


def pair_rows(left, right, heads):
    product = left * right
    size = product.shape[0] // heads
    return jnp.concatenate(
        [
            jnp.sum(product[h * size : (h + 1) * size, :], axis=0, keepdims=True)
            for h in range(heads)
        ],
        axis=0,
    )


def delta_kernel(heads, grad_ref, t_ref, spread_ref, r_ref, delta_ref):
    half = grad_ref.shape[1]
    grad_t = grad_ref[0].astype(F32).T
    twice = jnp.concatenate([grad_t, grad_t], axis=1)
    for p in range(heads // 2):
        cols = slice(2 * p * half, (2 * p + 2) * half)
        found = pair_rows(twice, t_ref[0, :, cols].astype(F32), heads)
        r_ref[0, :, cols] = found
        delta_ref[0, :, cols] = jnp.sum(found * spread_ref[:, cols], axis=0, keepdims=True)


def deltas(grad_att, t, spread, heads):
    _, half, width = grad_att.shape
    span = heads * half
    return pl.pallas_call(
        functools.partial(delta_kernel, heads),
        grid=(2,),
        in_specs=[
            pl.BlockSpec((1, half, width), lambda s: (s, 0, 0)),
            pl.BlockSpec((1, width, span), lambda s: (s, 0, 0)),
            pl.BlockSpec((heads, span), lambda s: (0, 0)),
        ],
        out_specs=[
            pl.BlockSpec((1, heads, span), lambda s: (s, 0, 0)),
            pl.BlockSpec((1, 1, span), lambda s: (s, 0, 0)),
        ],
        out_shape=[
            jax.ShapeDtypeStruct((2, heads, span), F32),
            jax.ShapeDtypeStruct((2, 1, span), F32),
        ],
        **params(4 * width * span, 4 * width * span),
    )(grad_att, t, spread)


def back_place(step, own, count):
    low = jnp.minimum(own, count - 1 - own)
    both = step < 2 * (low + 1)
    tile = jnp.where(both, step // 2, step - low - 1)
    part = jnp.where(both, step % 2, jnp.where(own > count - 1 - own, 0, 1))
    return low, both, tile, part


def back_kernel(
    count, heads, group, scale, sc, q_ref, ga_ref, k_ref, v_ref, kt_ref, lse_ref, delta_ref,
    mix_ref, weight_ref, mixc_ref, dk_ref, dv_ref, dq_ref, r_ref,
    fq, fa, total, dk_s, dv_s, bias_s,
):
    half, width = q_ref.shape[1], q_ref.shape[2]
    rows = k_ref.shape[1]
    step = pl.program_id(0)
    own = sc[0]
    low, both, tile, part = back_place(step, own, count)
    query_place = jnp.where(part == 0, own * rows, (count - 1 - own) * rows + half)

    @pl.when(step == 0)
    def start():
        for n in range(2):
            fold(fq, n, q_ref[n], mix_ref, heads, half)
            fold(fa, n, ga_ref[n], weight_ref, heads, half)
        total[...] = jnp.zeros(total.shape, F32)

    @pl.when(jnp.logical_not(both) | (part == 0))
    def clear():
        dk_s[...] = jnp.zeros(dk_s.shape, F32)
        dv_s[...] = jnp.zeros(dv_s.shape, F32)

    bias_s[...] = bias_of(sc, tile * rows, query_place, rows, half)
    span = group * half
    for c in range(heads // group):
        cols = slice(c * span, (c + 1) * span)
        fq_c, fa_c = fq[part, cols, :], fa[part, cols, :]
        logits = dot_nt(k_ref[0], fq_c)
        grad_prob = dot_nt(v_ref[0], fa_c)
        logits = logits + jnp.concatenate([bias_s[...]] * (group // 2), axis=1)
        prob = jnp.exp2(logits - lse_ref[part, :, cols])
        grad_logits = (prob * (grad_prob - delta_ref[part, :, cols])).astype(BF16)
        dv_s[...] += dot(prob.astype(BF16), fa_c)
        dk_s[...] += dot(grad_logits, fq_c)
        total[part, :, cols] += dot(kt_ref[0], grad_logits)

    @pl.when(jnp.logical_not(both) | (part == 1))
    def leave():
        dk_ref[0] = (dk_s[...] * LN2).astype(BF16)
        dv_ref[0] = dv_s[...].astype(BF16)

    @pl.when(step == count)
    def finish():
        for n in range(2):
            q_t = q_ref[n].astype(F32).T
            twice = jnp.concatenate([q_t, q_t], axis=1)
            grad = jnp.zeros((width, half), F32)
            for p in range(heads // 2):
                cols = slice(2 * p * half, (2 * p + 2) * half)
                piece = total[n, :, cols]
                r_ref[n, :, cols] = pair_rows(twice, piece, heads)
                grad += mixc_ref[:, 2 * p : 2 * p + 1] * piece[:, :half]
                grad += mixc_ref[:, 2 * p + 1 : 2 * p + 2] * piece[:, half:]
            dq_ref[n] = (grad.T * scale).astype(BF16)


def back(scalars, q, grad_att, k, v, kt, lse, delta, mix_rows, weight_rows, mix_cols, heads, scale):
    count, rows, width = k.shape
    half = q.shape[1]
    span = heads * half
    tile = lambda s, sc: (sc[HEAD + back_place(s, sc[0], count)[2]], 0, 0)
    whole = lambda s, sc: (0, 0, 0)
    fixed = lambda s, sc: (0, 0)
    group = math.gcd(heads, 4)
    once = pl.Buffered(1)
    return pl.pallas_call(
        functools.partial(back_kernel, count, heads, group, scale),
        grid_spec=pltpu.PrefetchScalarGridSpec(
            num_scalar_prefetch=1,
            grid=(count + 1,),
            in_specs=[
                pl.BlockSpec((2, half, width), whole, pipeline_mode=once),
                pl.BlockSpec((2, half, width), whole, pipeline_mode=once),
                pl.BlockSpec((1, rows, width), tile),
                pl.BlockSpec((1, rows, width), tile),
                pl.BlockSpec((1, width, rows), tile),
                pl.BlockSpec((2, 1, span), whole, pipeline_mode=once),
                pl.BlockSpec((2, 1, span), whole, pipeline_mode=once),
                pl.BlockSpec((heads, width), fixed),
                pl.BlockSpec((heads, width), fixed),
                pl.BlockSpec((width, heads), fixed),
            ],
            out_specs=[
                pl.BlockSpec((1, rows, width), tile),
                pl.BlockSpec((1, rows, width), tile),
                pl.BlockSpec((2, half, width), whole),
                pl.BlockSpec((2, heads, span), whole),
            ],
            scratch_shapes=[
                pltpu.VMEM((2, span, width), BF16),
                pltpu.VMEM((2, span, width), BF16),
                pltpu.VMEM((2, width, span), F32),
                pltpu.VMEM((rows, width), F32),
                pltpu.VMEM((rows, width), F32),
                pltpu.VMEM((rows, 2 * half), F32),
            ],
        ),
        out_shape=[
            jax.ShapeDtypeStruct((count, rows, width), BF16),
            jax.ShapeDtypeStruct((count, rows, width), BF16),
            jax.ShapeDtypeStruct((2, half, width), BF16),
            jax.ShapeDtypeStruct((2, heads, span), F32),
        ],
        **params(10 * (count + 1) * rows * span * width, 10 * count * rows * width),
    )(scalars, q, grad_att, k, v, kt, lse, delta, mix_rows, weight_rows, mix_cols)


def input_kernel(
    count, sc, dk_ref, dv_ref, x_ref, nt_ref, wk_ref, wv_ref, gain_ref, gq_ref, gm_ref,
    part_ref, dwk_ref, dwv_ref, gain_out, grad_s,
):
    rows = x_ref.shape[1]
    half = rows // 2
    j = pl.program_id(0)
    device = sc[HEAD + 2 * count + j]
    own = sc[0]
    valid = sc[HEAD + count + device] <= jnp.maximum(own, count - 1 - own)

    @pl.when(j == 0)
    def start():
        dwk_ref[...] = jnp.zeros(dwk_ref.shape, F32)
        dwv_ref[...] = jnp.zeros(dwv_ref.shape, F32)
        gain_out[...] = jnp.zeros(gain_out.shape, F32)

    @pl.when(valid)
    def seen():
        dk, dv = dk_ref[0], dv_ref[0]
        grad_s[...] = dot_nt(dk, wk_ref[...]) + dot_nt(dv, wv_ref[...])
        dwk_ref[...] += dot(nt_ref[0], dk)
        dwv_ref[...] += dot(nt_ref[0], dv)

    @pl.when(jnp.logical_not(valid))
    def unseen():
        grad_s[...] = jnp.zeros(grad_s.shape, F32)

    @pl.when(device == sc[1])
    def at_own():
        grad_s[:half, :] += gq_ref[0]

    @pl.when(device == sc[2])
    def at_partner():
        grad_s[half:, :] += gq_ref[1]

    x = x_ref[0].astype(F32)
    grad = grad_s[...]
    inverse = lax.rsqrt(jnp.mean(x * x, axis=-1, keepdims=True) + EPS)
    bare = x * inverse
    gained = grad * gain_ref[...]
    gain_out[...] += jnp.sum(grad * bare, axis=0, keepdims=True)
    back_x = inverse * (gained - bare * jnp.mean(gained * bare, axis=-1, keepdims=True))
    part_ref[0] = back_x.astype(BF16)

    @pl.when(device == sc[1])
    def own_rows():
        part_ref[0, :half, :] = (back_x[:half] + gm_ref[0]).astype(BF16)

    @pl.when(device == sc[2])
    def partner_rows():
        part_ref[0, half:, :] = (back_x[half:] + gm_ref[1]).astype(BF16)


def input_parts(scalars, dk, dv, x_rel, nt, wk, wv, gain, gq, gm):
    count, rows, width = x_rel.shape
    place = lambda j, sc: (sc[HEAD + 2 * count + j], 0, 0)
    fixed = lambda j, sc: (0, 0)
    whole = lambda j, sc: (0, 0, 0)
    return pl.pallas_call(
        functools.partial(input_kernel, count),
        grid_spec=pltpu.PrefetchScalarGridSpec(
            num_scalar_prefetch=1,
            grid=(count,),
            in_specs=[
                pl.BlockSpec((1, rows, width), place),
                pl.BlockSpec((1, rows, width), place),
                pl.BlockSpec((1, rows, width), lambda j, sc: (j, 0, 0)),
                pl.BlockSpec((1, width, rows), place),
                pl.BlockSpec((width, width), fixed),
                pl.BlockSpec((width, width), fixed),
                pl.BlockSpec((1, width), fixed),
                pl.BlockSpec((2, rows // 2, width), whole),
                pl.BlockSpec((2, rows // 2, width), whole),
            ],
            out_specs=[
                pl.BlockSpec((1, rows, width), place),
                pl.BlockSpec((width, width), fixed),
                pl.BlockSpec((width, width), fixed),
                pl.BlockSpec((1, width), fixed),
            ],
            scratch_shapes=[pltpu.VMEM((rows, width), F32)],
        ),
        out_shape=[
            jax.ShapeDtypeStruct((count, rows, width), BF16),
            jax.ShapeDtypeStruct((width, width), F32),
            jax.ShapeDtypeStruct((width, width), F32),
            jax.ShapeDtypeStruct((1, width), F32),
        ],
        **params(8 * count * rows * width * width, 10 * count * rows * width),
    )(scalars, dk, dv, x_rel, nt, wk, wv, gain, gq, gm)


def swaps(size, distance):
    return [(i, i ^ distance) for i in range(size)]


def gather_wt(value):
    size = lax.axis_size("wt")
    me = lax.axis_index("wt")
    pieces = [value]
    distance = size // 2
    while distance:
        pieces = pieces + [lax.ppermute(p, "wt", swaps(size, distance)) for p in pieces]
        distance //= 2
    bits = size.bit_length() - 1
    place = [int(format(n, "0%db" % bits)[::-1], 2) for n in range(size)]
    stacked = jnp.stack([pieces[place.index(n)] for n in range(size)])
    return jnp.concatenate(
        [lax.dynamic_index_in_dim(stacked, me ^ r, 0, keepdims=False) for r in range(size)], axis=0
    )


def ring(count):
    return [(i, (i + 2) % count) for i in range(count)]


def gather_ctx(value):
    count = lax.axis_size("ctx")
    pieces = []
    moving = value
    for k in range(count // 2):
        if k:
            moving = lax.ppermute(moving, "ctx", ring(count))
        pieces += [moving, lax.ppermute(moving, "ctx", swaps(count, 1))]
    return pieces


def relative_devices(count, me):
    outer, inner = me // 2, me % 2
    places = []
    for k in range(count // 2):
        base = 2 * jnp.mod(outer - k, count // 2)
        places += [base + inner, base + 1 - inner]
    return jnp.stack(places)


def scatter_ctx(parts):
    count = lax.axis_size("ctx")
    me = lax.axis_index("ctx")
    outer, inner = me // 2, me % 2
    total = None
    for k in range(1, count // 2 + 1):
        base = 2 * jnp.mod(outer - k, count // 2)
        kept = lax.dynamic_index_in_dim(parts, base + inner, 0, keepdims=False)
        sent = lax.dynamic_index_in_dim(parts, base + 1 - inner, 0, keepdims=False)
        found = kept.astype(F32) + lax.ppermute(sent, "ctx", swaps(count, 1)).astype(F32)
        if total is not None:
            found = found + lax.ppermute(total.astype(BF16), "ctx", ring(count)).astype(F32)
        total = found
    return total


def shards(
    residual_in,
    cotangent,
    block_order,
    doc_starts,
    gain_attn,
    w_query,
    w_key,
    w_value,
    mix_logit,
    mix_weight,
    w_output,
    gain_ffn,
    w_in,
    w_out,
):
    rows, width = residual_in.shape[1:]
    half = rows // 2
    heads = mix_logit.shape[1]
    size = width // heads
    scale = size ** (-0.5)
    count = lax.axis_size("ctx")
    me = lax.axis_index("ctx")
    wt_count = lax.axis_size("wt")
    starts = doc_starts[0]

    small = jnp.concatenate(
        [
            gain_attn.reshape(1, -1),
            gain_ffn.reshape(1, -1),
            mix_logit.reshape(1, -1),
            mix_weight.reshape(1, -1),
        ],
        axis=1,
    )
    small = lax.all_gather(small, "wt", axis=0, tiled=True).astype(F32)
    n_gain = gain_attn.shape[0]
    n_mix = mix_logit.size
    gain_one = small[:, :n_gain].reshape(1, width)
    gain_two = small[:, n_gain : 2 * n_gain].reshape(1, width)
    logit_mix = small[:, 2 * n_gain : 2 * n_gain + n_mix].reshape(heads, heads)
    weight_mix = small[:, 2 * n_gain + n_mix :].reshape(heads, heads)

    x_own = residual_in[0]
    x_rel = jnp.stack(gather_ctx(x_own))
    qkv_mat = gather_wt(jnp.concatenate([w_query, w_key, w_value], axis=1))
    query_mat, key_mat, value_mat = (qkv_mat[:, n * width : (n + 1) * width] for n in range(3))
    output_mat = lax.all_gather(w_output, "wt", axis=0, tiled=True)
    inner_mat = lax.all_gather(w_in, "wt", axis=0, tiled=True)
    outer_mat = lax.all_gather(w_out, "wt", axis=0, tiled=True)

    order = block_order.astype(jnp.int32)
    devices = jnp.arange(count, dtype=jnp.int32)
    by_block = jnp.sum(jnp.where(order[None, :] == devices[:, None], devices[None, :], 0), axis=1)
    own = order[me]
    partner = by_block[count - 1 - own]
    relative = relative_devices(count, me).astype(jnp.int32)
    partner_place = jnp.sum(jnp.where(relative == partner, devices, 0))
    scalars = jnp.concatenate(
        [jnp.stack([own, me.astype(jnp.int32), partner, starts[1], starts[2]]), by_block, order, relative]
    ).astype(jnp.int32)

    mix_by_g = jnp.repeat(logit_mix.T, size, axis=1)
    weight_by_g = jnp.repeat(weight_mix, size, axis=1)
    mix_rows = mix_by_g * (scale * LOG2E)
    spread = jnp.repeat(weight_mix.T, half, axis=1)

    k, v, kt, vt, nt = project(scalars, x_rel, gain_one, key_mat, value_mat)
    x_two = lax.dynamic_index_in_dim(x_rel, partner_place, 0, keepdims=False)[half:]
    x_low = jnp.concatenate([x_own[:half], x_two], axis=0)
    inputs = x_low.astype(F32)
    normed_low = rms_norm(inputs, gain_one).astype(BF16)
    q = dot(normed_low, query_mat).astype(BF16).reshape(2, half, width)

    def exchange(second):
        every = lax.all_gather(second, "ctx", axis=0)
        return lax.dynamic_index_in_dim(every, partner, 0, keepdims=False)

    dy_low = jnp.concatenate([cotangent[0, :half], exchange(cotangent[0, half:])], axis=0)

    attended, t, lse = attend(scalars, q, k, vt, mix_rows, weight_by_g.T, heads)
    attended_low = attended.reshape(rows, width)

    branch = dot(attended_low, output_mat)
    middle = inputs + branch
    normed_two, norm_two_back = jax.vjp(rms_norm, middle, gain_two)
    normed_two_low = normed_two.astype(BF16)
    hidden = dot(normed_two_low, inner_mat)
    active, gelu_back = jax.vjp(gelu_tanh, hidden)
    active_low = active.astype(BF16)
    feed = dot(active_low, outer_mat)
    output = middle + feed
    squares = jnp.stack([jnp.sum(output * output), jnp.sum(branch * branch), jnp.sum(feed * feed)])
    out_low = output.astype(BF16)
    output_own = jnp.concatenate([out_low[:half], exchange(out_low[half:])], axis=0)

    grad_outer = jnp.einsum("ti,to->io", active_low, dy_low, preferred_element_type=F32)
    grad_active = dot_nt(dy_low, outer_mat)
    grad_hidden_low = gelu_back(grad_active)[0].astype(BF16)
    grad_inner = jnp.einsum("ti,tf->if", normed_two_low, grad_hidden_low, preferred_element_type=F32)
    grad_normed_two = dot_nt(grad_hidden_low, inner_mat)
    grad_mid_norm, grad_gain_two = norm_two_back(grad_normed_two)
    grad_middle = dy_low.astype(F32) + grad_mid_norm
    grad_branch_low = grad_middle.astype(BF16)
    grad_output_mat = jnp.einsum(
        "ti,to->io", attended_low, grad_branch_low, preferred_element_type=F32
    )
    grad_att = dot_nt(grad_branch_low, output_mat).astype(BF16).reshape(2, half, width)

    def reduce(values):
        share = lax.psum_scatter(values.astype(BF16), "wt", scatter_dimension=0, tiled=True)
        return lax.psum(share, "ctx")

    grad_outer_own = reduce(grad_outer)
    grad_inner_own = reduce(grad_inner)
    grad_output_own = reduce(grad_output_mat)

    r_weight, delta = deltas(grad_att, t, spread, heads)
    dk, dv, dq, r_logit = back(
        scalars, q, grad_att, k, v, kt, lse, delta, mix_rows, weight_by_g, mix_by_g.T, heads, scale
    )
    dq_low = dq.reshape(rows, width)
    gq = dot_nt(dq_low, query_mat).reshape(2, half, width)
    grad_query_mat = jnp.einsum("ti,to->io", normed_low, dq_low, preferred_element_type=F32)
    parts, grad_key_mat, grad_value_mat, grad_gain_one = input_parts(
        scalars, dk, dv, x_rel, nt, key_mat, value_mat, gain_one, gq,
        grad_middle.reshape(2, half, width),
    )
    input_grad = scatter_ctx(parts).astype(BF16)
    qkv_own = reduce(jnp.concatenate([grad_query_mat, grad_key_mat, grad_value_mat], axis=1))

    by_heads = lambda found: jnp.sum(found.reshape(2, heads, heads, half), axis=(0, 3))
    grad_mix_weight = by_heads(r_weight).T
    grad_mix_logit = by_heads(r_logit) * scale
    shared = jnp.concatenate(
        [
            squares,
            grad_gain_one.reshape(-1),
            grad_gain_two.reshape(-1),
            grad_mix_logit.reshape(-1),
            grad_mix_weight.reshape(-1),
        ]
    )
    shared = lax.psum(shared, ("ctx", "wt"))
    entries = float(rows * width) * (count * wt_count)
    rms_values = jnp.sqrt(shared[:3] / entries)
    wt_me = lax.axis_index("wt")

    def own_rows(first, full):
        piece = shared[first : first + math.prod(full)].reshape(full)
        per = full[0] // wt_count
        return lax.dynamic_slice_in_dim(piece, wt_me * per, per, 0)

    grad_gain_one_own = own_rows(3, (width,))
    grad_gain_two_own = own_rows(3 + width, (width,))
    grad_mix_logit_own = own_rows(3 + 2 * width, (heads, heads))
    grad_mix_weight_own = own_rows(3 + 2 * width + heads * heads, (heads, heads))

    return (
        output_own[None],
        input_grad[None],
        rms_values,
        grad_gain_one_own,
        qkv_own[:, :width].astype(F32),
        qkv_own[:, width : 2 * width].astype(F32),
        qkv_own[:, 2 * width :].astype(F32),
        grad_mix_logit_own,
        grad_mix_weight_own,
        grad_output_own.astype(F32),
        grad_gain_two_own,
        grad_inner_own.astype(F32),
        grad_outer_own.astype(F32),
    )


def solution(mesh):
    tokens = P("wt", "ctx", None)
    matrix = P("wt", None)
    vector = P("wt")
    return jax.shard_map(
        shards,
        mesh=mesh,
        in_specs=(tokens, tokens, P(), matrix, vector)
        + (matrix,) * 6
        + (vector, matrix, matrix),
        out_specs=(tokens, tokens, P(), vector) + (matrix,) * 6 + (vector, matrix, matrix),
        check_vma=False,
    )
```

time: 3000 us -> 747 us (0.25)
  matrix products: 1230 us -> 50.3 us
  waiting for transfers between devices: 820 us -> 314 us
  local copies, waits for them, and re-layouts: 380 us -> 35 us
  Pallas kernels: 0 us -> 197 us
  starting transfers between devices: 215 us -> 25.2 us
  other arithmetic: 187 us -> 26 us
  loops' own time: 39.7 us -> 0 us
    dot_general x111 -> x10, matrix products: 1220 us -> 43.9 us  [the longest x4 19.5 us: dot(): return jnp.dot(left, right, preferred_element_type=F32)]
    ppermute x16 -> x17, waiting for transfers between devices: 491 us -> 94.8 us  [the longest x3 37.3 us: gather_ctx(): moving = lax.ppermute(moving, 'ctx', ring(count))]
    mul x12 -> x4, local copies, waits for them, and re-layouts: 208 us -> 1.01 us  [the longest x1 0.77 us: shards(): mix_rows = mix_by_g * (scale * LOG2E)]
    pallas_call x0 -> x5, Pallas kernels: none -> 197 us  [the longest x1 88 us: back(): pl.pallas_call(functools.partial(back_kernel, count, heads, group, scale)...]
    ppermute x16 -> x17, starting transfers between devices: 215 us -> 24.8 us  [the longest x3 8.38 us: gather_ctx(): moving = lax.ppermute(moving, 'ctx', ring(count))]
    all_gather x8 -> x5, waiting for transfers between devices: 101 us -> 0.03 us  [the longest x1 0.02 us: shards(): output_mat = lax.all_gather(w_output, 'wt', axis=0, tiled=True)]
    dot_general x4 -> x0, local copies, waits for them, and re-layouts: 68.9 us -> none  [delta_compute(): jnp.einsum('qhd,khd->hqk', grad_heads, value_heads, preferred_element_typ...]
    convert_element_type x32 -> x7, other arithmetic: 66 us -> 11.2 us  [the longest x3 4.57 us: scatter_ctx(): total.astype(BF16)]
  transfers between devices with their start and end apart: 31 -> 27, of which waited for: 25 -> 10; matrix products, arithmetic and copies ran while one was open for 59% -> 11% of each run, Pallas kernels for 0% -> 26%
where the time goes in v1:
time: 747 us; the launch traced here: 743 us
  waiting for transfers between devices  314 us (42%)
  Pallas kernels  197 us (26%)
  blocking collectives  75.5 us (10%)
  matrix products  50.3 us (7%)
  local copies, waits for them, and re-layouts  35 us (5%)
  other arithmetic  26 us (3%)
  starting transfers between devices  25.2 us (3%)
  between operations  20.5 us (3%)
    reduce_scatter x4, waiting for transfers between devices, reduce(): lax.psum_scatter(values.astype(BF16), 'wt', scatter_dimension=0, tiled=True)  118 us
    psum x1, waiting for transfers between devices, reduce(): return lax.psum(share, 'ctx')  99.7 us
    pallas_call x1, Pallas kernels, back(): pl.pallas_call(functools.partial(back_kernel, count, heads, group, scale)...  88 us
    pallas_call x1, Pallas kernels, attend(): pl.pallas_call(functools.partial(attend_kernel, count, heads, group), gri...  58.1 us
    psum x1, blocking collectives, shards(): shared = lax.psum(shared, ('ctx', 'wt'))  51.3 us
    ppermute x3, waiting for transfers between devices, gather_ctx(): moving = lax.ppermute(moving, 'ctx', ring(count))  37.3 us
    ppermute x3, waiting for transfers between devices, scatter_ctx(): lax.ppermute(total.astype(BF16), 'ctx', ring(count)).astype(F32)  33.7 us
    pallas_call x1, Pallas kernels, input_parts(): pl.pallas_call(functools.partial(input_kernel, count), grid_spec=pltpu.Pr...  29.7 us
  transfers between devices with their start and end apart: 27, of which 10 were waited for; matrix products, arithmetic and copies ran while one was open for 11% of the time, Pallas kernels for 26%

profile of v1, /device:TPU:0, one launch (start us, length us, event | category | flops | bytes accessed | tf_op | source)
XLA Modules:
  0.0 743.3 jit_solution(452348090899921764)
XLA Ops:
  19.4 24.2 %all-gather.1 = bf16[4,1,456]{2,1,0:T(2,128)(2,1)S(1)} all-gather(bf16[1,1,456]{2,1,0:T(2,128)(2,1)S(1)} %maximum_bitcast_fusion.1), channel_id=1, replica_groups=mesh['ctx'=8,'wt'=4] {'wt'}, dimensions={0}, use_global_device_ids=true | all-gather | bytes 4560 | tf_op jit(solution)/shard_map/all_gather | solution.py:550
  61.0 19.8 %collective-permute-done.3 = bf16[384,768]{1,0:T(8,128)(2,1)S(1)} collective-permute-done((bf16[384,768]{1,0:T(8,128)(2,1)S(1)}, bf16[384,768]{1,0:T(8,128)(2,1)S(1)}, u32[]{:S(2)}, u32[]{:S(2)}) %collective-permute-start.3) | collective-permute-done | bytes 589856 | tf_op jit(solution)/shard_map/ppermute | solution.py:485
  82.4 5.2 collective-permute-start.5
  89.5 17.4 %collective-permute-done.5 = bf16[384,768]{1,0:T(8,128)(2,1)S(1)} collective-permute-done((bf16[384,768]{1,0:T(8,128)(2,1)S(1)}, bf16[384,768]{1,0:T(8,128)(2,1)S(1)}, u32[]{:S(2)}, u32[]{:S(2)}) %collective-permute-start.5) | collective-permute-done | bytes 589856 | tf_op jit(solution)/shard_map/ppermute | solution.py:485
  110.4 10.5 %collective-permute-done.6 = bf16[384,768]{1,0:T(8,128)(2,1)S(1)} collective-permute-done((bf16[384,768]{1,0:T(8,128)(2,1)S(1)}, bf16[384,768]{1,0:T(8,128)(2,1)S(1)}, u32[]{:S(2)}, u32[]{:S(2)}) %collective-permute-start.6) | collective-permute-done | bytes 589856 | tf_op jit(solution)/shard_map/ppermute | solution.py:486
  123.3 15.4 %shard_map.237 = (bf16[8,384,768]{2,1,0:T(8,128)(2,1)}, bf16[8,384,768]{2,1,0:T(8,128)(2,1)}, bf16[8,768,384]{2,1,0:T(8,128)(2,1)}, bf16[8,768,384]{2,1,0:T(8,128)(2,1)}, bf16[8,768,384]{2,1,0:T(8,128)(2,1)}) custom-call(s32[29]{0:T(128)} %concatenate.30.sc, bf16[8,384,768]{2,1,0:T(8,128)(2,1)} %copy-done.23, f32[1,768]{1,0:T(1,128)} %reshape.143.gain_ref, ...), custom_call_target="tpu_custom_call" | custom-call | flops 7247757312 | bytes 28311552 | tf_op jit(solution)/shard_map/pallas_call | solution.py:67
  138.7 58.1 %shard_map.238 = (bf16[2,192,768]{2,1,0:T(8,128)(2,1)}, bf16[2,768,2304]{2,1,0:T(8,128)(2,1)}, f32[2,1,2304]{2,1,0:T(1,128)}) custom-call(s32[29]{0:T(128)} %concatenate.30.sc, bf16[2,192,768]{2,1,0:T(8,128)(2,1)} %bitcast.134, bf16[8,384,768]{2,1,0:T(8,128)(2,1)} %get-tuple-element.31.k_ref, bf16[8,768,384]{2,1,0:T(8,128)(2,1)} %get-tuple-element.32.vt_ref, ...), custom_call_target="tpu_custom_call" | custom-call | flops 24461180928 | bytes 14155776 | tf_op jit(solution)/shard_map/pallas_call | solution.py:165
  196.8 3.9 multiply_reduce_fusion.5
  203.0 7.0 fusion.33
  210.0 6.7 fusion.34
  216.8 5.8 fusion.6
  232.8 5.4 shard_map.239
  239.0 88.0 %shard_map.240 = (bf16[8,384,768]{2,1,0:T(8,128)(2,1)}, bf16[8,384,768]{2,1,0:T(8,128)(2,1)}, bf16[2,192,768]{2,1,0:T(8,128)(2,1)}, f32[2,12,2304]{2,1,0:T(8,128)}) custom-call(s32[29]{0:T(128)} %concatenate.30.sc, bf16[2,192,768]{2,1,0:T(8,128)(2,1)} %bitcast.135, bf16[2,192,768]{2,1,0:T(8,128)(2,1)} %bitcast.114, ...), custom_call_target="tpu_custom_call" | custom-call | flops 61152952320 | bytes 23592960 | tf_op jit(solution)/shard_map/pallas_call | solution.py:320
  329.8 29.7 %shard_map.241 = (bf16[8,384,768]{2,1,0:T(8,128)(2,1)}, f32[768,768]{1,0:T(8,128)}, f32[768,768]{1,0:T(8,128)}, f32[1,768]{1,0:T(1,128)}) custom-call(s32[29]{0:T(128)} %concatenate.30.sc, bf16[8,384,768]{2,1,0:T(8,128)(2,1)} %get-tuple-element.39.dk_ref, bf16[8,384,768]{2,1,0:T(8,128)(2,1)} %get-tuple-element.40.dv_ref, bf16[8,384,768]{2,1,0:T(8,128)(2,1)} %copy-done.23, ...), custom_call_target="tpu_custom_call" | custom-call | flops 14495514624 | bytes 23592960 | tf_op jit(solution)/shard_map/pallas_call | solution.py:421
  367.7 4.6 convolution_convert_fusion.1
  373.4 8.1 %convolution_convert_fusion = bf16[3072,768]{1,0:T(8,128)(2,1)} fusion(bf16[192,768]{1,0:T(8,128)(2,1)S(1)} %copy-done.4, bf16[192,768]{1,0:T(8,128)(2,1)S(1)} %copy-done.8, f32[384,3072]{1,0:T(8,128)} %fusion.33), kind=kOutput, calls=%fused_computation.2 | convolution fusion | flops 1826095104 | bytes 10027008 | tf_op jit(solution)/shard_map/ti,to->io/dot_general | solution.py:611
  388.8 17.2 %reduce-scatter.5.cloned.1.call-done = bf16[192,2304]{1,0:T(8,128)(2,1)} async-done(((bf16[768,2304]{1,0:T(8,128)(2,1)}), bf16[192,2304]{1,0:T(8,128)(2,1)}) %reduce-scatter.5.cloned.1.call-update) | async-done | bytes 884752 | tf_op jit(solution)/shard_map/reduce_scatter | solution.py:625
  406.0 50.4 %reduce-scatter.9.cloned.1.call-done = bf16[192,3072]{1,0:T(8,128)(2,1)} async-done(((bf16[768,3072]{1,0:T(8,128)(2,1)}), bf16[192,3072]{1,0:T(8,128)(2,1)}) %reduce-scatter.9.cloned.1.call-update) | async-done | bytes 1179664 | tf_op jit(solution)/shard_map/reduce_scatter | solution.py:625
  456.4 50.6 %reduce-scatter.11.cloned.1.call-done = bf16[768,768]{1,0:T(8,128)(2,1)} async-done(((bf16[3072,768]{1,0:T(8,128)(2,1)}), bf16[768,768]{1,0:T(8,128)(2,1)}) %reduce-scatter.11.cloned.1.call-update) | async-done | bytes 1179664 | tf_op jit(solution)/shard_map/reduce_scatter | solution.py:625
  512.6 13.4 %collective-permute-done.12 = bf16[384,768]{1,0:T(8,128)(2,1)S(1)} collective-permute-done((bf16[384,768]{1,0:T(8,128)(2,1)S(1)}, bf16[384,768]{1,0:T(8,128)(2,1)S(1)}, u32[]{:S(2)}, u32[]{:S(2)}) %collective-permute-start.12) | collective-permute-done | bytes 589856 | tf_op jit(solution)/shard_map/ppermute | solution.py:508
  526.0 7.7 %collective-permute-done.14 = bf16[384,768]{1,0:T(8,128)(2,1)S(1)} collective-permute-done((bf16[384,768]{1,0:T(8,128)(2,1)}, bf16[384,768]{1,0:T(8,128)(2,1)S(1)}, u32[]{:S(2)}, u32[]{:S(2)}) %collective-permute-start.14) | collective-permute-done | bytes 589856 | tf_op jit(solution)/shard_map/ppermute | solution.py:510
  543.0 51.3 %psum.35 = f32[1827]{0:T(1024)S(1)} all-reduce(f32[1827]{0:T(1024)S(1)} %concatenate.36), channel_id=1, replica_groups=mesh['ctx'=8,'wt'=4] {'ctx','wt'}, use_global_device_ids=true, to_apply=%region_13.14 | all-reduce | flops 1827 | bytes 14616 | tf_op jit(solution)/shard_map/psum | solution.py:658
  600.1 25.9 %collective-permute-done.16 = bf16[384,768]{1,0:T(8,128)(2,1)S(1)} collective-permute-done((bf16[384,768]{1,0:T(8,128)(2,1)S(1)}, bf16[384,768]{1,0:T(8,128)(2,1)S(1)}, u32[]{:S(2)}, u32[]{:S(2)}) %collective-permute-start.16) | collective-permute-done | bytes 589856 | tf_op jit(solution)/shard_map/ppermute | solution.py:510
  629.9 99.7 %all-reduce.3.cloned.1.call-done = (bf16[192,2304]{1,0:T(8,128)(2,1)}, bf16[192,768]{1,0:T(8,128)(2,1)}, bf16[192,3072]{1,0:T(8,128)(2,1)}, bf16[768,768]{1,0:T(8,128)(2,1)}) async-done(((bf16[192,2304]{1,0:T(8,128)(2,1)}, bf16[192,768]{1,0:T(8,128)(2,1)}, bf16[192,3072]{1,0:T(8,128)(2,1)}, bf16[768,768]{1,0:T(8,128)(2,1)}), (bf16[192,2304]{1,0:T(8,128)(2,1)}, bf16[192,768]{1,0:T(8,128)(2,1)}, ...) | async-done | bytes 3538960 | tf_op jit(solution)/shard_map/psum | solution.py:626
  (236 shorter events, 96.8 us)
Async XLA Ops:
  7.2 189.6 %all-gather.8.cloned.1.call-start = ((), (), s32[]{:S(2)}) async-start(), calls=%async_computation.4 | async-start | bytes 1474560 | tf_op jit(solution)/shard_map/all_gather | solution.py:562
  8.0 193.3 %all-gather.14.cloned.1.call-start = ((), (), s32[]{:S(2)}) async-start(), calls=%async_computation.7 | async-start | bytes 2654208 | tf_op jit(solution)/shard_map/all_gather | solution.py:590
  10.0 193.0 %all-gather.10.cloned.1.call-start = ((), (), s32[]{:S(2)}) async-start(), calls=%async_computation.5 | async-start | bytes 5898240 | tf_op jit(solution)/shard_map/all_gather | solution.py:563
  10.7 199.3 %all-gather.12.cloned.1.call-start = ((), (), s32[]{:S(2)}) async-start(), calls=%async_computation.6 | async-start | bytes 5898240 | tf_op jit(solution)/shard_map/all_gather | solution.py:564
  10.7 49.0 %collective-permute-start = (bf16[384,768]{1,0:T(8,128)(2,1)S(1)}, bf16[384,768]{1,0:T(8,128)(2,1)}, u32[]{:S(2)}, u32[]{:S(2)}) collective-permute-start(bf16[384,768]{1,0:T(8,128)(2,1)S(1)} %bitcast.116), channel_id=1, source_target_pairs={{0,4},{4,0},{8,12},{12,8},{16,20},{20,16},{24,28},{28,24},{1,5},{5... | collective-permute-start | bytes 1769480 | tf_op jit(solution)/shard_map/ppermute | solution.py:486
  13.8 43.7 %collective-permute-start.1 = (bf16[384,768]{1,0:T(8,128)(2,1)S(1)}, bf16[384,768]{1,0:T(8,128)(2,1)S(1)}, u32[]{:S(2)}, u32[]{:S(2)}) collective-permute-start(bf16[384,768]{1,0:T(8,128)(2,1)S(1)} %bitcast.117), channel_id=1, source_target_pairs={{0,8},{4,12},{8,16},{12,20},{16,24},{20,28},{24,0},{28,4},{1,9},{5... | collective-permute-start | bytes 1769480 | tf_op jit(solution)/shard_map/ppermute | solution.py:485
  15.5 44.2 %collective-permute-start.8 = (bf16[192,2304]{1,0:T(8,128)(2,1)S(1)}, bf16[192,2304]{1,0:T(8,128)(2,1)S(1)}, u32[]{:S(2)}, u32[]{:S(2)}) collective-permute-start(bf16[192,2304]{1,0:T(8,128)(2,1)S(1)} %constant_dynamic-update-slice_fusion.1), channel_id=1, source_target_pairs={{0,2},{1,3},{2,0},{3,1},{4,6},{5,7},{6,4},{7,5},{8,10},{9,11},{10,... | collective-permute-start | bytes 2654216 | tf_op jit(solution)/shard_map/ppermute | solution.py:465
  17.0 70.7 %collective-permute-start.7 = (bf16[192,2304]{1,0:T(8,128)(2,1)S(1)}, bf16[192,2304]{1,0:T(8,128)(2,1)}, u32[]{:S(2)}, u32[]{:S(2)}) collective-permute-start(bf16[192,2304]{1,0:T(8,128)(2,1)S(1)} %constant_dynamic-update-slice_fusion.1), channel_id=1, source_target_pairs={{0,1},{1,0},{2,3},{3,2},{4,5},{5,4},{6,7},{7,6},{8,9},{9,8},{10,11... | collective-permute-start | bytes 2654216 | tf_op jit(solution)/shard_map/ppermute | solution.py:465
  17.1 371.7 %reduce-scatter.7.cloned.1.call-start = ((), (), s32[]{:S(2)}) async-start(), calls=%async_computation.9 | async-start | bytes 1474560 | tf_op jit(solution)/shard_map/reduce_scatter | solution.py:625
  57.5 30.1 %collective-permute-start.2 = (bf16[384,768]{1,0:T(8,128)(2,1)S(1)}, bf16[384,768]{1,0:T(8,128)(2,1)S(1)}, u32[]{:S(2)}, u32[]{:S(2)}) collective-permute-start(bf16[384,768]{1,0:T(8,128)(2,1)S(1)} %collective-permute-done.1), channel_id=1, source_target_pairs={{0,4},{4,0},{8,12},{12,8},{16,20},{20,16},{24,28},{28,24},{1,5},{5... | collective-permute-start | bytes 1769480 | tf_op jit(solution)/shard_map/ppermute | solution.py:486
  59.7 28.0 %collective-permute-start.9 = (bf16[192,2304]{1,0:T(8,128)(2,1)S(1)}, bf16[192,2304]{1,0:T(8,128)(2,1)S(1)}, u32[]{:S(2)}, u32[]{:S(2)}) collective-permute-start(bf16[192,2304]{1,0:T(8,128)(2,1)S(1)} %collective-permute-done.8), channel_id=1, source_target_pairs={{0,1},{1,0},{2,3},{3,2},{4,5},{5,4},{6,7},{7,6},{8,9},{9,8},{10,11... | collective-permute-start | bytes 2654216 | tf_op jit(solution)/shard_map/ppermute | solution.py:465
  80.8 27.9 %collective-permute-start.4 = (bf16[384,768]{1,0:T(8,128)(2,1)S(1)}, bf16[384,768]{1,0:T(8,128)(2,1)S(1)}, u32[]{:S(2)}, u32[]{:S(2)}) collective-permute-start(bf16[384,768]{1,0:T(8,128)(2,1)S(1)} %collective-permute-done.3), channel_id=1, source_target_pairs={{0,4},{4,0},{8,12},{12,8},{16,20},{20,16},{24,28},{28,24},{1,5},{5... | collective-permute-start | bytes 1769480 | tf_op jit(solution)/shard_map/ppermute | solution.py:486
  82.4 24.5 %collective-permute-start.5 = (bf16[384,768]{1,0:T(8,128)(2,1)S(1)}, bf16[384,768]{1,0:T(8,128)(2,1)S(1)}, u32[]{:S(2)}, u32[]{:S(2)}) collective-permute-start(bf16[384,768]{1,0:T(8,128)(2,1)S(1)} %collective-permute-done.3), channel_id=1, source_target_pairs={{0,8},{4,12},{8,16},{12,20},{16,24},{20,28},{24,0},{28,4},{1,9},{5... | collective-permute-start | bytes 1769480 | tf_op jit(solution)/shard_map/ppermute | solution.py:485
  229.7 176.3 %reduce-scatter.5.cloned.1.call-start = ((), (), s32[]{:S(2)}) async-start(), calls=%async_computation.8 | async-start | bytes 4423680 | tf_op jit(solution)/shard_map/reduce_scatter | solution.py:625
  365.7 90.7 %reduce-scatter.9.cloned.1.call-start = ((), (), s32[]{:S(2)}) async-start(), calls=%async_computation.10 | async-start | bytes 5898240 | tf_op jit(solution)/shard_map/reduce_scatter | solution.py:625
  372.3 134.6 %reduce-scatter.11.cloned.1.call-start = ((), (), s32[]{:S(2)}) async-start(), calls=%async_computation.11 | async-start | bytes 5898240 | tf_op jit(solution)/shard_map/reduce_scatter | solution.py:625
  381.5 246.6 %all-gather.16.cloned.1.call-start = ((), (), s32[]{:S(2)}) async-start(), calls=%async_computation.12 | async-start | bytes 2654208 | tf_op jit(solution)/shard_map/all_gather | solution.py:590
  383.3 346.3 %all-reduce.3.cloned.1.call-start = ((), (), s32[]{:S(2)}) async-start(), calls=%async_computation.13 | async-start | bytes 7077888 | tf_op jit(solution)/shard_map/psum | solution.py:626
  386.2 122.3 %collective-permute-start.13 = (bf16[384,768]{1,0:T(8,128)(2,1)S(1)}, bf16[384,768]{1,0:T(8,128)(2,1)S(1)}, u32[]{:S(2)}, u32[]{:S(2)}) collective-permute-start(bf16[384,768]{1,0:T(8,128)(2,1)S(1)} %get-tuple-element.60), channel_id=1, source_target_pairs={{0,4},{4,0},{8,12},{12,8},{16,20},{20,16},{24,28},{28,24},{1,5},{5... | collective-permute-start | bytes 1769480 | tf_op jit(solution)/shard_map/ppermute | solution.py:508
  510.6 23.1 %collective-permute-start.14 = (bf16[384,768]{1,0:T(8,128)(2,1)}, bf16[384,768]{1,0:T(8,128)(2,1)S(1)}, u32[]{:S(2)}, u32[]{:S(2)}) collective-permute-start(bf16[384,768]{1,0:T(8,128)(2,1)} %fusion.11), channel_id=1, source_target_pairs={{0,8},{4,12},{8,16},{12,20},{16,24},{20,28},{24,0},{28,4},{1,9},{5... | collective-permute-start | bytes 1769480 | tf_op jit(solution)/shard_map/ppermute | solution.py:510
  512.0 82.3 %collective-permute-start.11 = (bf16[384,768]{1,0:T(8,128)(2,1)}, bf16[384,768]{1,0:T(8,128)(2,1)S(1)}, u32[]{:S(2)}, u32[]{:S(2)}) collective-permute-start(bf16[384,768]{1,0:T(8,128)(2,1)} %get-tuple-element.62), channel_id=1, source_target_pairs={{0,4},{4,0},{8,12},{12,8},{16,20},{20,16},{24,28},{28,24},{1,5},{5... | collective-permute-start | bytes 1769480 | tf_op jit(solution)/shard_map/ppermute | solution.py:508
  535.0 59.3 %collective-permute-start.15 = (bf16[384,768]{1,0:T(8,128)(2,1)S(1)}, bf16[384,768]{1,0:T(8,128)(2,1)S(1)}, u32[]{:S(2)}, u32[]{:S(2)}) collective-permute-start(bf16[384,768]{1,0:T(8,128)(2,1)S(1)} %fusion.13), channel_id=1, source_target_pairs={{0,8},{4,12},{8,16},{12,20},{16,24},{20,28},{24,0},{28,4},{1,9},{5... | collective-permute-start | bytes 1769480 | tf_op jit(solution)/shard_map/ppermute | solution.py:510
  535.2 64.9 %collective-permute-start.10 = (bf16[384,768]{1,0:T(8,128)(2,1)S(1)}, bf16[384,768]{1,0:T(8,128)(2,1)S(1)}, u32[]{:S(2)}, u32[]{:S(2)}) collective-permute-start(bf16[384,768]{1,0:T(8,128)(2,1)S(1)} %get-tuple-element.59), channel_id=1, source_target_pairs={{0,4},{4,0},{8,12},{12,8},{16,20},{20,16},{24,28},{28,24},{1,5},{5... | collective-permute-start | bytes 1769480 | tf_op jit(solution)/shard_map/ppermute | solution.py:508
  595.6 30.4 %collective-permute-start.16 = (bf16[384,768]{1,0:T(8,128)(2,1)S(1)}, bf16[384,768]{1,0:T(8,128)(2,1)S(1)}, u32[]{:S(2)}, u32[]{:S(2)}) collective-permute-start(bf16[384,768]{1,0:T(8,128)(2,1)S(1)} %fusion.15), channel_id=1, source_target_pairs={{0,8},{4,12},{8,16},{12,20},{16,24},{20,28},{24,0},{28,4},{1,9},{5... | collective-permute-start | bytes 1769480 | tf_op jit(solution)/shard_map/ppermute | solution.py:510
  (47 other events, 458.3 us)
Sparse Core Ops, SparseCore 0:
  9.6 26.5 all-gather.7
  39.0 64.3 all-gather.13
  105.0 35.8 all-gather.9
  142.2 37.4 all-gather.11
  229.8 23.9 reduce-scatter.6
  365.8 40.1 reduce-scatter.4
  408.5 47.8 reduce-scatter.8
  459.1 47.8 reduce-scatter.10
  509.7 64.1 all-gather.15
  577.8 151.8 all-reduce.2

commit v2 on v1

v2 whole, which is shorter than its diff:
```python
import functools
import math

import jax
import jax.numpy as jnp
from jax import lax
from jax.experimental import pallas as pl
from jax.experimental.pallas import tpu as pltpu
from jax.sharding import PartitionSpec as P

NEG = -1e30
EPS = 1e-06
LOG2E = 1.4426950408889634
LN2 = 0.6931471805599453
F32 = jnp.float32
BF16 = jnp.bfloat16
NT = (((1,), (1,)), ((), ()))
VMEM_BYTES = 60 * 1024 * 1024


def dot(left, right):
    return jnp.dot(left, right, preferred_element_type=F32)


def dot_nt(left, right):
    return lax.dot_general(left, right, NT, preferred_element_type=F32)


def rms_norm(values, gain):
    return values * lax.rsqrt(jnp.mean(values * values, axis=-1, keepdims=True) + EPS) * gain


def gelu_tanh(values):
    return jax.nn.gelu(values, approximate=True)


def params(flops, moved, dims=1):
    return dict(
        compiler_params=pltpu.CompilerParams(
            dimension_semantics=("arbitrary",) * dims, vmem_limit_bytes=VMEM_BYTES
        ),
        cost_estimate=pl.CostEstimate(flops=flops, bytes_accessed=moved, transcendentals=0),
    )


HEAD = 6


def assemble(me, target, pieces, per, cols=slice(None)):
    for n, piece in enumerate(pieces):
        rows = pl.ds(pl.multiple_of((me ^ n) * per, per), per)
        target[rows, :] = piece[:per, cols]


def project_kernel(batch, shares, sc, *refs):
    pieces, (gain_ref, *weights) = refs[:batch], refs[batch : batch + 1 + max(1, len(shares))]
    outs = refs[-(7 if shares else 6) :]
    k_ref, v_ref, kt_ref, vt_ref, nt_ref, x_out = outs[:6]
    width = x_out.shape[2]
    mat = outs[6] if shares else weights[0]
    if shares:

        @pl.when(pl.program_id(0) == 0)
        def start():
            assemble(sc[5], mat, weights, width // len(weights))

    def one(x_ref):
        x_low = x_ref[...]
        x_out[0] = x_low
        normed = rms_norm(x_low.astype(F32), gain_ref[...]).astype(BF16)
        nt_ref[0] = normed.T
        k = dot(normed, mat[:, :width]).astype(BF16)
        k_ref[0] = k
        kt_ref[0] = k.T
        v = dot(normed, mat[:, width:]).astype(BF16)
        v_ref[0] = v
        vt_ref[0] = v.T

    for n in range(batch):
        pl.when(pl.program_id(0) == n)(functools.partial(one, pieces[n]))


def project(scalars, count, first, pieces, gain, mat, before):
    batch = len(pieces)
    rows, width = pieces[0].shape
    place = lambda j, sc: (sc[HEAD + 2 * count + first + j], 0, 0)
    fixed = lambda j, sc: (0, 0)
    tall = jax.ShapeDtypeStruct((count, rows, width), BF16)
    wide = jax.ShapeDtypeStruct((count, width, rows), BF16)
    once = pl.Buffered(1)
    before = () if before is None else tuple(before)
    shares = tuple(mat) if isinstance(mat, (list, tuple)) else ()
    weights = shares or (mat,)
    out_specs = [
        pl.BlockSpec((1, rows, width), place),
        pl.BlockSpec((1, rows, width), place),
        pl.BlockSpec((1, width, rows), place),
        pl.BlockSpec((1, width, rows), place),
        pl.BlockSpec((1, width, rows), place),
        pl.BlockSpec((1, rows, width), place),
    ]
    out_shape = [tall, tall, wide, wide, wide, tall]
    if shares:
        out_specs.append(pl.BlockSpec((width, 2 * width), fixed, pipeline_mode=once))
        out_shape.append(jax.ShapeDtypeStruct((width, 2 * width), BF16))
    return pl.pallas_call(
        functools.partial(project_kernel, batch, shares),
        grid_spec=pltpu.PrefetchScalarGridSpec(
            num_scalar_prefetch=1,
            grid=(batch,),
            in_specs=[pl.BlockSpec((rows, width), fixed, pipeline_mode=once)] * batch
            + [pl.BlockSpec((1, width), fixed)]
            + [pl.BlockSpec(w.shape, fixed, pipeline_mode=once) for w in weights]
            + [pl.BlockSpec(memory_space=pl.ANY)] * len(before),
            out_specs=out_specs,
        ),
        out_shape=out_shape,
        input_output_aliases={batch + 2 + len(weights) + n: n for n in range(len(before))},
        **params(4 * batch * rows * width * width, 14 * batch * rows * width),
    )(scalars, *pieces, gain, *weights, *before)


def query_kernel(sc, x_ref, gain_ref, *refs):
    shares, (q_ref, x_out, mat) = refs[:-3], refs[-3:]

    @pl.when(pl.program_id(0) == 0)
    def start():
        assemble(sc[5], mat, shares, mat.shape[0] // len(shares), slice(0, mat.shape[1]))

    x_out[0] = x_ref[0]
    normed = rms_norm(x_ref[0].astype(F32), gain_ref[...]).astype(BF16)
    q_ref[0] = dot(normed, mat[...]).astype(BF16)


def queries(scalars, xg, gain, shares):
    count, rows, width = xg.shape
    half = rows // 2
    fixed = lambda n, sc: (0, 0)
    once = pl.Buffered(1)
    part = jax.ShapeDtypeStruct((2, half, width), BF16)
    return pl.pallas_call(
        query_kernel,
        grid_spec=pltpu.PrefetchScalarGridSpec(
            num_scalar_prefetch=1,
            grid=(2,),
            in_specs=[
                pl.BlockSpec((1, half, width), lambda n, sc: (sc[1 + n], n, 0)),
                pl.BlockSpec((1, width), fixed),
            ]
            + [pl.BlockSpec(w.shape, fixed, pipeline_mode=once) for w in shares],
            out_specs=[
                pl.BlockSpec((1, half, width), lambda n, sc: (n, 0, 0)),
                pl.BlockSpec((1, half, width), lambda n, sc: (n, 0, 0)),
                pl.BlockSpec((width, width), fixed, pipeline_mode=once),
            ],
        ),
        out_shape=[part, part, jax.ShapeDtypeStruct((width, width), BF16)],
        **params(2 * rows * width * width, 4 * width * width),
    )(scalars, xg, gain, *shares)


def doc_of(sc, place):
    return (place >= sc[3]).astype(jnp.int32) + (place >= sc[4]).astype(jnp.int32)


def set_bias(bias_s, sc, key_place, query_place):
    rows, twice = bias_s.shape
    half = twice // 2
    key_end, query_end = key_place + rows - 1, query_place + half - 1
    clear = (
        (key_end <= query_place)
        & (doc_of(sc, key_place) == doc_of(sc, query_end))
        & (doc_of(sc, key_end) == doc_of(sc, query_place))
        & (doc_of(sc, key_end) == doc_of(sc, query_end))
    )

    @pl.when(clear)
    def seen():
        bias_s[...] = jnp.zeros(bias_s.shape, F32)

    @pl.when(jnp.logical_not(clear))
    def mixed():
        key_pos = key_place + lax.broadcasted_iota(jnp.int32, (rows, 1), 0)
        lane = lax.broadcasted_iota(jnp.int32, (1, twice), 1)
        query_pos = query_place + jnp.where(lane >= half, lane - half, lane)
        visible = (key_pos <= query_pos) & (doc_of(sc, key_pos) == doc_of(sc, query_pos))
        bias_s[...] = jnp.where(visible, 0.0, NEG)


def fold(target, lead, source, mix_ref, heads, half):
    values = source.astype(F32)
    for g in range(heads):
        piece = (values * mix_ref[g : g + 1, :]).astype(BF16)
        if lead is None:
            target[g * half : (g + 1) * half, :] = piece
        else:
            target[lead, g * half : (g + 1) * half, :] = piece


def attend_kernel(
    count, heads, group, sc, q_ref, k_ref, vt_ref, mix_ref, spread_ref,
    att_ref, t_ref, lse_ref, folded, total, top, norm, bias_s, mixed_s, ahead,
):
    half, width = q_ref.shape[1], q_ref.shape[2]
    rows = k_ref.shape[1]
    step = pl.program_id(0)
    own = sc[0]
    first_half = step <= own
    tile = jnp.where(first_half, step, step - own - 1)
    query_place = jnp.where(first_half, own * rows, (count - 1 - own) * rows + half)

    @pl.when((step == 0) | (step == own + 1))
    def start():
        fold(folded, None, q_ref[0], mix_ref, heads, half)
        top[...] = jnp.full(top.shape, NEG, F32)
        norm[...] = jnp.zeros(norm.shape, F32)
        total[...] = jnp.zeros(total.shape, F32)

    set_bias(bias_s, sc, tile * rows, query_place)
    span = group * half
    chunks = [slice(c * span, (c + 1) * span) for c in range(heads // group)]
    ahead[0] = dot_nt(k_ref[0], folded[chunks[0], :])
    for c, cols in enumerate(chunks):
        if c + 1 < len(chunks):
            ahead[(c + 1) % 2] = dot_nt(k_ref[0], folded[chunks[c + 1], :])
        logits = ahead[c % 2] + jnp.concatenate([bias_s[...]] * (group // 2), axis=1)
        before = top[:, cols]
        after = jnp.maximum(before, jnp.max(logits, axis=0, keepdims=True))
        shrink = jnp.exp2(before - after)
        weights = jnp.exp2(logits - after)
        top[:, cols] = after
        norm[:, cols] = norm[:, cols] * shrink + jnp.sum(weights, axis=0, keepdims=True)
        total[:, cols] = total[:, cols] * shrink + dot(vt_ref[0], weights.astype(BF16))

    @pl.when((step == own) | (step == count))
    def finish():
        lse_ref[0] = top[...] + jnp.log2(norm[...])
        norm[...] = 1.0 / norm[...]
        mix_all(
            total, spread_ref, mixed_s, half,
            lambda h, rows, cols: scale_out(total, norm, t_ref, rows, cols),
        )
        att_ref[0] = (mixed_s[:, :half] + mixed_s[:, half:]).T.astype(BF16)


def scale_out(total, norm, t_ref, rows, cols):
    scaled = total[rows, cols] * norm[:, cols]
    t_ref[0, rows, cols] = scaled.astype(BF16)
    return scaled


def mix_all(total, spread_ref, mixed_s, half, find):
    heads = spread_ref.shape[0]
    size = mixed_s.shape[0] // heads
    for h in range(heads):
        rows = slice(h * size, (h + 1) * size)
        found = jnp.zeros((size, 2 * half), F32)
        for p in range(spread_ref.shape[1] // (2 * half)):
            cols = slice(2 * p * half, (2 * p + 2) * half)
            found += find(h, rows, cols) * spread_ref[h : h + 1, cols]
        mixed_s[rows, :] = found


def attend(scalars, q, k, vt, mix_rows, spread, heads):
    count, rows, width = k.shape
    half = q.shape[1]
    span = heads * half
    which = lambda s, sc: (jnp.where(s <= sc[0], 0, 1), 0, 0)
    tile = lambda s, sc: (sc[HEAD + jnp.where(s <= sc[0], s, s - sc[0] - 1)], 0, 0)
    fixed = lambda s, sc: (0, 0)
    group = math.gcd(heads, 4)
    return pl.pallas_call(
        functools.partial(attend_kernel, count, heads, group),
        grid_spec=pltpu.PrefetchScalarGridSpec(
            num_scalar_prefetch=1,
            grid=(count + 1,),
            in_specs=[
                pl.BlockSpec((1, half, width), which),
                pl.BlockSpec((1, rows, width), tile),
                pl.BlockSpec((1, width, rows), tile),
                pl.BlockSpec((heads, width), fixed),
                pl.BlockSpec((heads, span), fixed),
            ],
            out_specs=[
                pl.BlockSpec((1, half, width), which),
                pl.BlockSpec((1, width, span), which),
                pl.BlockSpec((1, 1, span), which),
            ],
            scratch_shapes=[
                pltpu.VMEM((span, width), BF16),
                pltpu.VMEM((width, span), F32),
                pltpu.VMEM((1, span), F32),
                pltpu.VMEM((1, span), F32),
                pltpu.VMEM((rows, 2 * half), F32),
                pltpu.VMEM((width, 2 * half), F32),
                pltpu.VMEM((2, rows, group * half), F32),
            ],
        ),
        out_shape=[
            jax.ShapeDtypeStruct((2, half, width), BF16),
            jax.ShapeDtypeStruct((2, width, span), BF16),
            jax.ShapeDtypeStruct((2, 1, span), F32),
        ],
        **params(4 * (count + 1) * rows * span * width, 6 * count * rows * width),
    )(scalars, q, k, vt, mix_rows, spread)


def pair_rows(left, right, heads):
    product = left * right
    size = product.shape[0] // heads
    return jnp.concatenate(
        [
            jnp.sum(product[h * size : (h + 1) * size, :], axis=0, keepdims=True)
            for h in range(heads)
        ],
        axis=0,
    )


def lanes_of(found, first, half, lanes=128):
    place = lax.broadcasted_iota(jnp.int32, (found.shape[0], lanes), 1)
    total = jnp.zeros((found.shape[0], lanes), F32)
    for n in range(found.shape[1] // half):
        piece = jnp.sum(found[:, n * half : (n + 1) * half], axis=1, keepdims=True)
        total = jnp.where(place == first + n, piece, total)
    return total


def delta_kernel(heads, grad_ref, t_ref, spread_ref, r_ref, delta_ref):
    half = grad_ref.shape[1]
    grad_t = grad_ref[0].astype(F32).T
    twice = jnp.concatenate([grad_t, grad_t], axis=1)
    sums = jnp.zeros(r_ref.shape, F32)
    for p in range(heads // 2):
        cols = slice(2 * p * half, (2 * p + 2) * half)
        found = pair_rows(twice, t_ref[0, :, cols].astype(F32), heads)
        sums += lanes_of(found, 2 * p, half)
        delta_ref[0, :, cols] = jnp.sum(found * spread_ref[:, cols], axis=0, keepdims=True)

    @pl.when(pl.program_id(0) == 0)
    def first():
        r_ref[...] = sums

    @pl.when(pl.program_id(0) == 1)
    def second():
        r_ref[...] += sums


def deltas(grad_att, t, spread, heads):
    _, half, width = grad_att.shape
    span = heads * half
    return pl.pallas_call(
        functools.partial(delta_kernel, heads),
        grid=(2,),
        in_specs=[
            pl.BlockSpec((1, half, width), lambda s: (s, 0, 0)),
            pl.BlockSpec((1, width, span), lambda s: (s, 0, 0)),
            pl.BlockSpec((heads, span), lambda s: (0, 0)),
        ],
        out_specs=[
            pl.BlockSpec((heads, 128), lambda s: (0, 0)),
            pl.BlockSpec((1, 1, span), lambda s: (s, 0, 0)),
        ],
        out_shape=[
            jax.ShapeDtypeStruct((heads, 128), F32),
            jax.ShapeDtypeStruct((2, 1, span), F32),
        ],
        **params(4 * width * span, 4 * width * span),
    )(grad_att, t, spread)


def back_place(step, own, count):
    low = jnp.minimum(own, count - 1 - own)
    both = step < 2 * (low + 1)
    tile = jnp.where(both, step // 2, step - low - 1)
    part = jnp.where(both, step % 2, jnp.where(own > count - 1 - own, 0, 1))
    return low, both, tile, part


def back_kernel(
    count, heads, base, group, scale, sc, q_ref, ga_ref, k_ref, v_ref, kt_ref, lse_ref, delta_ref,
    mix_ref, weight_ref, spread_ref, dk_ref, dv_ref, dq_ref, r_ref,
    fq, fa, total, dk_s, dv_s, bias_s, mixed_s, twice_s, rows_s, ahead_l, ahead_p,
):
    half, width = q_ref.shape[1], q_ref.shape[2]
    rows = k_ref.shape[1]
    step = pl.program_id(0)
    own = sc[0]
    low, both, tile, part = back_place(step, own, count)
    query_place = jnp.where(part == 0, own * rows, (count - 1 - own) * rows + half)

    @pl.when(step == 0)
    def start():
        for n in range(2):
            q = q_ref[n].astype(F32)
            ga = ga_ref[n].astype(F32)
            for g in range(group):
                cols = slice(g * half, (g + 1) * half)
                fq[n, cols, :] = (q * mix_ref[base + g : base + g + 1, :]).astype(BF16)
                fa[n, cols, :] = (ga * weight_ref[base + g : base + g + 1, :]).astype(BF16)
        total[...] = jnp.zeros(total.shape, F32)

    @pl.when(jnp.logical_not(both) | (part == 0))
    def clear():
        dk_s[...] = jnp.zeros(dk_s.shape, F32)
        dv_s[...] = jnp.zeros(dv_s.shape, F32)

    set_bias(bias_s, sc, tile * rows, query_place)
    chunk = math.gcd(group, 4)
    chunks = [slice(c * chunk * half, (c + 1) * chunk * half) for c in range(group // chunk)]

    def look(c):
        ahead_l[c % 2] = dot_nt(k_ref[0], fq[part, chunks[c], :])
        ahead_p[c % 2] = dot_nt(v_ref[0], fa[part, chunks[c], :])

    look(0)
    for c, cols in enumerate(chunks):
        if c + 1 < len(chunks):
            look(c + 1)
        logits = ahead_l[c % 2] + jnp.concatenate([bias_s[...]] * (chunk // 2), axis=1)
        prob = jnp.exp2(logits - lse_ref[part, :, cols])
        grad_logits = (prob * (ahead_p[c % 2] - delta_ref[part, :, cols])).astype(BF16)
        dv_s[...] += dot(prob.astype(BF16), fa[part, cols, :])
        dk_s[...] += dot(grad_logits, fq[part, cols, :])
        total[part, :, cols] += dot(kt_ref[0], grad_logits)

    @pl.when(jnp.logical_not(both) | (part == 1))
    def leave():
        dk_ref[0] = (dk_s[...] * LN2).astype(BF16)
        dv_ref[0] = dv_s[...].astype(BF16)

    @pl.when(step == count)
    def finish():
        sums = jnp.zeros(r_ref.shape, F32)
        size = width // heads
        for n in range(2):
            q_t = q_ref[n].astype(F32).T
            twice_s[...] = jnp.concatenate([q_t, q_t], axis=1)

            def find(h, rows, cols):
                piece = total[n, rows, cols]
                rows_s[h : h + 1, cols] = jnp.sum(piece * twice_s[rows, :], axis=0, keepdims=True)
                return piece

            mix_all(total, spread_ref, mixed_s, half, find)
            sums += lanes_of(rows_s[...], 0, half)
            dq_ref[n] = ((mixed_s[:, :half] + mixed_s[:, half:]).T * scale).astype(BF16)
        r_ref[...] = sums * scale


def back(
    scalars, base, group, q, grad_att, k, v, kt, lse, delta, mix_rows, weight_rows, spread, heads, scale
):
    count, rows, width = k.shape
    half = q.shape[1]
    span = group * half
    tile = lambda s, sc: (sc[HEAD + back_place(s, sc[0], count)[2]], 0, 0)
    whole = lambda s, sc: (0, 0, 0)
    cut = lambda s, sc: (0, 0, base // group)
    fixed = lambda s, sc: (0, 0)
    once = pl.Buffered(1)
    return pl.pallas_call(
        functools.partial(back_kernel, count, heads, base, group, scale),
        grid_spec=pltpu.PrefetchScalarGridSpec(
            num_scalar_prefetch=1,
            grid=(count + 1,),
            in_specs=[
                pl.BlockSpec((2, half, width), whole, pipeline_mode=once),
                pl.BlockSpec((2, half, width), whole, pipeline_mode=once),
                pl.BlockSpec((1, rows, width), tile),
                pl.BlockSpec((1, rows, width), tile),
                pl.BlockSpec((1, width, rows), tile),
                pl.BlockSpec((2, 1, span), cut, pipeline_mode=once),
                pl.BlockSpec((2, 1, span), cut, pipeline_mode=once),
                pl.BlockSpec((heads, width), fixed),
                pl.BlockSpec((heads, width), fixed),
                pl.BlockSpec((heads, span), fixed),
            ],
            out_specs=[
                pl.BlockSpec((1, rows, width), tile),
                pl.BlockSpec((1, rows, width), tile),
                pl.BlockSpec((2, half, width), whole),
                pl.BlockSpec((heads, 128), fixed),
            ],
            scratch_shapes=[
                pltpu.VMEM((2, span, width), BF16),
                pltpu.VMEM((2, span, width), BF16),
                pltpu.VMEM((2, width, span), F32),
                pltpu.VMEM((rows, width), F32),
                pltpu.VMEM((rows, width), F32),
                pltpu.VMEM((rows, 2 * half), F32),
                pltpu.VMEM((width, 2 * half), F32),
                pltpu.VMEM((width, 2 * half), F32),
                pltpu.VMEM((heads, span), F32),
                pltpu.VMEM((2, rows, math.gcd(group, 4) * half), F32),
                pltpu.VMEM((2, rows, math.gcd(group, 4) * half), F32),
            ],
        ),
        out_shape=[
            jax.ShapeDtypeStruct((count, rows, width), BF16),
            jax.ShapeDtypeStruct((count, rows, width), BF16),
            jax.ShapeDtypeStruct((2, half, width), BF16),
            jax.ShapeDtypeStruct((heads, 128), F32),
        ],
        **params(10 * (count + 1) * rows * span * width, 10 * count * rows * width),
    )(scalars, q, grad_att, k, v, kt, lse, delta, mix_rows, weight_rows, spread)


def put(keep_ref, send_ref, place, rows, value):
    @pl.when(place % 2 == 0)
    def kept():
        keep_ref[place // 2, rows, :] = value

    @pl.when(place % 2 == 1)
    def sent():
        send_ref[place // 2, rows, :] = value


def norm_parts(x):
    inverse = lax.rsqrt(jnp.mean(x * x, axis=-1, keepdims=True) + EPS)
    return inverse, x * inverse


def norm_back(inverse, bare, grad, gain):
    gained = grad * gain
    return inverse * (gained - bare * jnp.mean(gained * bare, axis=-1, keepdims=True))


def ffn_kernel(wt_count, sc, att_ref, x_ref, dy_ref, gain_ref, *refs):
    n = wt_count
    halves = (len(refs) - 16) // n
    wo_shares, win_shares = refs[:n], [refs[(i + 1) * n : (i + 2) * n] for i in range(halves)]
    (
        wout_ref,
        out_ref, gm_ref, gatt_ref, keep_ref, send_ref, gain_out, sq_ref,
        middle_s, low_s, low_t, feed_s, grad_s, wo_ref, win_ref,
    ) = refs[(halves + 1) * n :]
    j = pl.program_id(0)
    last = pl.num_programs(0) - 1
    me = sc[5]
    width = x_ref.shape[1]
    per = width // wt_count
    for i in range(halves):
        for side in range(2):
            pl.when(j == 2 * i + side)(
                functools.partial(
                    assemble, me, win_ref, win_shares[i], per, slice(side * width, (side + 1) * width)
                )
            )

    @pl.when(j == 0)
    def start():
        assemble(me, wo_ref, wo_shares, per, slice(width, 2 * width))
        branch = dot(att_ref[...], wo_ref[...])
        middle = x_ref[...].astype(F32) + branch
        middle_s[...] = middle
        _, bare = norm_parts(middle)
        low = (bare * gain_ref[...]).astype(BF16)
        low_s[...] = low
        low_t[...] = low.T
        feed_s[...] = jnp.zeros(feed_s.shape, F32)
        grad_s[...] = jnp.zeros(grad_s.shape, F32)
        sq_ref[...] = jnp.zeros(sq_ref.shape, F32)
        sq_ref[1:2, :] = jnp.broadcast_to(jnp.sum(branch * branch).reshape(1, 1), (1, 128))

    dy = dy_ref[...]
    hidden = dot(low_s[...], win_ref[...])
    grad_active = dot_nt(dy, wout_ref[...])
    square = hidden * hidden
    inner = jnp.tanh(hidden * (0.7978845608028654 + 0.7978845608028654 * 0.044715 * square))
    half_one = 0.5 + 0.5 * inner
    active = (hidden * half_one).astype(BF16)
    slope = half_one + (0.5 * hidden) * (1.0 - inner * inner) * (
        0.7978845608028654 + 3.0 * 0.7978845608028654 * 0.044715 * square
    )
    grad_hidden = (grad_active * slope).astype(BF16)
    feed_s[...] += dot(active, wout_ref[...])
    grad_s[...] += dot_nt(grad_hidden, win_ref[...])
    grad_out = dot(active.T, dy).astype(BF16)
    grad_in = dot(low_t[...], grad_hidden).astype(BF16)
    put(keep_ref, send_ref, j ^ me, slice(0, width), grad_out)
    for t in range(wt_count):
        rows = pl.ds(pl.multiple_of(width + j * per, per), per)
        put(keep_ref, send_ref, t ^ me, rows, grad_in[t * per : (t + 1) * per, :])

    @pl.when(j == last)
    def finish():
        middle = middle_s[...]
        feed = feed_s[...]
        output = middle + feed
        out_ref[...] = output.astype(BF16)
        sq_ref[0:1, :] = jnp.broadcast_to(jnp.sum(output * output).reshape(1, 1), (1, 128))
        sq_ref[2:3, :] = jnp.broadcast_to(jnp.sum(feed * feed).reshape(1, 1), (1, 128))
        inverse, bare = norm_parts(middle)
        grad = grad_s[...]
        gain_out[...] = jnp.sum(grad * bare, axis=0, keepdims=True)
        grad_middle = dy.astype(F32) + norm_back(inverse, bare, grad, gain_ref[...])
        gm_ref[...] = grad_middle
        low = grad_middle.astype(BF16)
        gatt_ref[...] = dot_nt(low, wo_ref[...]).astype(BF16)
        grad_o = dot(att_ref[...].T, low).astype(BF16)
        for t in range(wt_count):
            put(
                keep_ref, send_ref, t ^ me,
                slice(keep_ref.shape[1] - per, keep_ref.shape[1]),
                grad_o[t * per : (t + 1) * per, :],
            )


def ffn(scalars, wt_count, sq_rows, att, x, dy, gain, wo, wins, wout):
    rows, width = x.shape
    chunks = 2 * len(wins)
    per = width // wt_count
    total = width + per * chunks + per
    fixed = lambda j, sc: (0, 0)
    whole = lambda j, sc: (0, 0, 0)
    once = pl.Buffered(1)
    kernel = functools.partial(ffn_kernel, wt_count)
    shares = [*wo, *(share for win in wins for share in win)]
    return pl.pallas_call(
        kernel,
        grid_spec=pltpu.PrefetchScalarGridSpec(
            num_scalar_prefetch=1,
            grid=(chunks,),
            in_specs=[
                pl.BlockSpec((rows, width), fixed, pipeline_mode=once),
                pl.BlockSpec((rows, width), fixed, pipeline_mode=once),
                pl.BlockSpec((rows, width), fixed, pipeline_mode=once),
                pl.BlockSpec((1, width), fixed),
            ]
            + [pl.BlockSpec(w.shape, fixed, pipeline_mode=once) for w in shares]
            + [pl.BlockSpec((width, width), lambda j, sc: (j, 0))],
            out_specs=[
                pl.BlockSpec((rows, width), fixed),
                pl.BlockSpec((rows, width), fixed),
                pl.BlockSpec((rows, width), fixed),
                pl.BlockSpec((wt_count // 2, total, width), whole),
                pl.BlockSpec((wt_count // 2, total, width), whole),
                pl.BlockSpec((1, width), fixed),
                pl.BlockSpec((sq_rows, 128), fixed),
            ],
            scratch_shapes=[
                pltpu.VMEM((rows, width), F32),
                pltpu.VMEM((rows, width), BF16),
                pltpu.VMEM((width, rows), BF16),
                pltpu.VMEM((rows, width), F32),
                pltpu.VMEM((rows, width), F32),
                pltpu.VMEM((width, width), BF16),
                pltpu.VMEM((width, width), BF16),
            ],
        ),
        out_shape=[
            jax.ShapeDtypeStruct((rows, width), BF16),
            jax.ShapeDtypeStruct((rows, width), F32),
            jax.ShapeDtypeStruct((rows, width), BF16),
            jax.ShapeDtypeStruct((wt_count // 2, total, width), BF16),
            jax.ShapeDtypeStruct((wt_count // 2, total, width), BF16),
            jax.ShapeDtypeStruct((1, width), F32),
            jax.ShapeDtypeStruct((sq_rows, 128), F32),
        ],
        **params(10 * chunks * rows * width * width + 6 * rows * width * width, 24 * width * width),
    )(scalars, att, x, dy, gain, *shares, wout)


TAIL_ROWS = 16


def seen_by(sc, count, device):
    return sc[HEAD + count + device] <= jnp.maximum(sc[0], count - 1 - sc[0])


def weight_kernel(
    count, wt_count, sc, dk_ref, dv_ref, dq_ref, nt_ref, rl_ref, rw_ref, gain_two_ref, sq_ref,
    keep_ref, send_ref, dwq, dwk, dwv,
):
    width, rows = nt_ref.shape[1:]
    half = rows // 2
    device = pl.program_id(0)
    me_wt = sc[5]

    @pl.when(device == 0)
    def start():
        dwq[...] = jnp.zeros(dwq.shape, F32)
        dwk[...] = jnp.zeros(dwk.shape, F32)
        dwv[...] = jnp.zeros(dwv.shape, F32)

    @pl.when(seen_by(sc, count, device))
    def seen():
        dwk[...] += dot(nt_ref[0], dk_ref[0])
        dwv[...] += dot(nt_ref[0], dv_ref[0])

    def queries(n):
        empty = jnp.zeros((half, width), BF16)
        both = [dq_ref[n], empty] if n == 0 else [empty, dq_ref[n]]
        dwq[...] += dot(nt_ref[0], jnp.concatenate(both, axis=0))

    pl.when(device == sc[1])(functools.partial(queries, 0))
    pl.when(device == sc[2])(functools.partial(queries, 1))

    @pl.when(device == count - 1)
    def finish():
        per = width // wt_count

        def pad(value, lanes):
            empty = jnp.zeros((value.shape[0], lanes - value.shape[1]), F32)
            return jnp.concatenate([value, empty], axis=1)

        heads = rw_ref.shape[0]
        each = heads // wt_count
        square = jnp.concatenate([rw_ref[...], jnp.zeros((128 - heads, 128), F32)], axis=0).T
        below = keep_ref.shape[1] - 3 * per - TAIL_ROWS
        assert TAIL_ROWS >= 4 + 2 * each

        def tail(t):
            rows = [
                pad(gain_two_ref[:, t * per : (t + 1) * per], width),
                pad(sq_ref[0:3, :], width),
                pad(rl_ref[t * each : (t + 1) * each, :], width),
                pad(square[t * each : (t + 1) * each, :], width),
                jnp.zeros((TAIL_ROWS - 4 - 2 * each + below, width), F32),
            ]
            return jnp.concatenate(rows, axis=0).astype(BF16)

        for t in range(wt_count):
            cut = slice(t * per, (t + 1) * per)
            for n, total in enumerate((dwq, dwk, dwv)):
                put(keep_ref, send_ref, t ^ me_wt, slice(n * per, (n + 1) * per), total[cut, :].astype(BF16))
            put(keep_ref, send_ref, t ^ me_wt, slice(3 * per, keep_ref.shape[1]), tail(t))


def weight_grads(scalars, wt_count, total, dk, dv, dq, nt, rl, rw, gain_two, sq):
    count, rows, width = dk.shape
    place = lambda j, sc: (j, 0, 0)
    fixed = lambda j, sc: (0, 0)
    whole = lambda j, sc: (0, 0, 0)
    once = pl.Buffered(1)
    share = jax.ShapeDtypeStruct((wt_count // 2, total, width), BF16)
    return pl.pallas_call(
        functools.partial(weight_kernel, count, wt_count),
        grid_spec=pltpu.PrefetchScalarGridSpec(
            num_scalar_prefetch=1,
            grid=(count,),
            in_specs=[
                pl.BlockSpec((1, rows, width), place),
                pl.BlockSpec((1, rows, width), place),
                pl.BlockSpec((2, rows // 2, width), whole, pipeline_mode=once),
                pl.BlockSpec((1, width, rows), place),
                pl.BlockSpec(rl.shape, fixed),
                pl.BlockSpec(rw.shape, fixed),
                pl.BlockSpec((1, width), fixed),
                pl.BlockSpec(sq.shape, fixed),
            ],
            out_specs=[
                pl.BlockSpec((wt_count // 2, total, width), whole),
                pl.BlockSpec((wt_count // 2, total, width), whole),
            ],
            scratch_shapes=[pltpu.VMEM((width, width), F32)] * 3,
        ),
        out_shape=[share, share],
        **params(4 * count * rows * width * width, 10 * count * rows * width),
    )(scalars, dk, dv, dq, nt, rl, rw, gain_two, sq)


def token_kernel(
    count, first, sc, dk_ref, dv_ref, dq_ref, x_ref, wq_ref, mat_ref, gain_ref, gm_ref, part_ref
):
    rows, width = x_ref.shape[1:]
    half = rows // 2
    device = sc[HEAD + 2 * count + first + pl.program_id(0)]
    valid = seen_by(sc, count, device)

    @pl.when(valid)
    def seen():
        grad = dot_nt(dk_ref[0], mat_ref[:, :width]) + dot_nt(dv_ref[0], mat_ref[:, width:])
        inverse, bare = norm_parts(x_ref[0].astype(F32))
        part_ref[0] = norm_back(inverse, bare, grad, gain_ref[...]).astype(BF16)

    @pl.when(jnp.logical_not(valid))
    def unseen():
        part_ref[0] = jnp.zeros(part_ref.shape[1:], BF16)

    def queries(n):
        mine = slice(n * half, (n + 1) * half)
        grad = dot_nt(dq_ref[n], wq_ref[...])
        inverse, bare = norm_parts(x_ref[0, mine, :].astype(F32))
        found = norm_back(inverse, bare, grad, gain_ref[...]) + gm_ref[n]
        part_ref[0, mine, :] = (part_ref[0, mine, :].astype(F32) + found).astype(BF16)

    pl.when(device == sc[1])(functools.partial(queries, 0))
    pl.when(device == sc[2])(functools.partial(queries, 1))


def token_parts(scalars, first, batch, dk, dv, dq, xg, wq, mat, gain, gm):
    count, rows, width = xg.shape
    place = lambda j, sc: (sc[HEAD + 2 * count + first + j], 0, 0)
    fixed = lambda j, sc: (0, 0)
    whole = lambda j, sc: (0, 0, 0)
    once = pl.Buffered(1)
    return pl.pallas_call(
        functools.partial(token_kernel, count, first),
        grid_spec=pltpu.PrefetchScalarGridSpec(
            num_scalar_prefetch=1,
            grid=(batch,),
            in_specs=[
                pl.BlockSpec((1, rows, width), place),
                pl.BlockSpec((1, rows, width), place),
                pl.BlockSpec((2, rows // 2, width), whole, pipeline_mode=once),
                pl.BlockSpec((1, rows, width), place),
                pl.BlockSpec((width, width), fixed, pipeline_mode=once),
                pl.BlockSpec((width, 2 * width), fixed, pipeline_mode=once),
                pl.BlockSpec((1, width), fixed),
                pl.BlockSpec((2, rows // 2, width), whole, pipeline_mode=once),
            ],
            out_specs=pl.BlockSpec((1, rows, width), lambda j, sc: (j, 0, 0)),
        ),
        out_shape=jax.ShapeDtypeStruct((batch, rows, width), BF16),
        **params(4 * batch * rows * width * width, 8 * batch * rows * width),
    )(scalars, dk, dv, dq, xg, wq, mat, gain, gm)


def finish_kernel(entries, heads, sc, *refs):
    count = len(refs) - 12
    pieces, (wq_ref, wk_ref, wv_ref), outs, whole = refs[:count], refs[count : count + 3], refs[-9:-1], refs[-1]
    dq_ref, dk_ref, dv_ref, gain_ref, two_ref, logit_ref, weight_ref, rms_ref = outs
    per = pieces[0].shape[0]
    for n, piece in enumerate(pieces):
        whole[pl.ds(pl.multiple_of(sc[n] * per, 8), per), :] = piece[...].astype(F32)
    rows = wq_ref.shape[0]
    gain = jnp.zeros((rows, 1), F32)
    for n, (out, w) in enumerate(((dq_ref, wq_ref), (dk_ref, wk_ref), (dv_ref, wv_ref))):
        found = whole[n * rows : (n + 1) * rows, :]
        out[...] = found
        gain += jnp.sum(found * w[...].astype(F32), axis=1, keepdims=True)
    gain_ref[...] = gain
    tail = whole[3 * rows : 3 * rows + TAIL_ROWS, :]
    each = logit_ref.shape[0]
    two_ref[...] = tail[0:1, :rows]
    rms_ref[...] = jnp.sqrt(tail[1:4, 0:1] * (1.0 / entries))
    logit_ref[...] = tail[4 : 4 + each, :heads]
    weight_ref[...] = tail[4 + each : 4 + 2 * each, :heads]


def finish_grads(places, pieces, wq, wk, wv, entries, heads, each):
    count = len(pieces)
    rows, width = wq.shape
    ins = [*pieces, wq, wk, wv]
    shapes = [(rows, width)] * 3 + [(rows, 1), (1, rows), (each, heads), (each, heads), (3, 1)]
    fixed = lambda i, sc: (0, 0)
    return pl.pallas_call(
        functools.partial(finish_kernel, entries, heads),
        grid_spec=pltpu.PrefetchScalarGridSpec(
            num_scalar_prefetch=1,
            grid=(1,),
            in_specs=[pl.BlockSpec(v.shape, fixed) for v in ins],
            out_specs=[pl.BlockSpec(v, fixed) for v in shapes],
            scratch_shapes=[pltpu.VMEM((count * pieces[0].shape[0], width), F32)],
        ),
        out_shape=[jax.ShapeDtypeStruct(v, F32) for v in shapes],
        **params(0, 12 * rows * width),
    )(places, *ins)


def unpack_kernel(sum_ref, out_ref, in_ref, o_ref):
    rows, width = out_ref.shape
    per = o_ref.shape[0]
    out_ref[...] = sum_ref[:rows, :].astype(F32)
    chunks = in_ref.shape[1] // width
    for n in range(chunks):
        in_ref[:, n * width : (n + 1) * width] = sum_ref[rows + n * per : rows + (n + 1) * per, :].astype(F32)
    o_ref[...] = sum_ref[rows + chunks * per :, :].astype(F32)


def unpack(total, shapes):
    return pl.pallas_call(
        unpack_kernel,
        out_shape=[jax.ShapeDtypeStruct(shape, F32) for shape in shapes],
        **params(0, 6 * total.size, 0),
    )(total)


def swaps(size, distance):
    return [(i, i ^ distance) for i in range(size)]


def ring_order(count):
    return [2 * p if p < count // 2 else 2 * (count - 1 - p) + 1 for p in range(count)]


def ring(count, step):
    order = ring_order(count)
    return [(order[p], order[(p + step) % count]) for p in range(count)]


def ring_places(count, me, offsets):
    place = jnp.where((me & 1) == 0, me >> 1, count - 1 - (me >> 1))
    p = (place + jnp.array(offsets, jnp.int32)) & (count - 1)
    return jnp.where(p < count // 2, 2 * p, 2 * (count - 1 - p) + 1)


def ring_both(up, down):
    count = lax.axis_size("ctx")
    return lax.ppermute(up, "ctx", ring(count, 1)), lax.ppermute(down, "ctx", ring(count, -1))


def tie(*values):
    return lax.optimization_barrier(values)


def gather_all(value, stages, work):
    count = lax.axis_size("ctx")
    size = lax.axis_size("wt")
    half = value.shape[0] // 2
    rounds = [[(0, value)]]
    up = down = value
    shares, crossed = [], []
    for k in range(1, count // 2 + 1):
        last = k == count // 2
        up, down = ring_both(up[:half], down[half:]) if last else ring_both(up, down)
        tied = []
        if 2 <= k <= len(stages) + 1:
            tied.append(lax.ppermute(stages[k - 2], "wt", swaps(size, 1)))
            tied.append(lax.ppermute(crossed[k - 2], "wt", swaps(size, 1)))
        if k <= len(stages):
            crossed.append(lax.ppermute(stages[k - 1], "wt", swaps(size, 2)))
            if not last:
                tied.append(crossed.pop())
        done = work(rounds, shares) if k >= 3 else []
        up, down, done, *tied = tie(up, down, done, *tied)
        if k >= 3:
            work(rounds, shares, done)
        if k <= len(stages) and not last:
            crossed.append(tied.pop())
        if tied:
            shares.append([stages[k - 2], tied[0], crossed[k - 2], tied[1]])
        rounds.append([(count // 2, jnp.concatenate([up, down], axis=0))] if last else [(-k, up), (k, down)])
    return rounds, shares, crossed


def add(*values):
    return sum(v.astype(F32) for v in values).astype(BF16)


def far_start(far):
    half = far.shape[0] // 2
    up, down = ring_both(far[:half], far[half:])
    return up, down


def far_end(up, down):
    empty = jnp.zeros(up.shape, BF16)
    return jnp.concatenate([up, empty], axis=0), jnp.concatenate([empty, down], axis=0)


class Turning:
    def __init__(self, blocks, me):
        self.count = blocks.shape[0]
        self.blocks, self.me = blocks, me
        self.step, self.last = 0, self.count // 2
        self.pieces = []
        self.done = False

    def at(self, offset):
        place = ring_places(self.count, self.me, [offset])[0]
        return lax.dynamic_index_in_dim(self.blocks, place, 0, keepdims=False)

    def start(self):
        step, last = self.step, self.last
        if step == 0:
            return far_start(self.at(last))
        if step < last:
            return ring_both(
                add(self.up, self.at(last - step)), add(self.down, self.at(step - last))
            )
        if step < 2 * last - 1:
            return ring_both(self.up, self.down)
        half = self.up.shape[0] // 2
        return ring_both(self.up[:half], self.down[half:])

    def finish(self, up, down):
        step, last = self.step, self.last
        if step == 0:
            up, down = far_end(up, down)
        elif step == last - 1:
            up = down = add(up, down, self.at(0))
            self.pieces.append((0, up))
        elif last <= step < 2 * last - 1:
            k = step - last + 1
            self.pieces += [(-k, up), (k, down)]
        elif step == 2 * last - 1:
            self.pieces.append((last, jnp.concatenate([up, down], axis=0)))
            self.done = True
        self.up, self.down = up, down
        self.step += 1

    def ordered(self):
        found = {offset % self.count: piece for offset, piece in self.pieces}
        return [found[n] for n in range(self.count)]


def shards(
    residual_in,
    cotangent,
    block_order,
    doc_starts,
    gain_attn,
    w_query,
    w_key,
    w_value,
    mix_logit,
    mix_weight,
    w_output,
    gain_ffn,
    w_in,
    w_out,
):
    rows, width = residual_in.shape[1:]
    half = rows // 2
    heads = mix_logit.shape[1]
    size = width // heads
    scale = size ** (-0.5)
    count = lax.axis_size("ctx")
    me = lax.axis_index("ctx").astype(jnp.int32)
    wt_count = lax.axis_size("wt")
    starts = doc_starts[0]

    per = gain_attn.shape[0]
    across = lambda v, n: jnp.pad(v, ((0, n - v.shape[0]), (0, 2 * width - v.shape[1])))
    gains = jnp.concatenate([gain_attn, gain_ffn])[None, :]
    mixes_at = 8
    small = jnp.concatenate(
        [across(gains, mixes_at), across(jnp.concatenate([mix_logit, mix_weight], axis=1), mixes_at)], axis=0
    )
    kv_own = jnp.concatenate([jnp.concatenate([w_key, w_value], axis=1), small], axis=0)
    x_own = residual_in[0]
    stages = [kv_own, jnp.concatenate([w_query, w_output], axis=1)]
    stages += [w_in[:, n : n + 2 * width] for n in range(0, w_in.shape[1], 2 * width)]
    order = block_order.astype(jnp.int32)
    devices = jnp.arange(count, dtype=jnp.int32)
    by_block = jnp.sum(jnp.where(order[None, :] == devices[:, None], devices[None, :], 0), axis=1)
    own = order[me]
    partner = by_block[count - 1 - own]
    offsets = [0] + [o for k in range(1, count // 2) for o in (-k, k)] + [count // 2]
    relative = ring_places(count, me, offsets).astype(jnp.int32)
    wt_me = lax.axis_index("wt").astype(jnp.int32)
    scalars = jnp.concatenate(
        [
            jnp.stack([own, me, partner, starts[1], starts[2], wt_me]),
            by_block,
            order,
            relative,
        ]
    ).astype(jnp.int32)

    state = {"first": 0, "found": None, "seen": 0}

    def read_small(shares):
        small = jnp.stack([share[per:, : 2 * per] for share in shares[0]]).astype(F32)
        small = jnp.concatenate(
            [lax.dynamic_slice_in_dim(small, wt_me ^ n, 1, 0) for n in range(wt_count)], axis=0
        )
        gain_one = small[:, 0, :per].reshape(1, width)
        gain_two = small[:, 0, per:].reshape(1, width)
        mixes = small[:, mixes_at : mixes_at + mix_logit.shape[0], : 2 * heads].reshape(heads, 2 * heads)
        logit_mix, weight_mix = mixes[:, :heads], mixes[:, heads:]
        return gain_one, gain_two, logit_mix, weight_mix

    def work(rounds, shares, done=None):
        if done is not None:
            if done:
                *state["found"], state["mat"] = done
            return []
        if not state["seen"]:
            state["small"] = read_small(shares)
            state["mat"] = shares[0]
        batch = [piece for pieces in rounds[state["seen"] : -1] for _, piece in pieces]
        state["seen"] = len(rounds) - 1
        return project_batch(batch)

    def project_batch(batch):
        results = project(
            scalars, count, state["first"], batch, state["small"][0], state["mat"], state["found"]
        )
        state["first"] += len(batch)
        return [*results, state["mat"]][:7]

    rounds, shares, crossed = gather_all(x_own, stages, work)
    gain_one, gain_two, logit_mix, weight_mix = state["small"]
    qo_shares = shares[1]

    mix_by_g = jnp.repeat(logit_mix.T, size, axis=1)
    weight_by_g = jnp.repeat(weight_mix, size, axis=1)
    mix_rows = mix_by_g * (scale * LOG2E)
    spread = jnp.repeat(weight_mix.T, half, axis=1)
    logit_spread = jnp.repeat(logit_mix, half, axis=1)

    batch = [piece for pieces in rounds[state["seen"] :] for _, piece in pieces]
    k, v, kt, vt, nt, xg, kv_mat = project_batch(batch)
    xg, *crossed[len(shares) :] = tie(xg, *crossed[len(shares) :])
    q, x_low, query_mat = queries(scalars, xg, gain_one, qo_shares)
    x_low = x_low.reshape(rows, width)
    for n in range(len(shares), len(stages)):
        near = lax.ppermute(stages[n], "wt", swaps(wt_count, 1))
        both = lax.ppermute(crossed[n], "wt", swaps(wt_count, 1))
        q, near, both = lax.optimization_barrier((q, near, both))
        shares.append([stages[n], near, crossed[n], both])
    w_out_after, _ = lax.optimization_barrier((w_out, rounds[-1][0][1]))
    outer_mat = lax.all_gather(w_out_after, "wt", axis=0, tiled=True)

    def exchange(second):
        every = lax.all_gather(second, "ctx", axis=0)
        return lax.dynamic_index_in_dim(every, partner, 0, keepdims=False)

    dy_second, _ = lax.optimization_barrier((cotangent[0, half:], rounds[-1][0][1]))
    dy_low = jnp.concatenate([cotangent[0, :half], exchange(dy_second)], axis=0)

    attended, t, lse = attend(scalars, q, k, vt, mix_rows, spread, heads)
    out_low, grad_middle, grad_att, keep, send, grad_gain_two, squares = ffn(
        scalars, wt_count, heads, attended.reshape(rows, width), x_low, dy_low, gain_two,
        qo_shares, shares[2:], outer_mat,
    )
    output_own = jnp.concatenate([out_low[:half], exchange(out_low[half:])], axis=0)
    grad_att = grad_att.reshape(2, half, width)
    grad_middle = grad_middle.reshape(2, half, width)

    got = lax.ppermute(send, "wt", swaps(wt_count, 1))
    r_weight, delta = deltas(grad_att, t, spread, heads)
    summed = add(keep, got).reshape(2, count, -1, width).transpose(1, 0, 2, 3).reshape(-1, width)
    summed, delta = tie(summed, delta)
    summed = lax.psum_scatter(summed, "ctx", scatter_dimension=0, tiled=True)

    dk, dv, dq, r_logit = back(
        scalars, 0, heads, q, grad_att, k, v, kt, lse, delta, mix_rows, weight_by_g,
        logit_spread, heads, scale,
    )

    def parts(first, batch, dk):
        return token_parts(
            scalars, first, batch, dk, dv, dq, xg, query_mat, kv_mat, gain_one, grad_middle
        )

    last = count // 2
    far = parts(count - 1, 1, dk)
    dk, far = tie(dk, far)
    up, down = far_start(far[0])
    total = -(-(3 * per + TAIL_ROWS) // (8 * count)) * 8 * count
    keep, send = weight_grads(
        scalars, wt_count, total, dk, dv, dq, nt, r_logit, r_weight, grad_gain_two, squares
    )
    up, down, keep, send, summed, dk = tie(up, down, keep, send, summed, dk)
    up, down = far_end(up, down)
    summed = summed.reshape(2, -1, width)
    near = lax.ppermute(send, "wt", swaps(wt_count, 1))
    ffn_far = lax.ppermute(summed[1], "wt", swaps(wt_count, 2))
    pair = parts(2 * (last - 1) - 1, 2, dk)
    near, ffn_far, pair = tie(near, ffn_far, pair)
    over = lax.ppermute(add(keep[1], near[1]), "wt", swaps(wt_count, 2))
    share = add(summed[0], ffn_far)

    turn = None
    for k in range(last - 1, 0, -1):
        up, down = ring_both(add(up, pair[1]), add(down, pair[0]))
        beside = [over, share] if turn is None else list(turn.start())
        after = parts(2 * (k - 1) - 1, 2, dk) if k > 1 else parts(0, 1, dk)
        up, down, pair, *beside = tie(up, down, after, *beside)
        if turn is None:
            over, share = beside
            ffn_sum = lax.all_gather(share, "ctx", axis=0, tiled=True)
            turn = Turning(add(keep[0], near[0], over).reshape(count, -1, width), me)
        else:
            turn.finish(*beside)
    input_grad = add(up, down, pair[0])
    while not turn.done:
        turn.finish(*tie(*turn.start()))

    places = ring_places(count, me, list(range(count))).astype(jnp.int32)
    entries = float(rows * width) * (count * wt_count)
    grad_q, grad_k, grad_v, gain_sum, gain_two_grad, logit_grad, weight_grad, rms = finish_grads(
        places, turn.ordered(), w_query, w_key, w_value, entries, heads, heads // wt_count
    )
    grad_out, grad_in, grad_o = unpack(ffn_sum, (w_out.shape, w_in.shape, w_output.shape))
    return (
        output_own[None],
        input_grad[None],
        rms.reshape(3),
        gain_sum.reshape(per) / gain_attn.astype(F32),
        grad_q,
        grad_k,
        grad_v,
        logit_grad,
        weight_grad,
        grad_o,
        gain_two_grad.reshape(per),
        grad_in,
        grad_out,
    )


def solution(mesh):
    tokens = P("wt", "ctx", None)
    matrix = P("wt", None)
    vector = P("wt")
    return jax.shard_map(
        shards,
        mesh=mesh,
        in_specs=(tokens, tokens, P(), matrix, vector)
        + (matrix,) * 6
        + (vector, matrix, matrix),
        out_specs=(tokens, tokens, P(), vector) + (matrix,) * 6 + (vector, matrix, matrix),
        check_vma=False,
    )
```

time: 747 us -> 501 us (0.67)
  waiting for transfers between devices: 314 us -> 128 us
  blocking collectives: 75.5 us -> 0 us
  Pallas kernels: 197 us -> 250 us
  matrix products: 50.3 us -> 0 us
  starting transfers between devices: 25.2 us -> 45.4 us
  local copies, waits for them, and re-layouts: 35 us -> 22.8 us
    reduce_scatter x4 -> x1, waiting for transfers between devices: 118 us -> 0.02 us  [shards(): summed = lax.psum_scatter(summed, 'ctx', scatter_dimension=0, tiled=True)]
    psum x1 -> x0, waiting for transfers between devices: 99.7 us -> none  [reduce(): return lax.psum(share, 'ctx')]
    pallas_call x3 -> x14, Pallas kernels: 133 us -> 200 us  [the longest x1 82.6 us: back(): pl.pallas_call(functools.partial(back_kernel, count, heads, base, group,...]
    psum x1 -> x0, blocking collectives: 51.3 us -> none  [shards(): shared = lax.psum(shared, ('ctx', 'wt'))]
    dot_general x12 -> x0, matrix products: 50.3 us -> none  [the longest x4 19.5 us: dot(): return jnp.dot(left, right, preferred_element_type=F32)]
    all_gather x1 -> x0, blocking collectives: 24.2 us -> none  [shards(): small = lax.all_gather(small, 'wt', axis=0, tiled=True).astype(F32)]
    ppermute x17 -> x48, starting transfers between devices: 24.8 us -> 45 us  [the longest x16 22 us: ring_both(): lax.ppermute(up, 'ctx', ring(count, 1))]
    all_gather x3 -> x2, waiting for transfers between devices: 0.02 us -> 17.1 us  [the longest x1 17.1 us: shards(): outer_mat = lax.all_gather(w_out_after, 'wt', axis=0, tiled=True)]
  transfers between devices with their start and end apart: 27 -> 53, of which waited for: 10 -> 29; matrix products, arithmetic and copies ran while one was open for 11% -> 9% of each run, Pallas kernels for 26% -> 44%
where the time goes in v2:
time: 501 us; the launch traced here: 494 us
  Pallas kernels  250 us (50%)
  waiting for transfers between devices  128 us (26%)
  starting transfers between devices  45.4 us (9%)
  other arithmetic  29.2 us (6%)
  local copies, waits for them, and re-layouts  22.8 us (5%)
  between operations  18 us (4%)
    pallas_call x1, Pallas kernels, back(): pl.pallas_call(functools.partial(back_kernel, count, heads, base, group,...  82.6 us
    ppermute x16, waiting for transfers between devices, ring_both(): lax.ppermute(up, 'ctx', ring(count, 1))  58.3 us
    pallas_call x1, Pallas kernels, attend(): pl.pallas_call(functools.partial(attend_kernel, count, heads, group), gri...  45 us
    pallas_call x5, Pallas kernels, token_parts(): pl.pallas_call(functools.partial(token_kernel, count, first), grid_spec=p...  33.5 us
    ppermute x16, waiting for transfers between devices, ring_both(): lax.ppermute(down, 'ctx', ring(count, -1))  29.5 us
    pallas_call x1, Pallas kernels, ffn(): pl.pallas_call(kernel, grid_spec=pltpu.PrefetchScalarGridSpec(num_scalar_...  28.3 us
    pallas_call x3, Pallas kernels, project(): pl.pallas_call(functools.partial(project_kernel, batch, shares), grid_spe...  26.4 us
    ppermute x16, starting transfers between devices, ring_both(): lax.ppermute(up, 'ctx', ring(count, 1))  22 us
  transfers between devices with their start and end apart: 53, of which 29 were waited for; matrix products, arithmetic and copies ran while one was open for 9% of the time, Pallas kernels for 44%

profile of v2, /device:TPU:0, one launch (start us, length us, event | category | flops | bytes accessed | tf_op | source)
XLA Modules:
  0.0 493.6 jit_solution(18414472824245528096)
XLA Ops:
  25.5 5.0 %collective-permute-done.2.refs_6_ = bf16[208,1536]{1,0:T(8,128)(2,1)} collective-permute-done((bf16[208,1536]{1,0:T(8,128)(2,1)S(1)}, bf16[208,1536]{1,0:T(8,128)(2,1)}, u32[]{:S(2)}, u32[]{:S(2)}) %collective-permute-start.2) | collective-permute-done | bytes 639008 | tf_op jit(solution)/shard_map/ppermute | solution.py:924
  34.4 7.2 %collective-permute-done.7.refs_2_ = bf16[192,1536]{1,0:T(8,128)(2,1)S(1)} collective-permute-done((bf16[192,1536]{1,0:T(8,128)(2,1)S(1)}, bf16[192,1536]{1,0:T(8,128)(2,1)S(1)}, u32[]{:S(2)}, u32[]{:S(2)}) %collective-permute-start.7) | collective-permute-done | bytes 589856 | tf_op jit(solution)/shard_map/ppermute | solution.py:924
  51.9 10.0 %shard_map.327 = (bf16[8,384,768]{2,1,0:T(8,128)(2,1)}, bf16[8,384,768]{2,1,0:T(8,128)(2,1)}, bf16[8,768,384]{2,1,0:T(8,128)(2,1)}, bf16[8,768,384]{2,1,0:T(8,12...) custom-call(s32[30]{0:T(128)} %concatenate.49.sc, ...), custom_call_target="tpu_custom_call" | custom-call | flops 2717908992 | bytes 12386304 | tf_op jit(solution)/shard_map/pallas_call | solution.py:106
  69.5 7.3 %shard_map.328 = (bf16[8,384,768]{2,1,0:T(8,128)(2,1)}, bf16[8,384,768]{2,1,0:T(8,128)(2,1)}, bf16[8,768,384]{2,1,0:T(8,128)(2,1)}, bf16[8,768,384]{2,1,0:T(8,12...) custom-call(s32[30]{0:T(128)} %concatenate.49.sc, ...), custom_call_target="tpu_custom_call", output_to_operand_aliasing={{0}: (5, {}), {1}: (6, {}), {2}: (7, {}), {3}: (8, {}), {4}... | custom-call | flops 1811939328 | bytes 8257536 | tf_op jit(solution)/shard_map/pallas_call | solution.py:106
  79.6 9.2 %shard_map.329 = (bf16[8,384,768]{2,1,0:T(8,128)(2,1)}, bf16[8,384,768]{2,1,0:T(8,128)(2,1)}, bf16[8,768,384]{2,1,0:T(8,128)(2,1)}, bf16[8,768,384]{2,1,0:T(8,12...) custom-call(s32[30]{0:T(128)} %concatenate.49.sc, ...), custom_call_target="tpu_custom_call", output_to_operand_aliasing={{0}: (6, {}), {1}: (7, {}), {2}: (8, {}), {3}: (9, {}), {4}... | custom-call | flops 2717908992 | bytes 12386304 | tf_op jit(solution)/shard_map/pallas_call | solution.py:106
  88.7 4.5 collective-permute-done.17.refs_10_
  102.1 45.0 %shard_map.331 = (bf16[2,192,768]{2,1,0:T(8,128)(2,1)}, bf16[2,768,2304]{2,1,0:T(8,128)(2,1)}, f32[2,1,2304]{2,1,0:T(1,128)}) custom-call(s32[30]{0:T(128)} %concatenate.49.sc, bf16[2,192,768]{2,1,0:T(8,128)(2,1)} %get-tuple-element.188.q_ref, bf16[8,384,768]{2,1,0:T(8,128)(2,1)} %get-tuple-element.189.k_ref, ...), custom_call_target="tpu_custom_call" | custom-call | flops 24461180928 | bytes 14155776 | tf_op jit(solution)/shard_map/pallas_call | solution.py:272
  149.0 17.1 %all-gather.7.cloned.1.call-done.refs_12_ = bf16[3072,768]{1,0:T(8,128)(2,1)} async-done(((bf16[768,768]{1,0:T(8,128)(2,1)}), bf16[3072,768]{1,0:T(8,128)(2,1)}) %all-gather.7.cloned.1.call-update) | async-done | bytes 4718608 | tf_op jit(solution)/shard_map/all_gather | solution.py:1107
  166.1 28.3 %shard_map.332 = (bf16[384,768]{1,0:T(8,128)(2,1)}, f32[384,768]{1,0:T(8,128)}, bf16[384,768]{1,0:T(8,128)(2,1)}, bf16[2,1728,768]{2,1,0:T(8,128)(2,1)}, bf16[2,...) custom-call(s32[30]{0:T(128)} %concatenate.49.sc, bf16[384,768]{1,0:T(8,128)(2,1)} %bitcast.121, ...), custom_call_target="tpu_custom_call" | custom-call | flops 10418651136 | bytes 14155776 | tf_op jit(solution)/shard_map/pallas_call | solution.py:620
  194.7 5.2 %shard_map.333 = (f32[12,128]{1,0:T(8,128)}, f32[2,1,2304]{2,1,0:T(1,128)}) custom-call(bf16[2,192,768]{2,1,0:T(8,128)(2,1)} %bitcast.112, bf16[2,768,2304]{2,1,0:T(8,128)(2,1)} %get-tuple-element.206.t_ref, f32[12,2304]{1,0:T(8,128)} %reshape.123.spread_ref), custom_call_target="tpu_custom_call" | custom-call | flops 7077888 | bytes 7077888 | tf_op jit(solution)/shard_map/pallas_call | solution.py:352
  203.5 5.3 %add_convert_fusion = bf16[2,1728,768]{2,1,0:T(8,128)(2,1)S(1)} fusion(bf16[2,1728,768]{2,1,0:T(8,128)(2,1)} %collective-permute-done.20, bf16[2,1728,768]{2,1,0:T(8,128)(2,1)} %get-tuple-element.204), kind=kLoop, calls=%fused_computation | loop fusion | flops 10616832 | bytes 15925248 | tf_op jit(solution)/shard_map/convert_element_type | solution.py:940
  214.1 82.6 %shard_map.334 = (bf16[8,384,768]{2,1,0:T(8,128)(2,1)}, bf16[8,384,768]{2,1,0:T(8,128)(2,1)}, bf16[2,192,768]{2,1,0:T(8,128)(2,1)}, f32[12,128]{1,0:T(8,128)}) custom-call(s32[30]{0:T(128)} %concatenate.49.sc, bf16[2,192,768]{2,1,0:T(8,128)(2,1)} %get-tuple-element.188.q_ref, bf16[2,192,768]{2,1,0:T(8,128)(2,1)} %bitcast.113, ...), custom_call_target="tpu_custom_call" | custom-call | flops 61152952320 | bytes 23592960 | tf_op jit(solution)/shard_map/pallas_call | solution.py:462
  296.8 4.6 shard_map.335
  305.8 17.1 %shard_map.336 = (bf16[2,640,768]{2,1,0:T(8,128)(2,1)}, bf16[2,640,768]{2,1,0:T(8,128)(2,1)}) custom-call(s32[30]{0:T(128)} %concatenate.49.sc, bf16[8,384,768]{2,1,0:T(8,128)(2,1)} %get-tuple-element.227.dk_ref, bf16[8,384,768]{2,1,0:T(8,128)(2,1)} %get-tuple-element.210.dv_ref, bf16[2,192,768]{2,1,0:T(8,128)(2,1)} %get-tuple-element.211.dq_ref, ...), custom_call_target="tpu_custom_call" | custom-call | flops 7247757312 | bytes 23592960 | tf_op jit(solution)/shard_map/pallas_call | solution.py:738
  325.2 7.4 %shard_map.337 = bf16[2,384,768]{2,1,0:T(8,128)(2,1)} custom-call(s32[30]{0:T(128)} %concatenate.49.sc, bf16[8,384,768]{2,1,0:T(8,128)(2,1)} %get-tuple-element.227.dk_ref, bf16[8,384,768]{2,1,0:T(8,128)(2,1)} %get-tuple-element.210.dv_ref, bf16[2,192,768]{2,1,0:T(8,128)(2,1)} %get-tuple-element.211.dq_ref, bf16[8,384,768]{2,1,0:T(8,128)(2,1)} %get-tuple-element.183.x_ref, ...), custom_call_target="tpu_custom_call" | custom-call | flops 1811939328 | bytes 4718592 | tf_op jit(solution)/shard_map/pallas_call | solution.py:799
  342.1 8.5 %shard_map.338 = bf16[2,384,768]{2,1,0:T(8,128)(2,1)} custom-call(s32[30]{0:T(128)} %concatenate.49.sc, bf16[8,384,768]{2,1,0:T(8,128)(2,1)} %get-tuple-element.227.dk_ref, bf16[8,384,768]{2,1,0:T(8,128)(2,1)} %get-tuple-element.210.dv_ref, bf16[2,192,768]{2,1,0:T(8,128)(2,1)} %get-tuple-element.211.dq_ref, bf16[8,384,768]{2,1,0:T(8,128)(2,1)} %get-tuple-element.183.x_ref, ...), custom_call_target="tpu_custom_call" | custom-call | flops 1811939328 | bytes 4718592 | tf_op jit(solution)/shard_map/pallas_call | solution.py:799
  352.5 6.6 %collective-permute-done.25 = bf16[384,768]{1,0:T(8,128)(2,1)} collective-permute-done((bf16[384,768]{1,0:T(8,128)(2,1)}, bf16[384,768]{1,0:T(8,128)(2,1)}, u32[]{:S(2)}, u32[]{:S(2)}) %collective-permute-start.25) | collective-permute-done | bytes 589856 | tf_op jit(solution)/shard_map/ppermute | solution.py:902
  359.1 5.5 %collective-permute-done.26 = bf16[384,768]{1,0:T(8,128)(2,1)} collective-permute-done((bf16[384,768]{1,0:T(8,128)(2,1)}, bf16[384,768]{1,0:T(8,128)(2,1)}, u32[]{:S(2)}, u32[]{:S(2)}) %collective-permute-start.26) | collective-permute-done | bytes 589856 | tf_op jit(solution)/shard_map/ppermute | solution.py:902
  373.2 6.3 %shard_map.339 = bf16[2,384,768]{2,1,0:T(8,128)(2,1)} custom-call(s32[30]{0:T(128)} %concatenate.49.sc, bf16[8,384,768]{2,1,0:T(8,128)(2,1)} %get-tuple-element.227.dk_ref, bf16[8,384,768]{2,1,0:T(8,128)(2,1)} %get-tuple-element.210.dv_ref, bf16[2,192,768]{2,1,0:T(8,128)(2,1)} %get-tuple-element.211.dq_ref, bf16[8,384,768]{2,1,0:T(8,128)(2,1)} %get-tuple-element.183.x_ref, ...), custom_call_target="tpu_custom_call" | custom-call | flops 1811939328 | bytes 4718592 | tf_op jit(solution)/shard_map/pallas_call | solution.py:799
  379.6 9.9 %collective-permute-done.30 = bf16[40,768]{1,0:T(8,128)(2,1)S(1)} collective-permute-done((bf16[40,768]{1,0:T(8,128)(2,1)S(1)}, bf16[40,768]{1,0:T(8,128)(2,1)S(1)}, u32[]{:S(2)}, u32[]{:S(2)}) %collective-permute-start.30) | collective-permute-done | bytes 61472 | tf_op jit(solution)/shard_map/ppermute | solution.py:902
  398.2 6.6 %shard_map.340 = bf16[1,384,768]{2,1,0:T(8,128)(2,1)} custom-call(s32[30]{0:T(128)} %concatenate.49.sc, bf16[8,384,768]{2,1,0:T(8,128)(2,1)} %get-tuple-element.227.dk_ref, bf16[8,384,768]{2,1,0:T(8,128)(2,1)} %get-tuple-element.210.dv_ref, bf16[2,192,768]{2,1,0:T(8,128)(2,1)} %get-tuple-element.211.dq_ref, bf16[8,384,768]{2,1,0:T(8,128)(2,1)} %get-tuple-element.183.x_ref, ...), custom_call_target="tpu_custom_call" | custom-call | flops 905969664 | bytes 2359296 | tf_op jit(solution)/shard_map/pallas_call | solution.py:799
  404.8 16.1 %collective-permute-done.34 = bf16[80,768]{1,0:T(8,128)(2,1)S(1)} collective-permute-done((bf16[80,768]{1,0:T(8,128)(2,1)S(1)}, bf16[80,768]{1,0:T(8,128)(2,1)S(1)}, u32[]{:S(2)}, u32[]{:S(2)}) %collective-permute-start.34) | collective-permute-done | bytes 122912 | tf_op jit(solution)/shard_map/ppermute | solution.py:902
  426.2 4.9 collective-permute-done.36
  437.5 6.5 %collective-permute-done.38 = bf16[80,768]{1,0:T(8,128)(2,1)S(1)} collective-permute-done((bf16[80,768]{1,0:T(8,128)(2,1)S(1)}, bf16[80,768]{1,0:T(8,128)(2,1)S(1)}, u32[]{:S(2)}, u32[]{:S(2)}) %collective-permute-start.38) | collective-permute-done | bytes 122912 | tf_op jit(solution)/shard_map/ppermute | solution.py:902
  (229 shorter events, 148.5 us)
Async XLA Ops:
  7.2 139.9 %all-gather.11.cloned.1.call-start = ((), (), s32[]{:S(2)}) async-start(), calls=%async_computation.4 | async-start | bytes 2654208 | tf_op jit(solution)/shard_map/all_gather | solution.py:1110
  15.0 26.6 %collective-permute-start.5 = (bf16[208,1536]{1,0:T(8,128)(2,1)S(1)}, bf16[208,1536]{1,0:T(8,128)(2,1)}, u32[]{:S(2)}, u32[]{:S(2)}) collective-permute-start(bf16[208,1536]{1,0:T(8,128)(2,1)S(1)} %pad_maximum_fusion.refs_4_), channel_id=1, source_target_pairs={{0,1},{1,0},{2,3},{3,2},{4,5},{5,4},{6,7},{7,6},{8,9},{9,8},{10,11... | collective-permute-start | bytes 1916936 | tf_op jit(solution)/shard_map/ppermute | solution.py:921
  16.0 25.5 %collective-permute-start.7 = (bf16[192,1536]{1,0:T(8,128)(2,1)S(1)}, bf16[192,1536]{1,0:T(8,128)(2,1)S(1)}, u32[]{:S(2)}, u32[]{:S(2)}) collective-permute-start(bf16[192,1536]{1,0:T(8,128)(2,1)S(1)} %constant_dynamic-update-slice_fusion.refs_0_), channel_id=1, source_target_pairs={{0,2},{1,3},{2,0},{3,1},{4,6},{5,7},{6,4},{7,5},{8,10},{9,11},{10,... | collective-permute-start | bytes 1769480 | tf_op jit(solution)/shard_map/ppermute | solution.py:924
  30.5 17.8 %collective-permute-start.6 = (bf16[208,1536]{1,0:T(8,128)(2,1)}, bf16[208,1536]{1,0:T(8,128)(2,1)S(1)}, u32[]{:S(2)}, u32[]{:S(2)}) collective-permute-start(bf16[208,1536]{1,0:T(8,128)(2,1)} %collective-permute-done.2.refs_6_), channel_id=1, source_target_pairs={{0,1},{1,0},{2,3},{3,2},{4,5},{5,4},{6,7},{7,6},{8,9},{9,8},{10,11... | collective-permute-start | bytes 1916936 | tf_op jit(solution)/shard_map/ppermute | solution.py:922
  41.6 20.5 %collective-permute-start.10 = (bf16[192,1536]{1,0:T(8,128)(2,1)S(1)}, bf16[192,1536]{1,0:T(8,128)(2,1)}, u32[]{:S(2)}, u32[]{:S(2)}) collective-permute-start(bf16[192,1536]{1,0:T(8,128)(2,1)S(1)} %constant_dynamic-update-slice_fusion.refs_0_), channel_id=1, source_target_pairs={{0,1},{1,0},{2,3},{3,2},{4,5},{5,4},{6,7},{7,6},{8,9},{9,8},{10,11... | collective-permute-start | bytes 1769480 | tf_op jit(solution)/shard_map/ppermute | solution.py:921
  41.6 20.4 %collective-permute-start.12 = (bf16[192,1536]{1,0:T(8,128)(2,1)}, bf16[192,1536]{1,0:T(8,128)(2,1)}, u32[]{:S(2)}, u32[]{:S(2)}) collective-permute-start(bf16[192,1536]{1,0:T(8,128)(2,1)} %get-tuple-element.280.refs_4_), channel_id=1, source_target_pairs={{0,2},{1,3},{2,0},{3,1},{4,6},{5,7},{6,4},{7,5},{8,10},{9,11},{10,... | collective-permute-start | bytes 1769480 | tf_op jit(solution)/shard_map/ppermute | solution.py:924
  77.0 89.1 %all-gather.7.cloned.1.call-start = ((), (), s32[]{:S(2)}) async-start(), calls=%async_computation.1 | async-start | bytes 5898240 | tf_op jit(solution)/shard_map/all_gather | solution.py:1107
  77.7 245.2 %reduce-scatter.2.cloned.1.call-start = ((), (), s32[]{:S(2)}) async-start(), calls=%async_computation.2 | async-start | bytes 5971968 | tf_op jit(solution)/shard_map/reduce_scatter | solution.py:1129
  79.6 22.5 %collective-permute-start.18 = (bf16[192,1536]{1,0:T(8,128)(2,1)S(1)}, bf16[192,1536]{1,0:T(8,128)(2,1)}, u32[]{:S(2)}, u32[]{:S(2)}) collective-permute-start(bf16[192,1536]{1,0:T(8,128)(2,1)S(1)} %copy-done.12), channel_id=1, source_target_pairs={{0,1},{1,0},{2,3},{3,2},{4,5},{5,4},{6,7},{7,6},{8,9},{9,8},{10,11... | collective-permute-start | bytes 1769480 | tf_op jit(solution)/shard_map/ppermute | solution.py:1102
  211.6 248.0 %all-gather.13.cloned.1.call-start = ((), (), s32[]{:S(2)}) async-start(), calls=%async_computation.5 | async-start | bytes 2654208 | tf_op jit(solution)/shard_map/all_gather | solution.py:1110
  214.1 268.3 %all-gather.9.cloned.1.call-start = ((), (), s32[]{:S(2)}) async-start(), calls=%async_computation.3 | async-start | bytes 2985984 | tf_op jit(solution)/shard_map/all_gather | solution.py:1167
  302.5 20.4 %collective-permute-start.21 = (bf16[192,768]{1,0:T(8,128)(2,1)S(1)}, bf16[192,768]{1,0:T(8,128)(2,1)S(1)}, u32[]{:S(2)}, u32[]{:S(2)}) collective-permute-start(bf16[192,768]{1,0:T(8,128)(2,1)S(1)} %get-tuple-element.290), channel_id=1, source_target_pairs={{0,8},{8,16},{16,24},{24,28},{28,20},{20,12},{12,4},{4,0},{1,9},{9... | collective-permute-start | bytes 884744 | tf_op jit(solution)/shard_map/ppermute | solution.py:902
  305.0 17.9 %collective-permute-start.22 = (bf16[192,768]{1,0:T(8,128)(2,1)S(1)}, bf16[192,768]{1,0:T(8,128)(2,1)S(1)}, u32[]{:S(2)}, u32[]{:S(2)}) collective-permute-start(bf16[192,768]{1,0:T(8,128)(2,1)S(1)} %get-tuple-element.289), channel_id=1, source_target_pairs={{0,4},{8,0},{16,8},{24,16},{28,24},{20,28},{12,20},{4,12},{1,5},{9... | collective-permute-start | bytes 884744 | tf_op jit(solution)/shard_map/ppermute | solution.py:902
  336.9 27.8 %collective-permute-start.27 = (bf16[640,768]{1,0:T(8,128)(2,1)}, bf16[640,768]{1,0:T(8,128)(2,1)}, u32[]{:S(2)}, u32[]{:S(2)}) collective-permute-start(bf16[640,768]{1,0:T(8,128)(2,1)} %fusion.8), channel_id=1, source_target_pairs={{0,2},{1,3},{2,0},{3,1},{4,6},{5,7},{6,4},{7,5},{8,10},{9,11},{10,... | collective-permute-start | bytes 2949128 | tf_op jit(solution)/shard_map/ppermute | solution.py:1156
  338.6 20.5 %collective-permute-start.25 = (bf16[384,768]{1,0:T(8,128)(2,1)}, bf16[384,768]{1,0:T(8,128)(2,1)}, u32[]{:S(2)}, u32[]{:S(2)}) collective-permute-start(bf16[384,768]{1,0:T(8,128)(2,1)} %get-tuple-element.278), channel_id=1, source_target_pairs={{0,8},{8,16},{16,24},{24,28},{28,20},{20,12},{12,4},{4,0},{1,9},{9... | collective-permute-start | bytes 1769480 | tf_op jit(solution)/shard_map/ppermute | solution.py:902
  340.2 24.4 %collective-permute-start.26 = (bf16[384,768]{1,0:T(8,128)(2,1)}, bf16[384,768]{1,0:T(8,128)(2,1)}, u32[]{:S(2)}, u32[]{:S(2)}) collective-permute-start(bf16[384,768]{1,0:T(8,128)(2,1)} %get-tuple-element.277), channel_id=1, source_target_pairs={{0,4},{8,0},{16,8},{24,16},{28,24},{20,28},{12,20},{4,12},{1,5},{9... | collective-permute-start | bytes 1769480 | tf_op jit(solution)/shard_map/ppermute | solution.py:902
  367.2 24.9 %collective-permute-start.28 = (bf16[384,768]{1,0:T(8,128)(2,1)}, bf16[384,768]{1,0:T(8,128)(2,1)}, u32[]{:S(2)}, u32[]{:S(2)}) collective-permute-start(bf16[384,768]{1,0:T(8,128)(2,1)} %get-tuple-element.276), channel_id=1, source_target_pairs={{0,8},{8,16},{16,24},{24,28},{28,20},{20,12},{12,4},{4,0},{1,9},{9... | collective-permute-start | bytes 1769480 | tf_op jit(solution)/shard_map/ppermute | solution.py:902
  367.9 24.2 %collective-permute-start.29 = (bf16[384,768]{1,0:T(8,128)(2,1)}, bf16[384,768]{1,0:T(8,128)(2,1)}, u32[]{:S(2)}, u32[]{:S(2)}) collective-permute-start(bf16[384,768]{1,0:T(8,128)(2,1)} %get-tuple-element.275), channel_id=1, source_target_pairs={{0,4},{8,0},{16,8},{24,16},{28,24},{20,28},{12,20},{4,12},{1,5},{9... | collective-permute-start | bytes 1769480 | tf_op jit(solution)/shard_map/ppermute | solution.py:902
  371.1 18.4 %collective-permute-start.30 = (bf16[40,768]{1,0:T(8,128)(2,1)S(1)}, bf16[40,768]{1,0:T(8,128)(2,1)S(1)}, u32[]{:S(2)}, u32[]{:S(2)}) collective-permute-start(bf16[40,768]{1,0:T(8,128)(2,1)S(1)} %get-tuple-element.288), channel_id=1, source_target_pairs={{0,8},{8,16},{16,24},{24,28},{28,20},{20,12},{12,4},{4,0},{1,9},{9... | collective-permute-start | bytes 184328 | tf_op jit(solution)/shard_map/ppermute | solution.py:902
  371.9 20.2 %collective-permute-start.31 = (bf16[40,768]{1,0:T(8,128)(2,1)S(1)}, bf16[40,768]{1,0:T(8,128)(2,1)S(1)}, u32[]{:S(2)}, u32[]{:S(2)}) collective-permute-start(bf16[40,768]{1,0:T(8,128)(2,1)S(1)} %get-tuple-element.287), channel_id=1, source_target_pairs={{0,4},{8,0},{16,8},{24,16},{28,24},{20,28},{12,20},{4,12},{1,5},{9... | collective-permute-start | bytes 184328 | tf_op jit(solution)/shard_map/ppermute | solution.py:902
  394.0 29.2 %collective-permute-start.32 = (bf16[384,768]{1,0:T(8,128)(2,1)S(1)}, bf16[384,768]{1,0:T(8,128)(2,1)}, u32[]{:S(2)}, u32[]{:S(2)}) collective-permute-start(bf16[384,768]{1,0:T(8,128)(2,1)S(1)} %get-tuple-element.274), channel_id=1, source_target_pairs={{0,8},{8,16},{16,24},{24,28},{28,20},{20,12},{12,4},{4,0},{1,9},{9... | collective-permute-start | bytes 1769480 | tf_op jit(solution)/shard_map/ppermute | solution.py:902
  395.2 28.0 %collective-permute-start.33 = (bf16[384,768]{1,0:T(8,128)(2,1)S(1)}, bf16[384,768]{1,0:T(8,128)(2,1)}, u32[]{:S(2)}, u32[]{:S(2)}) collective-permute-start(bf16[384,768]{1,0:T(8,128)(2,1)S(1)} %get-tuple-element.273), channel_id=1, source_target_pairs={{0,4},{8,0},{16,8},{24,16},{28,24},{20,28},{12,20},{4,12},{1,5},{9... | collective-permute-start | bytes 1769480 | tf_op jit(solution)/shard_map/ppermute | solution.py:902
  396.1 24.8 %collective-permute-start.34 = (bf16[80,768]{1,0:T(8,128)(2,1)S(1)}, bf16[80,768]{1,0:T(8,128)(2,1)S(1)}, u32[]{:S(2)}, u32[]{:S(2)}) collective-permute-start(bf16[80,768]{1,0:T(8,128)(2,1)S(1)} %get-tuple-element.286), channel_id=1, source_target_pairs={{0,8},{8,16},{16,24},{24,28},{28,20},{20,12},{12,4},{4,0},{1,9},{9... | collective-permute-start | bytes 368648 | tf_op jit(solution)/shard_map/ppermute | solution.py:902
  397.3 25.9 %collective-permute-start.35 = (bf16[80,768]{1,0:T(8,128)(2,1)S(1)}, bf16[80,768]{1,0:T(8,128)(2,1)}, u32[]{:S(2)}, u32[]{:S(2)}) collective-permute-start(bf16[80,768]{1,0:T(8,128)(2,1)S(1)} %get-tuple-element.285), channel_id=1, source_target_pairs={{0,4},{8,0},{16,8},{24,16},{28,24},{20,28},{12,20},{4,12},{1,5},{9... | collective-permute-start | bytes 368648 | tf_op jit(solution)/shard_map/ppermute | solution.py:902
  (58 other events, 747.8 us)
Sparse Core Ops, SparseCore 0:
  77.1 51.3 all-gather.10
  130.0 35.9 all-gather.6
  211.7 108.2 reduce-scatter.1
  322.9 61.0 all-gather.12
  386.2 71.7 all-gather.8

commit v3 on v2

--- a/solution.py
+++ b/solution.py
@@ -528,13 +528,13 @@
 
 def ffn_kernel(wt_count, sc, att_ref, x_ref, dy_ref, gain_ref, *refs):
     n = wt_count
-    halves = (len(refs) - 16) // n
-    wo_shares, win_shares = refs[:n], [refs[(i + 1) * n : (i + 2) * n] for i in range(halves)]
+    halves = (len(refs) - 15) // n - 2
+    groups = [refs[i * n : (i + 1) * n] for i in range(halves + 2)]
+    wo_shares, win_shares, wout_shares = groups[0], groups[1:-1], groups[-1]
     (
-        wout_ref,
         out_ref, gm_ref, gatt_ref, keep_ref, send_ref, gain_out, sq_ref,
-        middle_s, low_s, low_t, feed_s, grad_s, wo_ref, win_ref,
-    ) = refs[(halves + 1) * n :]
+        middle_s, low_s, low_t, feed_s, grad_s, wo_ref, win_ref, wout_ref,
+    ) = refs[(halves + 2) * n :]
     j = pl.program_id(0)
     last = pl.num_programs(0) - 1
     me = sc[5]
@@ -547,6 +547,12 @@
                     assemble, me, win_ref, win_shares[i], per, slice(side * width, (side + 1) * width)
                 )
             )
+
+    def take(share):
+        wout_ref[...] = share[...]
+
+    for i, share in enumerate(wout_shares):
+        pl.when((j ^ me) == i)(functools.partial(take, share))
 
     @pl.when(j == 0)
     def start():
@@ -616,7 +622,7 @@
     whole = lambda j, sc: (0, 0, 0)
     once = pl.Buffered(1)
     kernel = functools.partial(ffn_kernel, wt_count)
-    shares = [*wo, *(share for win in wins for share in win)]
+    shares = [*wo, *(share for win in wins for share in win), *wout]
     return pl.pallas_call(
         kernel,
         grid_spec=pltpu.PrefetchScalarGridSpec(
@@ -628,8 +634,7 @@
                 pl.BlockSpec((rows, width), fixed, pipeline_mode=once),
                 pl.BlockSpec((1, width), fixed),
             ]
-            + [pl.BlockSpec(w.shape, fixed, pipeline_mode=once) for w in shares]
-            + [pl.BlockSpec((width, width), lambda j, sc: (j, 0))],
+            + [pl.BlockSpec(w.shape, fixed, pipeline_mode=once) for w in shares],
             out_specs=[
                 pl.BlockSpec((rows, width), fixed),
                 pl.BlockSpec((rows, width), fixed),
@@ -647,6 +652,7 @@
                 pltpu.VMEM((rows, width), F32),
                 pltpu.VMEM((width, width), BF16),
                 pltpu.VMEM((width, width), BF16),
+                pltpu.VMEM((width, width), BF16),
             ],
         ),
         out_shape=[
@@ -659,7 +665,7 @@
             jax.ShapeDtypeStruct((sq_rows, 128), F32),
         ],
         **params(10 * chunks * rows * width * width + 6 * rows * width * width, 24 * width * width),
-    )(scalars, att, x, dy, gain, *shares, wout)
+    )(scalars, att, x, dy, gain, *shares)
 
 
 TAIL_ROWS = 16
@@ -819,19 +825,17 @@
 
 
 def finish_kernel(entries, heads, sc, *refs):
-    count = len(refs) - 12
-    pieces, (wq_ref, wk_ref, wv_ref), outs, whole = refs[:count], refs[count : count + 3], refs[-9:-1], refs[-1]
+    count = len(refs) - 13
+    pieces, (wq_ref, wk_ref, wv_ref, own_ref), outs, whole = refs[:count], refs[count : count + 4], refs[-9:-1], refs[-1]
     dq_ref, dk_ref, dv_ref, gain_ref, two_ref, logit_ref, weight_ref, rms_ref = outs
-    per = pieces[0].shape[0]
-    for n, piece in enumerate(pieces):
-        whole[pl.ds(pl.multiple_of(sc[n] * per, 8), per), :] = piece[...].astype(F32)
+    gather_rows(sc, pieces, whole)
     rows = wq_ref.shape[0]
     gain = jnp.zeros((rows, 1), F32)
     for n, (out, w) in enumerate(((dq_ref, wq_ref), (dk_ref, wk_ref), (dv_ref, wv_ref))):
         found = whole[n * rows : (n + 1) * rows, :]
         out[...] = found
         gain += jnp.sum(found * w[...].astype(F32), axis=1, keepdims=True)
-    gain_ref[...] = gain
+    gain_ref[...] = jnp.broadcast_to(gain, (rows, 128)).T[0:1, :] / own_ref[...].astype(F32)
     tail = whole[3 * rows : 3 * rows + TAIL_ROWS, :]
     each = logit_ref.shape[0]
     two_ref[...] = tail[0:1, :rows]
@@ -840,11 +844,11 @@
     weight_ref[...] = tail[4 + each : 4 + 2 * each, :heads]
 
 
-def finish_grads(places, pieces, wq, wk, wv, entries, heads, each):
+def finish_grads(places, pieces, wq, wk, wv, gain, entries, heads, each):
     count = len(pieces)
     rows, width = wq.shape
-    ins = [*pieces, wq, wk, wv]
-    shapes = [(rows, width)] * 3 + [(rows, 1), (1, rows), (each, heads), (each, heads), (3, 1)]
+    ins = [*pieces, wq, wk, wv, gain]
+    shapes = [(rows, width)] * 3 + [(1, rows), (1, rows), (each, heads), (each, heads), (3, 1)]
     fixed = lambda i, sc: (0, 0)
     return pl.pallas_call(
         functools.partial(finish_kernel, entries, heads),
@@ -860,22 +864,40 @@
     )(places, *ins)
 
 
-def unpack_kernel(sum_ref, out_ref, in_ref, o_ref):
+def gather_rows(sc, pieces, whole):
+    per = pieces[0].shape[0]
+    for n, piece in enumerate(pieces):
+        whole[pl.ds(pl.multiple_of(sc[n] * per, 8), per), :] = piece[...].astype(F32)
+
+
+def unpack_kernel(sc, *refs):
+    pieces, (out_ref, in_ref, o_ref, whole) = refs[:-4], refs[-4:]
+    gather_rows(sc, pieces, whole)
     rows, width = out_ref.shape
     per = o_ref.shape[0]
-    out_ref[...] = sum_ref[:rows, :].astype(F32)
+    out_ref[...] = whole[:rows, :]
     chunks = in_ref.shape[1] // width
     for n in range(chunks):
-        in_ref[:, n * width : (n + 1) * width] = sum_ref[rows + n * per : rows + (n + 1) * per, :].astype(F32)
-    o_ref[...] = sum_ref[rows + chunks * per :, :].astype(F32)
-
-
-def unpack(total, shapes):
+        in_ref[:, n * width : (n + 1) * width] = whole[rows + n * per : rows + (n + 1) * per, :]
+    o_ref[...] = whole[rows + chunks * per :, :]
+
+
+def unpack(places, pieces, shapes):
+    total = len(pieces) * pieces[0].shape[0]
+    width = pieces[0].shape[1]
+    fixed = lambda i, sc: (0, 0)
     return pl.pallas_call(
         unpack_kernel,
+        grid_spec=pltpu.PrefetchScalarGridSpec(
+            num_scalar_prefetch=1,
+            grid=(1,),
+            in_specs=[pl.BlockSpec(v.shape, fixed) for v in pieces],
+            out_specs=[pl.BlockSpec(v, fixed) for v in shapes],
+            scratch_shapes=[pltpu.VMEM((total, width), F32)],
+        ),
         out_shape=[jax.ShapeDtypeStruct(shape, F32) for shape in shapes],
-        **params(0, 6 * total.size, 0),
-    )(total)
+        **params(0, 6 * total * width),
+    )(places, *pieces)
 
 
 def swaps(size, distance):
@@ -951,13 +973,45 @@
     return jnp.concatenate([up, empty], axis=0), jnp.concatenate([empty, down], axis=0)
 
 
+class Spreading:
+    def __init__(self, piece, count):
+        self.count, self.last = count, count // 2
+        self.up = self.down = piece
+        self.pieces = {0: piece}
+        self.step = 0
+
+    @property
+    def done(self):
+        return self.step == self.last
+
+    def start(self):
+        if self.step < self.last - 1:
+            return ring_both(self.up, self.down)
+        half = self.up.shape[0] // 2
+        return ring_both(self.up[:half], self.down[half:])
+
+    def finish(self, up, down):
+        self.step += 1
+        if self.done:
+            self.pieces[self.last] = jnp.concatenate([up, down], axis=0)
+        else:
+            self.pieces[self.count - self.step], self.pieces[self.step] = up, down
+        self.up, self.down = up, down
+
+    def ordered(self):
+        return [self.pieces[n] for n in range(self.count)]
+
+
 class Turning:
     def __init__(self, blocks, me):
-        self.count = blocks.shape[0]
+        self.count, self.last = blocks.shape[0], blocks.shape[0] // 2
         self.blocks, self.me = blocks, me
-        self.step, self.last = 0, self.count // 2
-        self.pieces = []
-        self.done = False
+        self.step = 0
+        self.spread = None
+
+    @property
+    def done(self):
+        return self.spread is not None and self.spread.done
 
     def at(self, offset):
         place = ring_places(self.count, self.me, [offset])[0]
@@ -965,36 +1019,21 @@
 
     def start(self):
         step, last = self.step, self.last
+        if self.spread is not None:
+            return self.spread.start()
         if step == 0:
             return far_start(self.at(last))
-        if step < last:
-            return ring_both(
-                add(self.up, self.at(last - step)), add(self.down, self.at(step - last))
-            )
-        if step < 2 * last - 1:
-            return ring_both(self.up, self.down)
-        half = self.up.shape[0] // 2
-        return ring_both(self.up[:half], self.down[half:])
+        return ring_both(add(self.up, self.at(last - step)), add(self.down, self.at(step - last)))
 
     def finish(self, up, down):
-        step, last = self.step, self.last
-        if step == 0:
+        if self.spread is not None:
+            return self.spread.finish(up, down)
+        if self.step == 0:
             up, down = far_end(up, down)
-        elif step == last - 1:
-            up = down = add(up, down, self.at(0))
-            self.pieces.append((0, up))
-        elif last <= step < 2 * last - 1:
-            k = step - last + 1
-            self.pieces += [(-k, up), (k, down)]
-        elif step == 2 * last - 1:
-            self.pieces.append((last, jnp.concatenate([up, down], axis=0)))
-            self.done = True
+        elif self.step == self.last - 1:
+            self.spread = Spreading(add(up, down, self.at(0)), self.count)
         self.up, self.down = up, down
         self.step += 1
-
-    def ordered(self):
-        found = {offset % self.count: piece for offset, piece in self.pieces}
-        return [found[n] for n in range(self.count)]
 
 
 def shards(
@@ -1103,8 +1142,9 @@
         both = lax.ppermute(crossed[n], "wt", swaps(wt_count, 1))
         q, near, both = lax.optimization_barrier((q, near, both))
         shares.append([stages[n], near, crossed[n], both])
-    w_out_after, _ = lax.optimization_barrier((w_out, rounds[-1][0][1]))
-    outer_mat = lax.all_gather(w_out_after, "wt", axis=0, tiled=True)
+    w_out, q = tie(w_out, q)
+    far_out = lax.ppermute(w_out, "wt", swaps(wt_count, 2))
+    near_out = lax.ppermute(w_out, "wt", swaps(wt_count, 1))
 
     def exchange(second):
         every = lax.all_gather(second, "ctx", axis=0)
@@ -1114,20 +1154,24 @@
     dy_low = jnp.concatenate([cotangent[0, :half], exchange(dy_second)], axis=0)
 
     attended, t, lse = attend(scalars, q, k, vt, mix_rows, spread, heads)
+    far_out, attended = tie(far_out, attended)
+    out_shares = [w_out, near_out, far_out, lax.ppermute(far_out, "wt", swaps(wt_count, 1))]
     out_low, grad_middle, grad_att, keep, send, grad_gain_two, squares = ffn(
         scalars, wt_count, heads, attended.reshape(rows, width), x_low, dy_low, gain_two,
-        qo_shares, shares[2:], outer_mat,
+        qo_shares, shares[2:], out_shares,
     )
-    output_own = jnp.concatenate([out_low[:half], exchange(out_low[half:])], axis=0)
     grad_att = grad_att.reshape(2, half, width)
     grad_middle = grad_middle.reshape(2, half, width)
 
     got = lax.ppermute(send, "wt", swaps(wt_count, 1))
     r_weight, delta = deltas(grad_att, t, spread, heads)
     summed = add(keep, got).reshape(2, count, -1, width).transpose(1, 0, 2, 3).reshape(-1, width)
-    summed, delta = tie(summed, delta)
+    leaving = Spreading(out_low[half:], count)
+    summed, delta, *moved = tie(summed, delta, *leaving.start())
+    leaving.finish(*moved)
     summed = lax.psum_scatter(summed, "ctx", scatter_dimension=0, tiled=True)
 
+    moved = leaving.start()
     dk, dv, dq, r_logit = back(
         scalars, 0, heads, q, grad_att, k, v, kt, lse, delta, mix_rows, weight_by_g,
         logit_spread, heads, scale,
@@ -1139,50 +1183,80 @@
         )
 
     last = count // 2
-    far = parts(count - 1, 1, dk)
-    dk, far = tie(dk, far)
-    up, down = far_start(far[0])
     total = -(-(3 * per + TAIL_ROWS) // (8 * count)) * 8 * count
+    dk, *moved = tie(dk, *moved)
+    leaving.finish(*moved)
+    moved = leaving.start()
     keep, send = weight_grads(
         scalars, wt_count, total, dk, dv, dq, nt, r_logit, r_weight, grad_gain_two, squares
     )
-    up, down, keep, send, summed, dk = tie(up, down, keep, send, summed, dk)
+    send, dk, *moved = tie(send, dk, *moved)
+    leaving.finish(*moved)
+    near = lax.ppermute(send, "wt", swaps(wt_count, 1))
+    far = parts(count - 1, 1, dk)
+    near, far, summed, *moved = tie(near, far, summed, *leaving.start())
+    leaving.finish(*moved)
+    summed = summed.reshape(2, -1, width)
+    ffn_far = lax.ppermute(summed[1], "wt", swaps(wt_count, 2))
+    up, down = far_start(far[0])
+    over = lax.ppermute(add(keep[1], near[1]), "wt", swaps(wt_count, 2))
+    pair = parts(2 * (last - 1) - 1, 2, dk)
+    up, down, pair, ffn_far = tie(up, down, pair, ffn_far)
     up, down = far_end(up, down)
-    summed = summed.reshape(2, -1, width)
-    near = lax.ppermute(send, "wt", swaps(wt_count, 1))
-    ffn_far = lax.ppermute(summed[1], "wt", swaps(wt_count, 2))
-    pair = parts(2 * (last - 1) - 1, 2, dk)
-    near, ffn_far, pair = tie(near, ffn_far, pair)
-    over = lax.ppermute(add(keep[1], near[1]), "wt", swaps(wt_count, 2))
-    share = add(summed[0], ffn_far)
+    spread = Spreading(add(summed[0], ffn_far), count)
 
     turn = None
     for k in range(last - 1, 0, -1):
         up, down = ring_both(add(up, pair[1]), add(down, pair[0]))
-        beside = [over, share] if turn is None else list(turn.start())
+        streams = [s for s in (spread, leaving) if not s.done]
+        moved = [stream.start() for stream in streams]
         after = parts(2 * (k - 1) - 1, 2, dk) if k > 1 else parts(0, 1, dk)
-        up, down, pair, *beside = tie(up, down, after, *beside)
         if turn is None:
-            over, share = beside
-            ffn_sum = lax.all_gather(share, "ctx", axis=0, tiled=True)
+            up, down, pair, moved, over = tie(up, down, after, moved, over)
             turn = Turning(add(keep[0], near[0], over).reshape(count, -1, width), me)
         else:
-            turn.finish(*beside)
+            if not turn.done:
+                after, *both = tie(after, *turn.start())
+                turn.finish(*both)
+            both = [] if turn.done else turn.start()
+            up, down, pair, moved, both = tie(up, down, after, moved, both)
+            if both:
+                turn.finish(*both)
+        for stream, both in zip(streams, moved):
+            stream.finish(*both)
     input_grad = add(up, down, pair[0])
+    while not leaving.done:
+        leaving.finish(*tie(*leaving.start()))
+    order_places = jnp.where((partner & 1) == 0, partner >> 1, count - 1 - (partner >> 1))
+    own_place = jnp.where((me & 1) == 0, me >> 1, count - 1 - (me >> 1))
+    offset = (order_places - own_place) & (count - 1)
+    second = leaving.pieces[1]
+    for n in range(2, count):
+        second = jnp.where(offset == n, leaving.pieces[n], second)
+    output_own = jnp.concatenate([out_low[:half], second], axis=0)
+    places = ring_places(count, me, list(range(count))).astype(jnp.int32)
+    ffn_grads = None
     while not turn.done:
-        turn.finish(*tie(*turn.start()))
-
-    places = ring_places(count, me, list(range(count))).astype(jnp.int32)
+        moving = [] if spread.done else list(spread.start())
+        one, two, *moving = tie(*turn.start(), *moving)
+        turn.finish(one, two)
+        if moving:
+            spread.finish(*moving)
+        elif ffn_grads is None:
+            ffn_grads = unpack(places, spread.ordered(), (w_out.shape, w_in.shape, w_output.shape))
+            turn_start = list(turn.start())
+            one, two, *ffn_grads = tie(*turn_start, *ffn_grads)
+            turn.finish(one, two)
+    grad_out, grad_in, grad_o = ffn_grads
     entries = float(rows * width) * (count * wt_count)
-    grad_q, grad_k, grad_v, gain_sum, gain_two_grad, logit_grad, weight_grad, rms = finish_grads(
-        places, turn.ordered(), w_query, w_key, w_value, entries, heads, heads // wt_count
+    grad_q, grad_k, grad_v, gain_grad, gain_two_grad, logit_grad, weight_grad, rms = finish_grads(
+        places, turn.spread.ordered(), w_query, w_key, w_value, gain_attn[None, :], entries, heads, heads // wt_count
     )
-    grad_out, grad_in, grad_o = unpack(ffn_sum, (w_out.shape, w_in.shape, w_output.shape))
     return (
         output_own[None],
         input_grad[None],
         rms.reshape(3),
-        gain_sum.reshape(per) / gain_attn.astype(F32),
+        gain_grad.reshape(per),
         grad_q,
         grad_k,
         grad_v,

time: 501 us -> 472 us (0.942)
  waiting for transfers between devices: 128 us -> 69.5 us
  starting transfers between devices: 45.4 us -> 61.2 us
    ppermute x16 -> x24, waiting for transfers between devices: 58.3 us -> 34.8 us  [ring_both(): lax.ppermute(up, 'ctx', ring(count, 1))]
    all_gather x2 -> x0, waiting for transfers between devices: 17.1 us -> none  [the longest x1 17.1 us: shards(): outer_mat = lax.all_gather(w_out_after, 'wt', axis=0, tiled=True)]
    ppermute x16 -> x24, starting transfers between devices: 22 us -> 34.5 us  [ring_both(): lax.ppermute(up, 'ctx', ring(count, 1))]
    ppermute x16 -> x24, waiting for transfers between devices: 29.5 us -> 21.4 us  [ring_both(): lax.ppermute(down, 'ctx', ring(count, -1))]
    ppermute x16 -> x24, starting transfers between devices: 15.3 us -> 17.2 us  [ring_both(): lax.ppermute(down, 'ctx', ring(count, -1))]
  transfers between devices with their start and end apart: 53 -> 69, of which waited for: 29 -> 22; matrix products, arithmetic and copies ran while one was open for 9% -> 10% of each run, Pallas kernels for 44% -> 48%
where the time goes in v3:
time: 472 us; the launch traced here: 464 us
  Pallas kernels  254 us (54%)
  waiting for transfers between devices  69.5 us (15%)
  starting transfers between devices  61.2 us (13%)
  other arithmetic  33.9 us (7%)
  local copies, waits for them, and re-layouts  25.7 us (5%)
  between operations  19.8 us (4%)
    pallas_call x1, Pallas kernels, back(): pl.pallas_call(functools.partial(back_kernel, count, heads, base, group,...  82.6 us
    pallas_call x1, Pallas kernels, attend(): pl.pallas_call(functools.partial(attend_kernel, count, heads, group), gri...  44.7 us
    ppermute x24, waiting for transfers between devices, ring_both(): lax.ppermute(up, 'ctx', ring(count, 1))  34.8 us
    ppermute x24, starting transfers between devices, ring_both(): lax.ppermute(up, 'ctx', ring(count, 1))  34.5 us
    pallas_call x5, Pallas kernels, token_parts(): pl.pallas_call(functools.partial(token_kernel, count, first), grid_spec=p...  33.7 us
    pallas_call x1, Pallas kernels, ffn(): pl.pallas_call(kernel, grid_spec=pltpu.PrefetchScalarGridSpec(num_scalar_...  29.7 us
    pallas_call x3, Pallas kernels, project(): pl.pallas_call(functools.partial(project_kernel, batch, shares), grid_spe...  26.5 us
    convert_element_type x11, other arithmetic, add(): return sum((v.astype(F32) for v in values)).astype(BF16)  22.4 us
  transfers between devices with their start and end apart: 69, of which 22 were waited for; matrix products, arithmetic and copies ran while one was open for 10% of the time, Pallas kernels for 48%

profile of v3, /device:TPU:0, one launch (start us, length us, event | category | flops | bytes accessed | tf_op | source)
XLA Modules:
  0.0 464.2 jit_solution(13081243551812175187)
XLA Ops:
  25.5 5.0 %collective-permute-done.2.refs_6_ = bf16[208,1536]{1,0:T(8,128)(2,1)} collective-permute-done((bf16[208,1536]{1,0:T(8,128)(2,1)S(1)}, bf16[208,1536]{1,0:T(8,128)(2,1)}, u32[]{:S(2)}, u32[]{:S(2)}) %collective-permute-start.2) | collective-permute-done | bytes 639008 | tf_op jit(solution)/shard_map/ppermute | solution.py:946
  34.4 7.2 %collective-permute-done.7.refs_2_ = bf16[192,1536]{1,0:T(8,128)(2,1)S(1)} collective-permute-done((bf16[192,1536]{1,0:T(8,128)(2,1)S(1)}, bf16[192,1536]{1,0:T(8,128)(2,1)S(1)}, u32[]{:S(2)}, u32[]{:S(2)}) %collective-permute-start.7) | collective-permute-done | bytes 589856 | tf_op jit(solution)/shard_map/ppermute | solution.py:946
  51.9 10.0 %shard_map.327 = (bf16[8,384,768]{2,1,0:T(8,128)(2,1)}, bf16[8,384,768]{2,1,0:T(8,128)(2,1)}, bf16[8,768,384]{2,1,0:T(8,128)(2,1)}, bf16[8,768,384]{2,1,0:T(8,12...) custom-call(s32[30]{0:T(128)} %concatenate.55.sc, ...), custom_call_target="tpu_custom_call" | custom-call | flops 2717908992 | bytes 12386304 | tf_op jit(solution)/shard_map/pallas_call | solution.py:106
  71.0 7.3 %shard_map.328 = (bf16[8,384,768]{2,1,0:T(8,128)(2,1)}, bf16[8,384,768]{2,1,0:T(8,128)(2,1)}, bf16[8,768,384]{2,1,0:T(8,128)(2,1)}, bf16[8,768,384]{2,1,0:T(8,12...) custom-call(s32[30]{0:T(128)} %concatenate.55.sc, ...), custom_call_target="tpu_custom_call", output_to_operand_aliasing={{0}: (5, {}), {1}: (6, {}), {2}: (7, {}), {3}: (8, {}), {4}... | custom-call | flops 1811939328 | bytes 8257536 | tf_op jit(solution)/shard_map/pallas_call | solution.py:106
  79.3 9.2 %shard_map.329 = (bf16[8,384,768]{2,1,0:T(8,128)(2,1)}, bf16[8,384,768]{2,1,0:T(8,128)(2,1)}, bf16[8,768,384]{2,1,0:T(8,128)(2,1)}, bf16[8,768,384]{2,1,0:T(8,12...) custom-call(s32[30]{0:T(128)} %concatenate.55.sc, ...), custom_call_target="tpu_custom_call", output_to_operand_aliasing={{0}: (6, {}), {1}: (7, {}), {2}: (8, {}), {3}: (9, {}), {4}... | custom-call | flops 2717908992 | bytes 12386304 | tf_op jit(solution)/shard_map/pallas_call | solution.py:106
  90.6 4.4 shard_map.330
  95.8 44.7 %shard_map.331 = (bf16[2,192,768]{2,1,0:T(8,128)(2,1)}, bf16[2,768,2304]{2,1,0:T(8,128)(2,1)}, f32[2,1,2304]{2,1,0:T(1,128)}) custom-call(s32[30]{0:T(128)} %concatenate.55.sc, bf16[2,192,768]{2,1,0:T(8,128)(2,1)} %get-tuple-element.212.q_ref, bf16[8,384,768]{2,1,0:T(8,128)(2,1)} %get-tuple-element.213.k_ref, ...), custom_call_target="tpu_custom_call" | custom-call | flops 24461180928 | bytes 14155776 | tf_op jit(solution)/shard_map/pallas_call | solution.py:272
  145.4 29.7 %shard_map.332 = (bf16[384,768]{1,0:T(8,128)(2,1)}, f32[384,768]{1,0:T(8,128)}, bf16[384,768]{1,0:T(8,128)(2,1)}, bf16[2,1728,768]{2,1,0:T(8,128)(2,1)}, bf16[2,...) custom-call(s32[30]{0:T(128)} %concatenate.55.sc, bf16[384,768]{1,0:T(8,128)(2,1)} %bitcast.119, ...), custom_call_target="tpu_custom_call" | custom-call | flops 10418651136 | bytes 14155776 | tf_op jit(solution)/shard_map/pallas_call | solution.py:626
  179.2 5.2 %shard_map.333 = (f32[12,128]{1,0:T(8,128)}, f32[2,1,2304]{2,1,0:T(1,128)}) custom-call(bf16[2,192,768]{2,1,0:T(8,128)(2,1)} %bitcast.110, bf16[2,768,2304]{2,1,0:T(8,128)(2,1)} %get-tuple-element.228.t_ref, f32[12,2304]{1,0:T(8,128)} %reshape.123.spread_ref), custom_call_target="tpu_custom_call" | custom-call | flops 7077888 | bytes 7077888 | tf_op jit(solution)/shard_map/pallas_call | solution.py:352
  184.5 5.3 %add_convert_fusion = bf16[2,1728,768]{2,1,0:T(8,128)(2,1)S(1)} fusion(bf16[2,1728,768]{2,1,0:T(8,128)(2,1)} %collective-permute-done.23, bf16[2,1728,768]{2,1,0:T(8,128)(2,1)} %get-tuple-element.225), kind=kLoop, calls=%fused_computation | loop fusion | flops 10616832 | bytes 15925248 | tf_op jit(solution)/shard_map/convert_element_type | solution.py:962
  196.2 82.6 %shard_map.334 = (bf16[8,384,768]{2,1,0:T(8,128)(2,1)}, bf16[8,384,768]{2,1,0:T(8,128)(2,1)}, bf16[2,192,768]{2,1,0:T(8,128)(2,1)}, f32[12,128]{1,0:T(8,128)}) custom-call(s32[30]{0:T(128)} %concatenate.55.sc, bf16[2,192,768]{2,1,0:T(8,128)(2,1)} %get-tuple-element.212.q_ref, bf16[2,192,768]{2,1,0:T(8,128)(2,1)} %bitcast.111, ...), custom_call_target="tpu_custom_call" | custom-call | flops 61152952320 | bytes 23592960 | tf_op jit(solution)/shard_map/pallas_call | solution.py:462
  281.0 18.4 %shard_map.335 = (bf16[2,640,768]{2,1,0:T(8,128)(2,1)}, bf16[2,640,768]{2,1,0:T(8,128)(2,1)}) custom-call(s32[30]{0:T(128)} %concatenate.55.sc, bf16[8,384,768]{2,1,0:T(8,128)(2,1)} %get-tuple-element.250.dk_ref, bf16[8,384,768]{2,1,0:T(8,128)(2,1)} %get-tuple-element.239.dv_ref, bf16[2,192,768]{2,1,0:T(8,128)(2,1)} %get-tuple-element.240.dq_ref, ...), custom_call_target="tpu_custom_call" | custom-call | flops 7247757312 | bytes 23592960 | tf_op jit(solution)/shard_map/pallas_call | solution.py:744
  305.1 6.0 %shard_map.336 = bf16[1,384,768]{2,1,0:T(8,128)(2,1)} custom-call(s32[30]{0:T(128)} %concatenate.55.sc, bf16[8,384,768]{2,1,0:T(8,128)(2,1)} %get-tuple-element.250.dk_ref, bf16[8,384,768]{2,1,0:T(8,128)(2,1)} %get-tuple-element.239.dv_ref, bf16[2,192,768]{2,1,0:T(8,128)(2,1)} %get-tuple-element.240.dq_ref, bf16[8,384,768]{2,1,0:T(8,128)(2,1)} %get-tuple-element.205.x_ref, ...), custom_call_target="tpu_custom_call" | custom-call | flops 905969664 | bytes 2359296 | tf_op jit(solution)/shard_map/pallas_call | solution.py:805
  319.7 6.2 %shard_map.337 = bf16[2,384,768]{2,1,0:T(8,128)(2,1)} custom-call(s32[30]{0:T(128)} %concatenate.55.sc, bf16[8,384,768]{2,1,0:T(8,128)(2,1)} %get-tuple-element.250.dk_ref, bf16[8,384,768]{2,1,0:T(8,128)(2,1)} %get-tuple-element.239.dv_ref, bf16[2,192,768]{2,1,0:T(8,128)(2,1)} %get-tuple-element.240.dq_ref, bf16[8,384,768]{2,1,0:T(8,128)(2,1)} %get-tuple-element.205.x_ref, ...), custom_call_target="tpu_custom_call" | custom-call | flops 1811939328 | bytes 4718592 | tf_op jit(solution)/shard_map/pallas_call | solution.py:805
  334.7 7.4 %shard_map.338 = bf16[2,384,768]{2,1,0:T(8,128)(2,1)} custom-call(s32[30]{0:T(128)} %concatenate.55.sc, bf16[8,384,768]{2,1,0:T(8,128)(2,1)} %get-tuple-element.250.dk_ref, bf16[8,384,768]{2,1,0:T(8,128)(2,1)} %get-tuple-element.239.dv_ref, bf16[2,192,768]{2,1,0:T(8,128)(2,1)} %get-tuple-element.240.dq_ref, bf16[8,384,768]{2,1,0:T(8,128)(2,1)} %get-tuple-element.205.x_ref, ...), custom_call_target="tpu_custom_call" | custom-call | flops 1811939328 | bytes 4718592 | tf_op jit(solution)/shard_map/pallas_call | solution.py:805
  342.1 8.6 %collective-permute-done.38.refs_7_ = bf16[216,768]{1,0:T(8,128)(2,1)} collective-permute-done((bf16[216,768]{1,0:T(8,128)(2,1)S(1)}, bf16[216,768]{1,0:T(8,128)(2,1)}, u32[]{:S(2)}, u32[]{:S(2)}) %collective-permute-start.38) | collective-permute-done | bytes 331808 | tf_op jit(solution)/shard_map/ppermute | solution.py:924
  359.6 7.4 %shard_map.339 = bf16[2,384,768]{2,1,0:T(8,128)(2,1)} custom-call(s32[30]{0:T(128)} %concatenate.55.sc, bf16[8,384,768]{2,1,0:T(8,128)(2,1)} %get-tuple-element.250.dk_ref, bf16[8,384,768]{2,1,0:T(8,128)(2,1)} %get-tuple-element.239.dv_ref, bf16[2,192,768]{2,1,0:T(8,128)(2,1)} %get-tuple-element.240.dq_ref, bf16[8,384,768]{2,1,0:T(8,128)(2,1)} %get-tuple-element.205.x_ref, ...), custom_call_target="tpu_custom_call" | custom-call | flops 1811939328 | bytes 4718592 | tf_op jit(solution)/shard_map/pallas_call | solution.py:805
  368.4 4.9 %collective-permute-done.43 = bf16[40,768]{1,0:T(8,128)(2,1)S(1)} collective-permute-done((bf16[40,768]{1,0:T(8,128)(2,1)S(1)}, bf16[40,768]{1,0:T(8,128)(2,1)S(1)}, u32[]{:S(2)}, u32[]{:S(2)}) %collective-permute-start.43) | collective-permute-done | bytes 61472 | tf_op jit(solution)/shard_map/ppermute | solution.py:924
  376.0 4.2 collective-permute-done.47
  382.2 3.9 collective-permute-done.48
  394.3 6.7 %shard_map.340 = bf16[1,384,768]{2,1,0:T(8,128)(2,1)} custom-call(s32[30]{0:T(128)} %concatenate.55.sc, bf16[8,384,768]{2,1,0:T(8,128)(2,1)} %get-tuple-element.250.dk_ref, bf16[8,384,768]{2,1,0:T(8,128)(2,1)} %get-tuple-element.239.dv_ref, bf16[2,192,768]{2,1,0:T(8,128)(2,1)} %get-tuple-element.240.dq_ref, bf16[8,384,768]{2,1,0:T(8,128)(2,1)} %get-tuple-element.205.x_ref, ...), custom_call_target="tpu_custom_call" | custom-call | flops 905969664 | bytes 2359296 | tf_op jit(solution)/shard_map/pallas_call | solution.py:805
  405.7 8.2 %collective-permute-done.55 = bf16[80,768]{1,0:T(8,128)(2,1)S(1)} collective-permute-done((bf16[80,768]{1,0:T(8,128)(2,1)S(1)}, bf16[80,768]{1,0:T(8,128)(2,1)S(1)}, u32[]{:S(2)}, u32[]{:S(2)}) %collective-permute-start.55) | collective-permute-done | bytes 122912 | tf_op jit(solution)/shard_map/ppermute | solution.py:924
  415.6 4.6 collective-permute-done.56
  440.2 5.2 %shard_map.341 = (f32[768,768]{1,0:T(8,128)}, f32[192,3072]{1,0:T(8,128)}, f32[192,768]{1,0:T(8,128)}) custom-call(s32[8]{0:T(128)} %compare_select_fusion.sc, bf16[216,768]{1,0:T(8,128)(2,1)} %copy-done.5, bf16[216,768]{1,0:T(8,128)(2,1)} %collective-permute-done.39.refs_1_, bf16[216,768]{1,0:T(8,128)(2,1)} %collective-permute-done.46.refs_2_, ...), custom_call_target="tpu_custom_call" | custom-call | bytes 7962624 | tf_op jit(solution)/shard_map/pallas_call | solution.py:889
  (294 shorter events, 141.8 us)
Async XLA Ops:
  7.2 136.3 %all-gather.3.cloned.1.call-start = ((), (), s32[]{:S(2)}) async-start(), calls=%async_computation.2 | async-start | bytes 2654208 | tf_op jit(solution)/shard_map/all_gather | solution.py:1150
  15.0 26.6 %collective-permute-start.5 = (bf16[208,1536]{1,0:T(8,128)(2,1)S(1)}, bf16[208,1536]{1,0:T(8,128)(2,1)}, u32[]{:S(2)}, u32[]{:S(2)}) collective-permute-start(bf16[208,1536]{1,0:T(8,128)(2,1)S(1)} %pad_maximum_fusion.refs_4_), channel_id=1, source_target_pairs={{0,1},{1,0},{2,3},{3,2},{4,5},{5,4},{6,7},{7,6},{8,9},{9,8},{10,11... | collective-permute-start | bytes 1916936 | tf_op jit(solution)/shard_map/ppermute | solution.py:943
  16.0 25.5 %collective-permute-start.7 = (bf16[192,1536]{1,0:T(8,128)(2,1)S(1)}, bf16[192,1536]{1,0:T(8,128)(2,1)S(1)}, u32[]{:S(2)}, u32[]{:S(2)}) collective-permute-start(bf16[192,1536]{1,0:T(8,128)(2,1)S(1)} %constant_dynamic-update-slice_fusion.refs_0_), channel_id=1, source_target_pairs={{0,2},{1,3},{2,0},{3,1},{4,6},{5,7},{6,4},{7,5},{8,10},{9,11},{10,... | collective-permute-start | bytes 1769480 | tf_op jit(solution)/shard_map/ppermute | solution.py:946
  41.6 20.5 %collective-permute-start.10 = (bf16[192,1536]{1,0:T(8,128)(2,1)S(1)}, bf16[192,1536]{1,0:T(8,128)(2,1)}, u32[]{:S(2)}, u32[]{:S(2)}) collective-permute-start(bf16[192,1536]{1,0:T(8,128)(2,1)S(1)} %constant_dynamic-update-slice_fusion.refs_0_), channel_id=1, source_target_pairs={{0,1},{1,0},{2,3},{3,2},{4,5},{5,4},{6,7},{7,6},{8,9},{9,8},{10,11... | collective-permute-start | bytes 1769480 | tf_op jit(solution)/shard_map/ppermute | solution.py:943
  41.6 20.4 %collective-permute-start.12 = (bf16[192,1536]{1,0:T(8,128)(2,1)}, bf16[192,1536]{1,0:T(8,128)(2,1)}, u32[]{:S(2)}, u32[]{:S(2)}) collective-permute-start(bf16[192,1536]{1,0:T(8,128)(2,1)} %get-tuple-element.324.refs_4_), channel_id=1, source_target_pairs={{0,2},{1,3},{2,0},{3,1},{4,6},{5,7},{6,4},{7,5},{8,10},{9,11},{10,... | collective-permute-start | bytes 1769480 | tf_op jit(solution)/shard_map/ppermute | solution.py:946
  65.6 23.0 %collective-permute-start.17 = (bf16[192,1536]{1,0:T(8,128)(2,1)}, bf16[192,1536]{1,0:T(8,128)(2,1)}, u32[]{:S(2)}, u32[]{:S(2)}) collective-permute-start(bf16[192,1536]{1,0:T(8,128)(2,1)} %get-tuple-element.323.refs_8_), channel_id=1, source_target_pairs={{0,2},{1,3},{2,0},{3,1},{4,6},{5,7},{6,4},{7,5},{8,10},{9,11},{10,... | collective-permute-start | bytes 1769480 | tf_op jit(solution)/shard_map/ppermute | solution.py:946
  78.5 232.6 %reduce-scatter.2.cloned.1.call-start = ((), (), s32[]{:S(2)}) async-start(), calls=%async_computation.1 | async-start | bytes 5971968 | tf_op jit(solution)/shard_map/reduce_scatter | solution.py:1172
  95.0 45.6 %collective-permute-start.20 = (bf16[768,768]{1,0:T(8,128)(2,1)S(1)}, bf16[768,768]{1,0:T(8,128)(2,1)}, u32[]{:S(2)}, u32[]{:S(2)}) collective-permute-start(bf16[768,768]{1,0:T(8,128)(2,1)S(1)} %copy-done.41), channel_id=1, source_target_pairs={{0,2},{1,3},{2,0},{3,1},{4,6},{5,7},{6,4},{7,5},{8,10},{9,11},{10,... | collective-permute-start | bytes 3538952 | tf_op jit(solution)/shard_map/ppermute | solution.py:1146
  95.6 49.8 %collective-permute-start.21 = (bf16[768,768]{1,0:T(8,128)(2,1)S(1)}, bf16[768,768]{1,0:T(8,128)(2,1)}, u32[]{:S(2)}, u32[]{:S(2)}) collective-permute-start(bf16[768,768]{1,0:T(8,128)(2,1)S(1)} %copy-done.41), channel_id=1, source_target_pairs={{0,1},{1,0},{2,3},{3,2},{4,5},{5,4},{6,7},{7,6},{8,9},{9,8},{10,11... | collective-permute-start | bytes 3538952 | tf_op jit(solution)/shard_map/ppermute | solution.py:1147
  194.2 84.7 %collective-permute-start.26 = (bf16[192,768]{1,0:T(8,128)(2,1)S(1)}, bf16[192,768]{1,0:T(8,128)(2,1)S(1)}, u32[]{:S(2)}, u32[]{:S(2)}) collective-permute-start(bf16[192,768]{1,0:T(8,128)(2,1)S(1)} %collective-permute-done.24), channel_id=1, source_target_pairs={{0,8},{8,16},{16,24},{24,28},{28,20},{20,12},{12,4},{4,0},{1,9},{9... | collective-permute-start | bytes 884744 | tf_op jit(solution)/shard_map/ppermute | solution.py:924
  195.8 83.0 %collective-permute-start.27 = (bf16[192,768]{1,0:T(8,128)(2,1)S(1)}, bf16[192,768]{1,0:T(8,128)(2,1)S(1)}, u32[]{:S(2)}, u32[]{:S(2)}) collective-permute-start(bf16[192,768]{1,0:T(8,128)(2,1)S(1)} %collective-permute-done.25), channel_id=1, source_target_pairs={{0,4},{8,0},{16,8},{24,16},{28,24},{20,28},{12,20},{4,12},{1,5},{9... | collective-permute-start | bytes 884744 | tf_op jit(solution)/shard_map/ppermute | solution.py:924
  278.9 20.5 %collective-permute-start.28 = (bf16[192,768]{1,0:T(8,128)(2,1)S(1)}, bf16[192,768]{1,0:T(8,128)(2,1)S(1)}, u32[]{:S(2)}, u32[]{:S(2)}) collective-permute-start(bf16[192,768]{1,0:T(8,128)(2,1)S(1)} %collective-permute-done.26), channel_id=1, source_target_pairs={{0,8},{8,16},{16,24},{24,28},{28,20},{20,12},{12,4},{4,0},{1,9},{9... | collective-permute-start | bytes 884744 | tf_op jit(solution)/shard_map/ppermute | solution.py:924
  280.9 22.0 %collective-permute-start.29 = (bf16[192,768]{1,0:T(8,128)(2,1)S(1)}, bf16[192,768]{1,0:T(8,128)(2,1)S(1)}, u32[]{:S(2)}, u32[]{:S(2)}) collective-permute-start(bf16[192,768]{1,0:T(8,128)(2,1)S(1)} %collective-permute-done.27), channel_id=1, source_target_pairs={{0,4},{8,0},{16,8},{24,16},{28,24},{20,28},{12,20},{4,12},{1,5},{9... | collective-permute-start | bytes 884744 | tf_op jit(solution)/shard_map/ppermute | solution.py:924
  319.0 32.0 %collective-permute-start.40 = (bf16[640,768]{1,0:T(8,128)(2,1)S(1)}, bf16[640,768]{1,0:T(8,128)(2,1)}, u32[]{:S(2)}, u32[]{:S(2)}) collective-permute-start(bf16[640,768]{1,0:T(8,128)(2,1)S(1)} %fusion.8), channel_id=1, source_target_pairs={{0,2},{1,3},{2,0},{3,1},{4,6},{5,7},{6,4},{7,5},{8,10},{9,11},{10,... | collective-permute-start | bytes 2949128 | tf_op jit(solution)/shard_map/ppermute | solution.py:1202
  329.5 21.5 %collective-permute-start.36 = (bf16[384,768]{1,0:T(8,128)(2,1)}, bf16[384,768]{1,0:T(8,128)(2,1)}, u32[]{:S(2)}, u32[]{:S(2)}) collective-permute-start(bf16[384,768]{1,0:T(8,128)(2,1)} %get-tuple-element.322), channel_id=1, source_target_pairs={{0,8},{8,16},{16,24},{24,28},{28,20},{20,12},{12,4},{4,0},{1,9},{9... | collective-permute-start | bytes 1769480 | tf_op jit(solution)/shard_map/ppermute | solution.py:924
  330.6 20.4 %collective-permute-start.37 = (bf16[384,768]{1,0:T(8,128)(2,1)}, bf16[384,768]{1,0:T(8,128)(2,1)}, u32[]{:S(2)}, u32[]{:S(2)}) collective-permute-start(bf16[384,768]{1,0:T(8,128)(2,1)} %get-tuple-element.321), channel_id=1, source_target_pairs={{0,4},{8,0},{16,8},{24,16},{28,24},{20,28},{12,20},{4,12},{1,5},{9... | collective-permute-start | bytes 1769480 | tf_op jit(solution)/shard_map/ppermute | solution.py:924
  332.6 18.0 %collective-permute-start.38 = (bf16[216,768]{1,0:T(8,128)(2,1)S(1)}, bf16[216,768]{1,0:T(8,128)(2,1)}, u32[]{:S(2)}, u32[]{:S(2)}) collective-permute-start(bf16[216,768]{1,0:T(8,128)(2,1)S(1)} %add_convert_fusion.2.refs_0_), channel_id=1, source_target_pairs={{0,8},{8,16},{16,24},{24,28},{28,20},{20,12},{12,4},{4,0},{1,9},{9... | collective-permute-start | bytes 995336 | tf_op jit(solution)/shard_map/ppermute | solution.py:924
  355.5 30.6 %collective-permute-start.41 = (bf16[384,768]{1,0:T(8,128)(2,1)}, bf16[384,768]{1,0:T(8,128)(2,1)S(1)}, u32[]{:S(2)}, u32[]{:S(2)}) collective-permute-start(bf16[384,768]{1,0:T(8,128)(2,1)} %get-tuple-element.320), channel_id=1, source_target_pairs={{0,8},{8,16},{16,24},{24,28},{28,20},{20,12},{12,4},{4,0},{1,9},{9... | collective-permute-start | bytes 1769480 | tf_op jit(solution)/shard_map/ppermute | solution.py:924
  356.8 29.2 %collective-permute-start.42 = (bf16[384,768]{1,0:T(8,128)(2,1)}, bf16[384,768]{1,0:T(8,128)(2,1)S(1)}, u32[]{:S(2)}, u32[]{:S(2)}) collective-permute-start(bf16[384,768]{1,0:T(8,128)(2,1)} %get-tuple-element.319), channel_id=1, source_target_pairs={{0,4},{8,0},{16,8},{24,16},{28,24},{20,28},{12,20},{4,12},{1,5},{9... | collective-permute-start | bytes 1769480 | tf_op jit(solution)/shard_map/ppermute | solution.py:924
  367.0 19.0 %collective-permute-start.45 = (bf16[216,768]{1,0:T(8,128)(2,1)}, bf16[216,768]{1,0:T(8,128)(2,1)}, u32[]{:S(2)}, u32[]{:S(2)}) collective-permute-start(bf16[216,768]{1,0:T(8,128)(2,1)} %collective-permute-done.38.refs_7_), channel_id=1, source_target_pairs={{0,8},{8,16},{16,24},{24,28},{28,20},{20,12},{12,4},{4,0},{1,9},{9... | collective-permute-start | bytes 995336 | tf_op jit(solution)/shard_map/ppermute | solution.py:924
  392.2 28.0 %collective-permute-start.49 = (bf16[384,768]{1,0:T(8,128)(2,1)}, bf16[384,768]{1,0:T(8,128)(2,1)}, u32[]{:S(2)}, u32[]{:S(2)}) collective-permute-start(bf16[384,768]{1,0:T(8,128)(2,1)} %get-tuple-element.318), channel_id=1, source_target_pairs={{0,8},{8,16},{16,24},{24,28},{28,20},{20,12},{12,4},{4,0},{1,9},{9... | collective-permute-start | bytes 1769480 | tf_op jit(solution)/shard_map/ppermute | solution.py:924
  393.3 27.0 %collective-permute-start.50 = (bf16[384,768]{1,0:T(8,128)(2,1)S(1)}, bf16[384,768]{1,0:T(8,128)(2,1)}, u32[]{:S(2)}, u32[]{:S(2)}) collective-permute-start(bf16[384,768]{1,0:T(8,128)(2,1)S(1)} %get-tuple-element.317), channel_id=1, source_target_pairs={{0,4},{8,0},{16,8},{24,16},{28,24},{20,28},{12,20},{4,12},{1,5},{9... | collective-permute-start | bytes 1769480 | tf_op jit(solution)/shard_map/ppermute | solution.py:924
  401.0 19.2 %collective-permute-start.53 = (bf16[216,768]{1,0:T(8,128)(2,1)}, bf16[216,768]{1,0:T(8,128)(2,1)S(1)}, u32[]{:S(2)}, u32[]{:S(2)}) collective-permute-start(bf16[216,768]{1,0:T(8,128)(2,1)} %collective-permute-done.45.refs_6_), channel_id=1, source_target_pairs={{0,8},{8,16},{16,24},{24,28},{28,20},{20,12},{12,4},{4,0},{1,9},{9... | collective-permute-start | bytes 995336 | tf_op jit(solution)/shard_map/ppermute | solution.py:924
  402.0 18.2 %collective-permute-start.54 = (bf16[216,768]{1,0:T(8,128)(2,1)}, bf16[216,768]{1,0:T(8,128)(2,1)S(1)}, u32[]{:S(2)}, u32[]{:S(2)}) collective-permute-start(bf16[216,768]{1,0:T(8,128)(2,1)} %collective-permute-done.46.refs_2_), channel_id=1, source_target_pairs={{0,4},{8,0},{16,8},{24,16},{28,24},{20,28},{12,20},{4,12},{1,5},{9... | collective-permute-start | bytes 995336 | tf_op jit(solution)/shard_map/ppermute | solution.py:924
  (90 other events, 1150.0 us)
Sparse Core Ops, SparseCore 0:
  78.6 50.4 all-gather.2
  192.7 112.3 reduce-scatter.1

commit v4 on v3

--- a/solution.py
+++ b/solution.py
@@ -54,10 +54,10 @@
 
 def project_kernel(batch, shares, sc, *refs):
     pieces, (gain_ref, *weights) = refs[:batch], refs[batch : batch + 1 + max(1, len(shares))]
-    outs = refs[-(7 if shares else 6) :]
-    k_ref, v_ref, kt_ref, vt_ref, nt_ref, x_out = outs[:6]
+    outs = refs[-(4 if shares else 3) :]
+    k_ref, v_ref, x_out = outs[:3]
     width = x_out.shape[2]
-    mat = outs[6] if shares else weights[0]
+    mat = outs[3] if shares else weights[0]
     if shares:
 
         @pl.when(pl.program_id(0) == 0)
@@ -68,13 +68,8 @@
         x_low = x_ref[...]
         x_out[0] = x_low
         normed = rms_norm(x_low.astype(F32), gain_ref[...]).astype(BF16)
-        nt_ref[0] = normed.T
-        k = dot(normed, mat[:, :width]).astype(BF16)
-        k_ref[0] = k
-        kt_ref[0] = k.T
-        v = dot(normed, mat[:, width:]).astype(BF16)
-        v_ref[0] = v
-        vt_ref[0] = v.T
+        k_ref[0] = dot(normed, mat[:, :width]).astype(BF16)
+        v_ref[0] = dot(normed, mat[:, width:]).astype(BF16)
 
     for n in range(batch):
         pl.when(pl.program_id(0) == n)(functools.partial(one, pieces[n]))
@@ -86,20 +81,12 @@
     place = lambda j, sc: (sc[HEAD + 2 * count + first + j], 0, 0)
     fixed = lambda j, sc: (0, 0)
     tall = jax.ShapeDtypeStruct((count, rows, width), BF16)
-    wide = jax.ShapeDtypeStruct((count, width, rows), BF16)
     once = pl.Buffered(1)
     before = () if before is None else tuple(before)
     shares = tuple(mat) if isinstance(mat, (list, tuple)) else ()
     weights = shares or (mat,)
-    out_specs = [
-        pl.BlockSpec((1, rows, width), place),
-        pl.BlockSpec((1, rows, width), place),
-        pl.BlockSpec((1, width, rows), place),
-        pl.BlockSpec((1, width, rows), place),
-        pl.BlockSpec((1, width, rows), place),
-        pl.BlockSpec((1, rows, width), place),
-    ]
-    out_shape = [tall, tall, wide, wide, wide, tall]
+    out_specs = [pl.BlockSpec((1, rows, width), place)] * 3
+    out_shape = [tall] * 3
     if shares:
         out_specs.append(pl.BlockSpec((width, 2 * width), fixed, pipeline_mode=once))
         out_shape.append(jax.ShapeDtypeStruct((width, 2 * width), BF16))
@@ -116,7 +103,7 @@
         ),
         out_shape=out_shape,
         input_output_aliases={batch + 2 + len(weights) + n: n for n in range(len(before))},
-        **params(4 * batch * rows * width * width, 14 * batch * rows * width),
+        **params(4 * batch * rows * width * width, 8 * batch * rows * width),
     )(scalars, *pieces, gain, *weights, *before)
 
 
@@ -198,8 +185,8 @@
 
 
 def attend_kernel(
-    count, heads, group, sc, q_ref, k_ref, vt_ref, mix_ref, spread_ref,
-    att_ref, t_ref, lse_ref, folded, total, top, norm, bias_s, mixed_s, ahead,
+    count, heads, group, sc, q_ref, k_ref, v_ref, mix_ref, spread_ref,
+    att_ref, t_ref, lse_ref, folded, total, top, norm, bias_s, mixed_s, ahead, vt_s,
 ):
     half, width = q_ref.shape[1], q_ref.shape[2]
     rows = k_ref.shape[1]
@@ -219,6 +206,7 @@
     set_bias(bias_s, sc, tile * rows, query_place)
     span = group * half
     chunks = [slice(c * span, (c + 1) * span) for c in range(heads // group)]
+    vt_s[...] = v_ref[0].T
     ahead[0] = dot_nt(k_ref[0], folded[chunks[0], :])
     for c, cols in enumerate(chunks):
         if c + 1 < len(chunks):
@@ -230,7 +218,7 @@
         weights = jnp.exp2(logits - after)
         top[:, cols] = after
         norm[:, cols] = norm[:, cols] * shrink + jnp.sum(weights, axis=0, keepdims=True)
-        total[:, cols] = total[:, cols] * shrink + dot(vt_ref[0], weights.astype(BF16))
+        total[:, cols] = total[:, cols] * shrink + dot(vt_s[...], weights.astype(BF16))
 
     @pl.when((step == own) | (step == count))
     def finish():
@@ -261,7 +249,7 @@
         mixed_s[rows, :] = found
 
 
-def attend(scalars, q, k, vt, mix_rows, spread, heads):
+def attend(scalars, q, k, v, mix_rows, spread, heads):
     count, rows, width = k.shape
     half = q.shape[1]
     span = heads * half
@@ -277,7 +265,7 @@
             in_specs=[
                 pl.BlockSpec((1, half, width), which),
                 pl.BlockSpec((1, rows, width), tile),
-                pl.BlockSpec((1, width, rows), tile),
+                pl.BlockSpec((1, rows, width), tile),
                 pl.BlockSpec((heads, width), fixed),
                 pl.BlockSpec((heads, span), fixed),
             ],
@@ -294,6 +282,7 @@
                 pltpu.VMEM((rows, 2 * half), F32),
                 pltpu.VMEM((width, 2 * half), F32),
                 pltpu.VMEM((2, rows, group * half), F32),
+                pltpu.VMEM((width, rows), BF16),
             ],
         ),
         out_shape=[
@@ -302,7 +291,7 @@
             jax.ShapeDtypeStruct((2, 1, span), F32),
         ],
         **params(4 * (count + 1) * rows * span * width, 6 * count * rows * width),
-    )(scalars, q, k, vt, mix_rows, spread)
+    )(scalars, q, k, v, mix_rows, spread)
 
 
 def pair_rows(left, right, heads):
@@ -378,9 +367,9 @@
 
 
 def back_kernel(
-    count, heads, base, group, scale, sc, q_ref, ga_ref, k_ref, v_ref, kt_ref, lse_ref, delta_ref,
+    count, heads, base, group, scale, sc, q_ref, ga_ref, k_ref, v_ref, lse_ref, delta_ref,
     mix_ref, weight_ref, spread_ref, dk_ref, dv_ref, dq_ref, r_ref,
-    fq, fa, total, dk_s, dv_s, bias_s, mixed_s, twice_s, rows_s, ahead_l, ahead_p,
+    fq, fa, total, dk_s, dv_s, bias_s, kt_s, mixed_s, twice_s, rows_s, ahead_l, ahead_p,
 ):
     half, width = q_ref.shape[1], q_ref.shape[2]
     rows = k_ref.shape[1]
@@ -413,6 +402,7 @@
         ahead_l[c % 2] = dot_nt(k_ref[0], fq[part, chunks[c], :])
         ahead_p[c % 2] = dot_nt(v_ref[0], fa[part, chunks[c], :])
 
+    kt_s[...] = k_ref[0].T
     look(0)
     for c, cols in enumerate(chunks):
         if c + 1 < len(chunks):
@@ -422,7 +412,7 @@
         grad_logits = (prob * (ahead_p[c % 2] - delta_ref[part, :, cols])).astype(BF16)
         dv_s[...] += dot(prob.astype(BF16), fa[part, cols, :])
         dk_s[...] += dot(grad_logits, fq[part, cols, :])
-        total[part, :, cols] += dot(kt_ref[0], grad_logits)
+        total[part, :, cols] += dot(kt_s[...], grad_logits)
 
     @pl.when(jnp.logical_not(both) | (part == 1))
     def leave():
@@ -449,7 +439,7 @@
 
 
 def back(
-    scalars, base, group, q, grad_att, k, v, kt, lse, delta, mix_rows, weight_rows, spread, heads, scale
+    scalars, base, group, q, grad_att, k, v, lse, delta, mix_rows, weight_rows, spread, heads, scale
 ):
     count, rows, width = k.shape
     half = q.shape[1]
@@ -469,7 +459,6 @@
                 pl.BlockSpec((2, half, width), whole, pipeline_mode=once),
                 pl.BlockSpec((1, rows, width), tile),
                 pl.BlockSpec((1, rows, width), tile),
-                pl.BlockSpec((1, width, rows), tile),
                 pl.BlockSpec((2, 1, span), cut, pipeline_mode=once),
                 pl.BlockSpec((2, 1, span), cut, pipeline_mode=once),
                 pl.BlockSpec((heads, width), fixed),
@@ -489,6 +478,7 @@
                 pltpu.VMEM((rows, width), F32),
                 pltpu.VMEM((rows, width), F32),
                 pltpu.VMEM((rows, 2 * half), F32),
+                pltpu.VMEM((width, rows), BF16),
                 pltpu.VMEM((width, 2 * half), F32),
                 pltpu.VMEM((width, 2 * half), F32),
                 pltpu.VMEM((heads, span), F32),
@@ -503,7 +493,7 @@
             jax.ShapeDtypeStruct((heads, 128), F32),
         ],
         **params(10 * (count + 1) * rows * span * width, 10 * count * rows * width),
-    )(scalars, q, grad_att, k, v, kt, lse, delta, mix_rows, weight_rows, spread)
+    )(scalars, q, grad_att, k, v, lse, delta, mix_rows, weight_rows, spread)
 
 
 def put(keep_ref, send_ref, place, rows, value):
@@ -528,35 +518,94 @@
 
 def ffn_kernel(wt_count, sc, att_ref, x_ref, dy_ref, gain_ref, *refs):
     n = wt_count
-    halves = (len(refs) - 15) // n - 2
+    halves = (len(refs) - 21) // n - 2
+    chunks = 2 * halves
     groups = [refs[i * n : (i + 1) * n] for i in range(halves + 2)]
     wo_shares, win_shares, wout_shares = groups[0], groups[1:-1], groups[-1]
     (
         out_ref, gm_ref, gatt_ref, keep_ref, send_ref, gain_out, sq_ref,
-        middle_s, low_s, low_t, feed_s, grad_s, wo_ref, win_ref, wout_ref,
+        middle_s, low_s, low_t, feed_s, grad_s, wo_ref, win_buf, wout_buf, leave_out, leave_in, leave_o,
+        wo_sem, in_sem, out_sem,
     ) = refs[(halves + 2) * n :]
     j = pl.program_id(0)
-    last = pl.num_programs(0) - 1
     me = sc[5]
     width = x_ref.shape[1]
-    per = width // wt_count
-    for i in range(halves):
-        for side in range(2):
-            pl.when(j == 2 * i + side)(
-                functools.partial(
-                    assemble, me, win_ref, win_shares[i], per, slice(side * width, (side + 1) * width)
-                )
+    per = width // n
+    slot = j % 2
+
+    def share_rows(i):
+        return pl.ds(pl.multiple_of((me ^ i) * per, per), per)
+
+    def wo_copies():
+        return [
+            pltpu.make_async_copy(
+                wo_shares[i].at[:, pl.ds(width, width)], wo_ref.at[share_rows(i), :], wo_sem.at[i]
             )
-
-    def take(share):
-        wout_ref[...] = share[...]
-
-    for i, share in enumerate(wout_shares):
-        pl.when((j ^ me) == i)(functools.partial(take, share))
+            for i in range(n)
+        ]
+
+    def in_copies(c):
+        return [
+            pltpu.make_async_copy(
+                win_shares[c // 2][i].at[:, pl.ds(c % 2 * width, width)],
+                win_buf.at[c % 2, share_rows(i), :],
+                in_sem.at[c % 2, i],
+            )
+            for i in range(n)
+        ]
+
+    def outer_copy(c, i):
+        return pltpu.make_async_copy(wout_shares[i], wout_buf.at[c % 2], in_sem.at[c % 2, n])
+
+    def fetch(c):
+        for copy in in_copies(c):
+            copy.start()
+        for i in range(n):
+            pl.when((c ^ me) == i)(outer_copy(c, i).start)
+
+    def arrive(c):
+        for copy in in_copies(c):
+            copy.wait()
+        outer_copy(c, 0).wait()
+
+    def leaving(source, place, first, sem):
+        target = (keep_ref, send_ref)[place % 2]
+        rows = pl.ds(first, source.shape[0])
+        return pltpu.make_async_copy(source, target.at[rows, pl.ds(place // 2 * width, width)], sem)
+
+    def depart(source, target, first, sem):
+        for place in range(n):
+            pl.when((target ^ me) == place)(leaving(source, place, first, sem).start)
+
+    def outgoing(c):
+        yield leave_out.at[c % 2], c, 0, out_sem.at[c % 2, n]
+        for t in range(n):
+            yield leave_in.at[c % 2, pl.ds(t * per, per), :], t, width + c * per, out_sem.at[c % 2, t]
+
+    def gone(c):
+        for source, _, first, sem in outgoing(c):
+            leaving(source, 0, first, sem).wait()
 
     @pl.when(j == 0)
     def start():
-        assemble(me, wo_ref, wo_shares, per, slice(width, 2 * width))
+        for copy in wo_copies():
+            copy.start()
+        fetch(0)
+        for copy in wo_copies():
+            copy.wait()
+
+    for c in range(chunks):
+
+        @pl.when(j == c)
+        def move():
+            if c + 1 < chunks:
+                fetch(c + 1)
+            if c >= 2:
+                gone(c - 2)
+            arrive(c)
+
+    @pl.when(j == 0)
+    def first():
         branch = dot(att_ref[...], wo_ref[...])
         middle = x_ref[...].astype(F32) + branch
         middle_s[...] = middle
@@ -570,8 +619,9 @@
         sq_ref[1:2, :] = jnp.broadcast_to(jnp.sum(branch * branch).reshape(1, 1), (1, 128))
 
     dy = dy_ref[...]
-    hidden = dot(low_s[...], win_ref[...])
-    grad_active = dot_nt(dy, wout_ref[...])
+    win, wout = win_buf[slot], wout_buf[slot]
+    hidden = dot(low_s[...], win)
+    grad_active = dot_nt(dy, wout)
     square = hidden * hidden
     inner = jnp.tanh(hidden * (0.7978845608028654 + 0.7978845608028654 * 0.044715 * square))
     half_one = 0.5 + 0.5 * inner
@@ -580,16 +630,19 @@
         0.7978845608028654 + 3.0 * 0.7978845608028654 * 0.044715 * square
     )
     grad_hidden = (grad_active * slope).astype(BF16)
-    feed_s[...] += dot(active, wout_ref[...])
-    grad_s[...] += dot_nt(grad_hidden, win_ref[...])
-    grad_out = dot(active.T, dy).astype(BF16)
-    grad_in = dot(low_t[...], grad_hidden).astype(BF16)
-    put(keep_ref, send_ref, j ^ me, slice(0, width), grad_out)
-    for t in range(wt_count):
-        rows = pl.ds(pl.multiple_of(width + j * per, per), per)
-        put(keep_ref, send_ref, t ^ me, rows, grad_in[t * per : (t + 1) * per, :])
-
-    @pl.when(j == last)
+    feed_s[...] += dot(active, wout)
+    grad_s[...] += dot_nt(grad_hidden, win)
+    leave_out[slot] = dot(active.T, dy).astype(BF16)
+    leave_in[slot] = dot(low_t[...], grad_hidden).astype(BF16)
+
+    for c in range(chunks):
+
+        @pl.when(j == c)
+        def part():
+            for copy in outgoing(c):
+                depart(*copy)
+
+    @pl.when(j == chunks - 1)
     def finish():
         middle = middle_s[...]
         feed = feed_s[...]
@@ -603,14 +656,15 @@
         grad_middle = dy.astype(F32) + norm_back(inverse, bare, grad, gain_ref[...])
         gm_ref[...] = grad_middle
         low = grad_middle.astype(BF16)
+        leave_o[...] = dot(att_ref[...].T, low).astype(BF16)
+        rows = width + per * chunks
+        for t in range(n):
+            depart(leave_o.at[pl.ds(t * per, per), :], t, rows, wo_sem.at[t])
         gatt_ref[...] = dot_nt(low, wo_ref[...]).astype(BF16)
-        grad_o = dot(att_ref[...].T, low).astype(BF16)
-        for t in range(wt_count):
-            put(
-                keep_ref, send_ref, t ^ me,
-                slice(keep_ref.shape[1] - per, keep_ref.shape[1]),
-                grad_o[t * per : (t + 1) * per, :],
-            )
+        for c in range(max(chunks - 2, 0), chunks):
+            gone(c)
+        for t in range(n):
+            leaving(leave_o.at[pl.ds(t * per, per), :], 0, rows, wo_sem.at[t]).wait()
 
 
 def ffn(scalars, wt_count, sq_rows, att, x, dy, gain, wo, wins, wout):
@@ -619,12 +673,13 @@
     per = width // wt_count
     total = width + per * chunks + per
     fixed = lambda j, sc: (0, 0)
-    whole = lambda j, sc: (0, 0, 0)
     once = pl.Buffered(1)
-    kernel = functools.partial(ffn_kernel, wt_count)
     shares = [*wo, *(share for win in wins for share in win), *wout]
+    anywhere = pl.BlockSpec(memory_space=pl.ANY)
+    square = pltpu.VMEM((width, width), BF16)
+    squares = pltpu.VMEM((2, width, width), BF16)
     return pl.pallas_call(
-        kernel,
+        functools.partial(ffn_kernel, wt_count),
         grid_spec=pltpu.PrefetchScalarGridSpec(
             num_scalar_prefetch=1,
             grid=(chunks,),
@@ -634,13 +689,13 @@
                 pl.BlockSpec((rows, width), fixed, pipeline_mode=once),
                 pl.BlockSpec((1, width), fixed),
             ]
-            + [pl.BlockSpec(w.shape, fixed, pipeline_mode=once) for w in shares],
+            + [anywhere] * len(shares),
             out_specs=[
                 pl.BlockSpec((rows, width), fixed),
                 pl.BlockSpec((rows, width), fixed),
                 pl.BlockSpec((rows, width), fixed),
-                pl.BlockSpec((wt_count // 2, total, width), whole),
-                pl.BlockSpec((wt_count // 2, total, width), whole),
+                anywhere,
+                anywhere,
                 pl.BlockSpec((1, width), fixed),
                 pl.BlockSpec((sq_rows, 128), fixed),
             ],
@@ -650,17 +705,23 @@
                 pltpu.VMEM((width, rows), BF16),
                 pltpu.VMEM((rows, width), F32),
                 pltpu.VMEM((rows, width), F32),
-                pltpu.VMEM((width, width), BF16),
-                pltpu.VMEM((width, width), BF16),
-                pltpu.VMEM((width, width), BF16),
+                square,
+                squares,
+                squares,
+                squares,
+                squares,
+                square,
+                pltpu.SemaphoreType.DMA((wt_count,)),
+                pltpu.SemaphoreType.DMA((2, wt_count + 1)),
+                pltpu.SemaphoreType.DMA((2, wt_count + 1)),
             ],
         ),
         out_shape=[
             jax.ShapeDtypeStruct((rows, width), BF16),
             jax.ShapeDtypeStruct((rows, width), F32),
             jax.ShapeDtypeStruct((rows, width), BF16),
-            jax.ShapeDtypeStruct((wt_count // 2, total, width), BF16),
-            jax.ShapeDtypeStruct((wt_count // 2, total, width), BF16),
+            jax.ShapeDtypeStruct((total, wt_count // 2 * width), BF16),
+            jax.ShapeDtypeStruct((total, wt_count // 2 * width), BF16),
             jax.ShapeDtypeStruct((1, width), F32),
             jax.ShapeDtypeStruct((sq_rows, 128), F32),
         ],
@@ -676,10 +737,10 @@
 
 
 def weight_kernel(
-    count, wt_count, sc, dk_ref, dv_ref, dq_ref, nt_ref, rl_ref, rw_ref, gain_two_ref, sq_ref,
-    keep_ref, send_ref, dwq, dwk, dwv,
+    count, wt_count, sc, dk_ref, dv_ref, dq_ref, x_ref, gain_ref, rl_ref, rw_ref, gain_two_ref, sq_ref,
+    keep_ref, send_ref, dwq, dwk, dwv, normed_t,
 ):
-    width, rows = nt_ref.shape[1:]
+    rows, width = x_ref.shape[1:]
     half = rows // 2
     device = pl.program_id(0)
     me_wt = sc[5]
@@ -692,13 +753,14 @@
 
     @pl.when(seen_by(sc, count, device))
     def seen():
-        dwk[...] += dot(nt_ref[0], dk_ref[0])
-        dwv[...] += dot(nt_ref[0], dv_ref[0])
+        normed_t[...] = rms_norm(x_ref[0].astype(F32), gain_ref[...]).astype(BF16).T
+        dwk[...] += dot(normed_t[...], dk_ref[0])
+        dwv[...] += dot(normed_t[...], dv_ref[0])
 
     def queries(n):
         empty = jnp.zeros((half, width), BF16)
         both = [dq_ref[n], empty] if n == 0 else [empty, dq_ref[n]]
-        dwq[...] += dot(nt_ref[0], jnp.concatenate(both, axis=0))
+        dwq[...] += dot(normed_t[...], jnp.concatenate(both, axis=0))
 
     pl.when(device == sc[1])(functools.partial(queries, 0))
     pl.when(device == sc[2])(functools.partial(queries, 1))
@@ -734,7 +796,7 @@
             put(keep_ref, send_ref, t ^ me_wt, slice(3 * per, keep_ref.shape[1]), tail(t))
 
 
-def weight_grads(scalars, wt_count, total, dk, dv, dq, nt, rl, rw, gain_two, sq):
+def weight_grads(scalars, wt_count, total, dk, dv, dq, xg, gain, rl, rw, gain_two, sq):
     count, rows, width = dk.shape
     place = lambda j, sc: (j, 0, 0)
     fixed = lambda j, sc: (0, 0)
@@ -750,7 +812,8 @@
                 pl.BlockSpec((1, rows, width), place),
                 pl.BlockSpec((1, rows, width), place),
                 pl.BlockSpec((2, rows // 2, width), whole, pipeline_mode=once),
-                pl.BlockSpec((1, width, rows), place),
+                pl.BlockSpec((1, rows, width), place),
+                pl.BlockSpec((1, width), fixed),
                 pl.BlockSpec(rl.shape, fixed),
                 pl.BlockSpec(rw.shape, fixed),
                 pl.BlockSpec((1, width), fixed),
@@ -760,11 +823,11 @@
                 pl.BlockSpec((wt_count // 2, total, width), whole),
                 pl.BlockSpec((wt_count // 2, total, width), whole),
             ],
-            scratch_shapes=[pltpu.VMEM((width, width), F32)] * 3,
+            scratch_shapes=[pltpu.VMEM((width, width), F32)] * 3 + [pltpu.VMEM((width, rows), BF16)],
         ),
         out_shape=[share, share],
         **params(4 * count * rows * width * width, 10 * count * rows * width),
-    )(scalars, dk, dv, dq, nt, rl, rw, gain_two, sq)
+    )(scalars, dk, dv, dq, xg, gain, rl, rw, gain_two, sq)
 
 
 def token_kernel(
@@ -1120,7 +1183,7 @@
             scalars, count, state["first"], batch, state["small"][0], state["mat"], state["found"]
         )
         state["first"] += len(batch)
-        return [*results, state["mat"]][:7]
+        return [*results, state["mat"]][:4]
 
     rounds, shares, crossed = gather_all(x_own, stages, work)
     gain_one, gain_two, logit_mix, weight_mix = state["small"]
@@ -1133,7 +1196,7 @@
     logit_spread = jnp.repeat(logit_mix, half, axis=1)
 
     batch = [piece for pieces in rounds[state["seen"] :] for _, piece in pieces]
-    k, v, kt, vt, nt, xg, kv_mat = project_batch(batch)
+    k, v, xg, kv_mat = project_batch(batch)
     xg, *crossed[len(shares) :] = tie(xg, *crossed[len(shares) :])
     q, x_low, query_mat = queries(scalars, xg, gain_one, qo_shares)
     x_low = x_low.reshape(rows, width)
@@ -1153,7 +1216,7 @@
     dy_second, _ = lax.optimization_barrier((cotangent[0, half:], rounds[-1][0][1]))
     dy_low = jnp.concatenate([cotangent[0, :half], exchange(dy_second)], axis=0)
 
-    attended, t, lse = attend(scalars, q, k, vt, mix_rows, spread, heads)
+    attended, t, lse = attend(scalars, q, k, v, mix_rows, spread, heads)
     far_out, attended = tie(far_out, attended)
     out_shares = [w_out, near_out, far_out, lax.ppermute(far_out, "wt", swaps(wt_count, 1))]
     out_low, grad_middle, grad_att, keep, send, grad_gain_two, squares = ffn(
@@ -1165,7 +1228,7 @@
 
     got = lax.ppermute(send, "wt", swaps(wt_count, 1))
     r_weight, delta = deltas(grad_att, t, spread, heads)
-    summed = add(keep, got).reshape(2, count, -1, width).transpose(1, 0, 2, 3).reshape(-1, width)
+    summed = add(keep, got)
     leaving = Spreading(out_low[half:], count)
     summed, delta, *moved = tie(summed, delta, *leaving.start())
     leaving.finish(*moved)
@@ -1173,7 +1236,7 @@
 
     moved = leaving.start()
     dk, dv, dq, r_logit = back(
-        scalars, 0, heads, q, grad_att, k, v, kt, lse, delta, mix_rows, weight_by_g,
+        scalars, 0, heads, q, grad_att, k, v, lse, delta, mix_rows, weight_by_g,
         logit_spread, heads, scale,
     )
 
@@ -1188,7 +1251,7 @@
     leaving.finish(*moved)
     moved = leaving.start()
     keep, send = weight_grads(
-        scalars, wt_count, total, dk, dv, dq, nt, r_logit, r_weight, grad_gain_two, squares
+        scalars, wt_count, total, dk, dv, dq, xg, gain_one, r_logit, r_weight, grad_gain_two, squares
     )
     send, dk, *moved = tie(send, dk, *moved)
     leaving.finish(*moved)
@@ -1196,14 +1259,13 @@
     far = parts(count - 1, 1, dk)
     near, far, summed, *moved = tie(near, far, summed, *leaving.start())
     leaving.finish(*moved)
-    summed = summed.reshape(2, -1, width)
-    ffn_far = lax.ppermute(summed[1], "wt", swaps(wt_count, 2))
+    ffn_far = lax.ppermute(summed[:, width:], "wt", swaps(wt_count, 2))
     up, down = far_start(far[0])
     over = lax.ppermute(add(keep[1], near[1]), "wt", swaps(wt_count, 2))
     pair = parts(2 * (last - 1) - 1, 2, dk)
     up, down, pair, ffn_far = tie(up, down, pair, ffn_far)
     up, down = far_end(up, down)
-    spread = Spreading(add(summed[0], ffn_far), count)
+    spread = Spreading(add(summed[:, :width], ffn_far), count)
 
     turn = None
     for k in range(last - 1, 0, -1):

time: 472 us -> 461 us (0.977)
  Pallas kernels: 254 us -> 246 us
  local copies, waits for them, and re-layouts: 25.7 us -> 20.8 us
    pallas_call x1, Pallas kernels: 29.7 us -> 24.2 us  [ffn(): pl.pallas_call(functools.partial(ffn_kernel, wt_count), grid_spec=pltpu.P...]
where the time goes in v4:
time: 461 us; the launch traced here: 455 us
  Pallas kernels  246 us (53%)
  waiting for transfers between devices  70.4 us (15%)
  starting transfers between devices  61.1 us (13%)
  other arithmetic  36.7 us (8%)
  local copies, waits for them, and re-layouts  20.8 us (5%)
  between operations  20 us (4%)
    pallas_call x1, Pallas kernels, back(): pl.pallas_call(functools.partial(back_kernel, count, heads, base, group,...  82.5 us
    pallas_call x1, Pallas kernels, attend(): pl.pallas_call(functools.partial(attend_kernel, count, heads, group), gri...  44.5 us
    ppermute x24, starting transfers between devices, ring_both(): lax.ppermute(up, 'ctx', ring(count, 1))  38.4 us
    ppermute x24, waiting for transfers between devices, ring_both(): lax.ppermute(up, 'ctx', ring(count, 1))  37.6 us
    pallas_call x5, Pallas kernels, token_parts(): pl.pallas_call(functools.partial(token_kernel, count, first), grid_spec=p...  33.5 us
    convert_element_type x11, other arithmetic, add(): return sum((v.astype(F32) for v in values)).astype(BF16)  25 us
    pallas_call x1, Pallas kernels, ffn(): pl.pallas_call(functools.partial(ffn_kernel, wt_count), grid_spec=pltpu.P...  24.2 us
    pallas_call x3, Pallas kernels, project(): pl.pallas_call(functools.partial(project_kernel, batch, shares), grid_spe...  23.1 us
  transfers between devices with their start and end apart: 69, of which 22 were waited for; matrix products, arithmetic and copies ran while one was open for 10% of the time, Pallas kernels for 48%

profile of v4, /device:TPU:0, one launch (start us, length us, event | category | flops | bytes accessed | tf_op | source)
XLA Modules:
  0.0 454.7 jit_solution(7172925103244772752)
XLA Ops:
  25.4 5.2 %collective-permute-done.2.refs_6_ = bf16[208,1536]{1,0:T(8,128)(2,1)} collective-permute-done((bf16[208,1536]{1,0:T(8,128)(2,1)S(1)}, bf16[208,1536]{1,0:T(8,128)(2,1)}, u32[]{:S(2)}, u32[]{:S(2)}) %collective-permute-start.2) | collective-permute-done | bytes 639008 | tf_op jit(solution)/shard_map/ppermute | solution.py:1009
  34.5 7.2 %collective-permute-done.7.refs_2_ = bf16[192,1536]{1,0:T(8,128)(2,1)S(1)} collective-permute-done((bf16[192,1536]{1,0:T(8,128)(2,1)S(1)}, bf16[192,1536]{1,0:T(8,128)(2,1)S(1)}, u32[]{:S(2)}, u32[]{:S(2)}) %collective-permute-start.7) | collective-permute-done | bytes 589856 | tf_op jit(solution)/shard_map/ppermute | solution.py:1009
  52.1 8.8 %shard_map.327 = (bf16[8,384,768]{2,1,0:T(8,128)(2,1)}, bf16[8,384,768]{2,1,0:T(8,128)(2,1)}, bf16[8,384,768]{2,1,0:T(8,128)(2,1)}, bf16[768,1536]{1,0:T(8,128)(2,1)}) custom-call(s32[30]{0:T(128)} %concatenate.55.sc, bf16[384,768]{1,0:T(8,128)(2,1)} %bitcast.109, bf16[384,768]{1,0:T(8,128)(2,1)} %collective-permute-done.refs_1_, ...), custom_call_target="tpu_custom_call" | custom-call | flops 2717908992 | bytes 7077888 | tf_op jit(solution)/shard_map/pallas_call | solution.py:93
  70.1 6.5 %shard_map.328 = (bf16[8,384,768]{2,1,0:T(8,128)(2,1)}, bf16[8,384,768]{2,1,0:T(8,128)(2,1)}, bf16[8,384,768]{2,1,0:T(8,128)(2,1)}) custom-call(s32[30]{0:T(128)} %concatenate.55.sc, bf16[384,768]{1,0:T(8,128)(2,1)} %collective-permute-done.3.refs_0_, ...), custom_call_target="tpu_custom_call", output_to_operand_aliasing={{0}: (5, {}), {1}: (6, {}), {2}: (7, {})} | custom-call | flops 1811939328 | bytes 4718592 | tf_op jit(solution)/shard_map/pallas_call | solution.py:93
  78.6 7.9 %shard_map.329 = (bf16[8,384,768]{2,1,0:T(8,128)(2,1)}, bf16[8,384,768]{2,1,0:T(8,128)(2,1)}, bf16[8,384,768]{2,1,0:T(8,128)(2,1)}) custom-call(s32[30]{0:T(128)} %concatenate.55.sc, bf16[384,768]{1,0:T(8,128)(2,1)} %copy-done.4, bf16[384,768]{1,0:T(8,128)(2,1)} %copy-done.5, ...), custom_call_target="tpu_custom_call", output_to_operand_aliasing={{0}: (6, {}), {1}: (7, {}), {2}: (8, {})} | custom-call | flops 2717908992 | bytes 7077888 | tf_op jit(solution)/shard_map/pallas_call | solution.py:93
  88.6 4.3 shard_map.330
  94.4 44.5 %shard_map.331 = (bf16[2,192,768]{2,1,0:T(8,128)(2,1)}, bf16[2,768,2304]{2,1,0:T(8,128)(2,1)}, f32[2,1,2304]{2,1,0:T(1,128)}) custom-call(s32[30]{0:T(128)} %concatenate.55.sc, bf16[2,192,768]{2,1,0:T(8,128)(2,1)} %get-tuple-element.185.q_ref, bf16[8,384,768]{2,1,0:T(8,128)(2,1)} %get-tuple-element.186.k_ref, bf16[8,384,768]{2,1,0:T(8,128)(2,1)} %get-tuple-element.187.v_ref, ...), custom_call_target="tpu_custom_call" | custom-call | flops 24461180928 | bytes 14155776 | tf_op jit(solution)/shard_map/pallas_call | solution.py:260
  143.9 24.2 %shard_map.332 = (bf16[384,768]{1,0:T(8,128)(2,1)}, f32[384,768]{1,0:T(8,128)}, bf16[384,768]{1,0:T(8,128)(2,1)}, bf16[1728,1536]{1,0:T(8,128)(2,1)}, bf16[1728,...) custom-call(s32[30]{0:T(128)} %concatenate.55.sc, bf16[384,768]{1,0:T(8,128)(2,1)} %bitcast.113, ...), custom_call_target="tpu_custom_call" | custom-call | flops 10418651136 | bytes 14155776 | tf_op jit(solution)/shard_map/pallas_call | solution.py:681
  172.1 5.2 %shard_map.333 = (f32[12,128]{1,0:T(8,128)}, f32[2,1,2304]{2,1,0:T(1,128)}) custom-call(bf16[2,192,768]{2,1,0:T(8,128)(2,1)} %bitcast.104, bf16[2,768,2304]{2,1,0:T(8,128)(2,1)} %get-tuple-element.201.t_ref, f32[12,2304]{1,0:T(8,128)} %reshape.112.spread_ref), custom_call_target="tpu_custom_call" | custom-call | flops 7077888 | bytes 7077888 | tf_op jit(solution)/shard_map/pallas_call | solution.py:341
  177.3 7.9 %add_convert_fusion = bf16[1728,1536]{1,0:T(8,128)(2,1)} fusion(bf16[1728,1536]{1,0:T(8,128)(2,1)} %collective-permute-done.23, bf16[1728,1536]{1,0:T(8,128)(2,1)} %get-tuple-element.198), kind=kLoop, calls=%fused_computation | loop fusion | flops 10616832 | bytes 15925248 | tf_op jit(solution)/shard_map/convert_element_type | solution.py:1025
  188.9 82.5 %shard_map.334 = (bf16[8,384,768]{2,1,0:T(8,128)(2,1)}, bf16[8,384,768]{2,1,0:T(8,128)(2,1)}, bf16[2,192,768]{2,1,0:T(8,128)(2,1)}, f32[12,128]{1,0:T(8,128)}) custom-call(s32[30]{0:T(128)} %concatenate.55.sc, bf16[2,192,768]{2,1,0:T(8,128)(2,1)} %get-tuple-element.185.q_ref, bf16[2,192,768]{2,1,0:T(8,128)(2,1)} %bitcast.105, ...), custom_call_target="tpu_custom_call" | custom-call | flops 61152952320 | bytes 23592960 | tf_op jit(solution)/shard_map/pallas_call | solution.py:452
  274.5 19.5 %shard_map.335 = (bf16[2,640,768]{2,1,0:T(8,128)(2,1)}, bf16[2,640,768]{2,1,0:T(8,128)(2,1)}) custom-call(s32[30]{0:T(128)} %concatenate.55.sc, bf16[8,384,768]{2,1,0:T(8,128)(2,1)} %get-tuple-element.220.dk_ref, bf16[8,384,768]{2,1,0:T(8,128)(2,1)} %get-tuple-element.210.dv_ref, bf16[2,192,768]{2,1,0:T(8,128)(2,1)} %get-tuple-element.211.dq_ref, ...), custom_call_target="tpu_custom_call" | custom-call | flops 7247757312 | bytes 23592960 | tf_op jit(solution)/shard_map/pallas_call | solution.py:806
  296.8 6.0 %shard_map.336 = bf16[1,384,768]{2,1,0:T(8,128)(2,1)} custom-call(s32[30]{0:T(128)} %concatenate.55.sc, bf16[8,384,768]{2,1,0:T(8,128)(2,1)} %get-tuple-element.220.dk_ref, bf16[8,384,768]{2,1,0:T(8,128)(2,1)} %get-tuple-element.210.dv_ref, bf16[2,192,768]{2,1,0:T(8,128)(2,1)} %get-tuple-element.211.dq_ref, bf16[8,384,768]{2,1,0:T(8,128)(2,1)} %get-tuple-element.178.x_ref, ...), custom_call_target="tpu_custom_call" | custom-call | flops 905969664 | bytes 2359296 | tf_op jit(solution)/shard_map/pallas_call | solution.py:868
  310.5 7.4 %shard_map.337 = bf16[2,384,768]{2,1,0:T(8,128)(2,1)} custom-call(s32[30]{0:T(128)} %concatenate.55.sc, bf16[8,384,768]{2,1,0:T(8,128)(2,1)} %get-tuple-element.220.dk_ref, bf16[8,384,768]{2,1,0:T(8,128)(2,1)} %get-tuple-element.210.dv_ref, bf16[2,192,768]{2,1,0:T(8,128)(2,1)} %get-tuple-element.211.dq_ref, bf16[8,384,768]{2,1,0:T(8,128)(2,1)} %get-tuple-element.178.x_ref, ...), custom_call_target="tpu_custom_call" | custom-call | flops 1811939328 | bytes 4718592 | tf_op jit(solution)/shard_map/pallas_call | solution.py:868
  325.9 7.3 %shard_map.338 = bf16[2,384,768]{2,1,0:T(8,128)(2,1)} custom-call(s32[30]{0:T(128)} %concatenate.55.sc, bf16[8,384,768]{2,1,0:T(8,128)(2,1)} %get-tuple-element.220.dk_ref, bf16[8,384,768]{2,1,0:T(8,128)(2,1)} %get-tuple-element.210.dv_ref, bf16[2,192,768]{2,1,0:T(8,128)(2,1)} %get-tuple-element.211.dq_ref, bf16[8,384,768]{2,1,0:T(8,128)(2,1)} %get-tuple-element.178.x_ref, ...), custom_call_target="tpu_custom_call" | custom-call | flops 1811939328 | bytes 4718592 | tf_op jit(solution)/shard_map/pallas_call | solution.py:868
  333.1 9.3 %collective-permute-done.38.refs_7_ = bf16[216,768]{1,0:T(8,128)(2,1)} collective-permute-done((bf16[216,768]{1,0:T(8,128)(2,1)S(1)}, bf16[216,768]{1,0:T(8,128)(2,1)}, u32[]{:S(2)}, u32[]{:S(2)}) %collective-permute-start.38) | collective-permute-done | bytes 331808 | tf_op jit(solution)/shard_map/ppermute | solution.py:987
  352.4 6.2 %shard_map.339 = bf16[2,384,768]{2,1,0:T(8,128)(2,1)} custom-call(s32[30]{0:T(128)} %concatenate.55.sc, bf16[8,384,768]{2,1,0:T(8,128)(2,1)} %get-tuple-element.220.dk_ref, bf16[8,384,768]{2,1,0:T(8,128)(2,1)} %get-tuple-element.210.dv_ref, bf16[2,192,768]{2,1,0:T(8,128)(2,1)} %get-tuple-element.211.dq_ref, bf16[8,384,768]{2,1,0:T(8,128)(2,1)} %get-tuple-element.178.x_ref, ...), custom_call_target="tpu_custom_call" | custom-call | flops 1811939328 | bytes 4718592 | tf_op jit(solution)/shard_map/pallas_call | solution.py:868
  360.9 5.2 %collective-permute-done.43 = bf16[40,768]{1,0:T(8,128)(2,1)S(1)} collective-permute-done((bf16[40,768]{1,0:T(8,128)(2,1)S(1)}, bf16[40,768]{1,0:T(8,128)(2,1)S(1)}, u32[]{:S(2)}, u32[]{:S(2)}) %collective-permute-start.43) | collective-permute-done | bytes 61472 | tf_op jit(solution)/shard_map/ppermute | solution.py:987
  368.8 3.6 collective-permute-done.47
  373.7 4.6 %collective-permute-done.48 = bf16[80,768]{1,0:T(8,128)(2,1)} collective-permute-done((bf16[80,768]{1,0:T(8,128)(2,1)}, bf16[80,768]{1,0:T(8,128)(2,1)}, u32[]{:S(2)}, u32[]{:S(2)}) %collective-permute-start.48) | collective-permute-done | bytes 122912 | tf_op jit(solution)/shard_map/ppermute | solution.py:987
  386.5 6.6 %shard_map.340 = bf16[1,384,768]{2,1,0:T(8,128)(2,1)} custom-call(s32[30]{0:T(128)} %concatenate.55.sc, bf16[8,384,768]{2,1,0:T(8,128)(2,1)} %get-tuple-element.220.dk_ref, bf16[8,384,768]{2,1,0:T(8,128)(2,1)} %get-tuple-element.210.dv_ref, bf16[2,192,768]{2,1,0:T(8,128)(2,1)} %get-tuple-element.211.dq_ref, bf16[8,384,768]{2,1,0:T(8,128)(2,1)} %get-tuple-element.178.x_ref, ...), custom_call_target="tpu_custom_call" | custom-call | flops 905969664 | bytes 2359296 | tf_op jit(solution)/shard_map/pallas_call | solution.py:868
  398.2 8.6 %collective-permute-done.55 = bf16[80,768]{1,0:T(8,128)(2,1)S(1)} collective-permute-done((bf16[80,768]{1,0:T(8,128)(2,1)S(1)}, bf16[80,768]{1,0:T(8,128)(2,1)S(1)}, u32[]{:S(2)}, u32[]{:S(2)}) %collective-permute-start.55) | collective-permute-done | bytes 122912 | tf_op jit(solution)/shard_map/ppermute | solution.py:987
  407.1 6.2 %collective-permute-done.56 = bf16[80,768]{1,0:T(8,128)(2,1)} collective-permute-done((bf16[80,768]{1,0:T(8,128)(2,1)}, bf16[80,768]{1,0:T(8,128)(2,1)}, u32[]{:S(2)}, u32[]{:S(2)}) %collective-permute-start.56) | collective-permute-done | bytes 122912 | tf_op jit(solution)/shard_map/ppermute | solution.py:987
  431.8 5.3 %shard_map.341 = (f32[768,768]{1,0:T(8,128)}, f32[192,3072]{1,0:T(8,128)}, f32[192,768]{1,0:T(8,128)}) custom-call(s32[8]{0:T(128)} %compare_select_fusion.sc, bf16[216,768]{1,0:T(8,128)(2,1)} %copy-done.8, bf16[216,768]{1,0:T(8,128)(2,1)} %collective-permute-done.39.refs_1_, bf16[216,768]{1,0:T(8,128)(2,1)} %collective-permute-done.46.refs_2_, ...), custom_call_target="tpu_custom_call" | custom-call | bytes 7962624 | tf_op jit(solution)/shard_map/pallas_call | solution.py:952
  (321 shorter events, 134.7 us)
Async XLA Ops:
  7.2 134.8 %all-gather.3.cloned.1.call-start = ((), (), s32[]{:S(2)}) async-start(), calls=%async_computation.2 | async-start | bytes 2654208 | tf_op jit(solution)/shard_map/all_gather | solution.py:1213
  15.1 26.6 %collective-permute-start.5 = (bf16[208,1536]{1,0:T(8,128)(2,1)S(1)}, bf16[208,1536]{1,0:T(8,128)(2,1)}, u32[]{:S(2)}, u32[]{:S(2)}) collective-permute-start(bf16[208,1536]{1,0:T(8,128)(2,1)S(1)} %pad_maximum_fusion.refs_4_), channel_id=1, source_target_pairs={{0,1},{1,0},{2,3},{3,2},{4,5},{5,4},{6,7},{7,6},{8,9},{9,8},{10,11... | collective-permute-start | bytes 1916936 | tf_op jit(solution)/shard_map/ppermute | solution.py:1006
  15.2 26.5 %collective-permute-start.7 = (bf16[192,1536]{1,0:T(8,128)(2,1)S(1)}, bf16[192,1536]{1,0:T(8,128)(2,1)S(1)}, u32[]{:S(2)}, u32[]{:S(2)}) collective-permute-start(bf16[192,1536]{1,0:T(8,128)(2,1)S(1)} %constant_dynamic-update-slice_fusion.refs_0_), channel_id=1, source_target_pairs={{0,2},{1,3},{2,0},{3,1},{4,6},{5,7},{6,4},{7,5},{8,10},{9,11},{10,... | collective-permute-start | bytes 1769480 | tf_op jit(solution)/shard_map/ppermute | solution.py:1009
  41.7 19.3 %collective-permute-start.10 = (bf16[192,1536]{1,0:T(8,128)(2,1)S(1)}, bf16[192,1536]{1,0:T(8,128)(2,1)}, u32[]{:S(2)}, u32[]{:S(2)}) collective-permute-start(bf16[192,1536]{1,0:T(8,128)(2,1)S(1)} %constant_dynamic-update-slice_fusion.refs_0_), channel_id=1, source_target_pairs={{0,1},{1,0},{2,3},{3,2},{4,5},{5,4},{6,7},{7,6},{8,9},{9,8},{10,11... | collective-permute-start | bytes 1769480 | tf_op jit(solution)/shard_map/ppermute | solution.py:1006
  41.7 19.2 %collective-permute-start.12 = (bf16[192,1536]{1,0:T(8,128)(2,1)}, bf16[192,1536]{1,0:T(8,128)(2,1)}, u32[]{:S(2)}, u32[]{:S(2)}) collective-permute-start(bf16[192,1536]{1,0:T(8,128)(2,1)} %get-tuple-element.294.refs_4_), channel_id=1, source_target_pairs={{0,2},{1,3},{2,0},{3,1},{4,6},{5,7},{6,4},{7,5},{8,10},{9,11},{10,... | collective-permute-start | bytes 1769480 | tf_op jit(solution)/shard_map/ppermute | solution.py:1009
  65.7 20.8 %collective-permute-start.17 = (bf16[192,1536]{1,0:T(8,128)(2,1)}, bf16[192,1536]{1,0:T(8,128)(2,1)}, u32[]{:S(2)}, u32[]{:S(2)}) collective-permute-start(bf16[192,1536]{1,0:T(8,128)(2,1)} %get-tuple-element.293.refs_8_), channel_id=1, source_target_pairs={{0,2},{1,3},{2,0},{3,1},{4,6},{5,7},{6,4},{7,5},{8,10},{9,11},{10,... | collective-permute-start | bytes 1769480 | tf_op jit(solution)/shard_map/ppermute | solution.py:1009
  77.9 225.0 %reduce-scatter.2.cloned.1.call-start = ((), (), s32[]{:S(2)}) async-start(), calls=%async_computation.1 | async-start | bytes 5971968 | tf_op jit(solution)/shard_map/reduce_scatter | solution.py:1235
  93.7 45.2 %collective-permute-start.20 = (bf16[768,768]{1,0:T(8,128)(2,1)}, bf16[768,768]{1,0:T(8,128)(2,1)S(1)}, u32[]{:S(2)}, u32[]{:S(2)}) collective-permute-start(bf16[768,768]{1,0:T(8,128)(2,1)} %refs_12_), channel_id=1, source_target_pairs={{0,2},{1,3},{2,0},{3,1},{4,6},{5,7},{6,4},{7,5},{8,10},{9,11},{10,... | collective-permute-start | bytes 3538952 | tf_op jit(solution)/shard_map/ppermute | solution.py:1209
  94.3 49.6 %collective-permute-start.21 = (bf16[768,768]{1,0:T(8,128)(2,1)}, bf16[768,768]{1,0:T(8,128)(2,1)}, u32[]{:S(2)}, u32[]{:S(2)}) collective-permute-start(bf16[768,768]{1,0:T(8,128)(2,1)} %refs_12_), channel_id=1, source_target_pairs={{0,1},{1,0},{2,3},{3,2},{4,5},{5,4},{6,7},{7,6},{8,9},{9,8},{10,11... | collective-permute-start | bytes 3538952 | tf_op jit(solution)/shard_map/ppermute | solution.py:1210
  186.9 84.6 %collective-permute-start.26 = (bf16[192,768]{1,0:T(8,128)(2,1)S(1)}, bf16[192,768]{1,0:T(8,128)(2,1)S(1)}, u32[]{:S(2)}, u32[]{:S(2)}) collective-permute-start(bf16[192,768]{1,0:T(8,128)(2,1)S(1)} %collective-permute-done.24), channel_id=1, source_target_pairs={{0,8},{8,16},{16,24},{24,28},{28,20},{20,12},{12,4},{4,0},{1,9},{9... | collective-permute-start | bytes 884744 | tf_op jit(solution)/shard_map/ppermute | solution.py:987
  188.8 82.7 %collective-permute-start.27 = (bf16[192,768]{1,0:T(8,128)(2,1)S(1)}, bf16[192,768]{1,0:T(8,128)(2,1)S(1)}, u32[]{:S(2)}, u32[]{:S(2)}) collective-permute-start(bf16[192,768]{1,0:T(8,128)(2,1)S(1)} %collective-permute-done.25), channel_id=1, source_target_pairs={{0,4},{8,0},{16,8},{24,16},{28,24},{20,28},{12,20},{4,12},{1,5},{9... | collective-permute-start | bytes 884744 | tf_op jit(solution)/shard_map/ppermute | solution.py:987
  271.5 22.5 %collective-permute-start.28 = (bf16[192,768]{1,0:T(8,128)(2,1)S(1)}, bf16[192,768]{1,0:T(8,128)(2,1)S(1)}, u32[]{:S(2)}, u32[]{:S(2)}) collective-permute-start(bf16[192,768]{1,0:T(8,128)(2,1)S(1)} %collective-permute-done.26), channel_id=1, source_target_pairs={{0,8},{8,16},{16,24},{24,28},{28,20},{20,12},{12,4},{4,0},{1,9},{9... | collective-permute-start | bytes 884744 | tf_op jit(solution)/shard_map/ppermute | solution.py:987
  274.5 20.2 %collective-permute-start.29 = (bf16[192,768]{1,0:T(8,128)(2,1)S(1)}, bf16[192,768]{1,0:T(8,128)(2,1)S(1)}, u32[]{:S(2)}, u32[]{:S(2)}) collective-permute-start(bf16[192,768]{1,0:T(8,128)(2,1)S(1)} %collective-permute-done.27), channel_id=1, source_target_pairs={{0,4},{8,0},{16,8},{24,16},{28,24},{20,28},{12,20},{4,12},{1,5},{9... | collective-permute-start | bytes 884744 | tf_op jit(solution)/shard_map/ppermute | solution.py:987
  310.1 33.8 %collective-permute-start.40 = (bf16[640,768]{1,0:T(8,128)(2,1)S(1)}, bf16[640,768]{1,0:T(8,128)(2,1)}, u32[]{:S(2)}, u32[]{:S(2)}) collective-permute-start(bf16[640,768]{1,0:T(8,128)(2,1)S(1)} %fusion.8), channel_id=1, source_target_pairs={{0,2},{1,3},{2,0},{3,1},{4,6},{5,7},{6,4},{7,5},{8,10},{9,11},{10,... | collective-permute-start | bytes 2949128 | tf_op jit(solution)/shard_map/ppermute | solution.py:1264
  320.7 23.2 %collective-permute-start.36 = (bf16[384,768]{1,0:T(8,128)(2,1)}, bf16[384,768]{1,0:T(8,128)(2,1)}, u32[]{:S(2)}, u32[]{:S(2)}) collective-permute-start(bf16[384,768]{1,0:T(8,128)(2,1)} %get-tuple-element.292), channel_id=1, source_target_pairs={{0,8},{8,16},{16,24},{24,28},{28,20},{20,12},{12,4},{4,0},{1,9},{9... | collective-permute-start | bytes 1769480 | tf_op jit(solution)/shard_map/ppermute | solution.py:987
  322.7 21.2 %collective-permute-start.37 = (bf16[384,768]{1,0:T(8,128)(2,1)}, bf16[384,768]{1,0:T(8,128)(2,1)}, u32[]{:S(2)}, u32[]{:S(2)}) collective-permute-start(bf16[384,768]{1,0:T(8,128)(2,1)} %get-tuple-element.291), channel_id=1, source_target_pairs={{0,4},{8,0},{16,8},{24,16},{28,24},{20,28},{12,20},{4,12},{1,5},{9... | collective-permute-start | bytes 1769480 | tf_op jit(solution)/shard_map/ppermute | solution.py:987
  323.8 18.7 %collective-permute-start.38 = (bf16[216,768]{1,0:T(8,128)(2,1)S(1)}, bf16[216,768]{1,0:T(8,128)(2,1)}, u32[]{:S(2)}, u32[]{:S(2)}) collective-permute-start(bf16[216,768]{1,0:T(8,128)(2,1)S(1)} %add_convert_fusion.2.refs_0_), channel_id=1, source_target_pairs={{0,8},{8,16},{16,24},{24,28},{28,20},{20,12},{12,4},{4,0},{1,9},{9... | collective-permute-start | bytes 995336 | tf_op jit(solution)/shard_map/ppermute | solution.py:987
  348.3 30.0 %collective-permute-start.41 = (bf16[384,768]{1,0:T(8,128)(2,1)}, bf16[384,768]{1,0:T(8,128)(2,1)S(1)}, u32[]{:S(2)}, u32[]{:S(2)}) collective-permute-start(bf16[384,768]{1,0:T(8,128)(2,1)} %get-tuple-element.290), channel_id=1, source_target_pairs={{0,8},{8,16},{16,24},{24,28},{28,20},{20,12},{12,4},{4,0},{1,9},{9... | collective-permute-start | bytes 1769480 | tf_op jit(solution)/shard_map/ppermute | solution.py:987
  349.4 28.9 %collective-permute-start.42 = (bf16[384,768]{1,0:T(8,128)(2,1)}, bf16[384,768]{1,0:T(8,128)(2,1)S(1)}, u32[]{:S(2)}, u32[]{:S(2)}) collective-permute-start(bf16[384,768]{1,0:T(8,128)(2,1)} %get-tuple-element.289), channel_id=1, source_target_pairs={{0,4},{8,0},{16,8},{24,16},{28,24},{20,28},{12,20},{4,12},{1,5},{9... | collective-permute-start | bytes 1769480 | tf_op jit(solution)/shard_map/ppermute | solution.py:987
  358.7 19.6 %collective-permute-start.45 = (bf16[216,768]{1,0:T(8,128)(2,1)}, bf16[216,768]{1,0:T(8,128)(2,1)}, u32[]{:S(2)}, u32[]{:S(2)}) collective-permute-start(bf16[216,768]{1,0:T(8,128)(2,1)} %collective-permute-done.38.refs_7_), channel_id=1, source_target_pairs={{0,8},{8,16},{16,24},{24,28},{28,20},{20,12},{12,4},{4,0},{1,9},{9... | collective-permute-start | bytes 995336 | tf_op jit(solution)/shard_map/ppermute | solution.py:987
  384.5 28.9 %collective-permute-start.49 = (bf16[384,768]{1,0:T(8,128)(2,1)}, bf16[384,768]{1,0:T(8,128)(2,1)}, u32[]{:S(2)}, u32[]{:S(2)}) collective-permute-start(bf16[384,768]{1,0:T(8,128)(2,1)} %get-tuple-element.288), channel_id=1, source_target_pairs={{0,8},{8,16},{16,24},{24,28},{28,20},{20,12},{12,4},{4,0},{1,9},{9... | collective-permute-start | bytes 1769480 | tf_op jit(solution)/shard_map/ppermute | solution.py:987
  385.8 27.6 %collective-permute-start.50 = (bf16[384,768]{1,0:T(8,128)(2,1)S(1)}, bf16[384,768]{1,0:T(8,128)(2,1)}, u32[]{:S(2)}, u32[]{:S(2)}) collective-permute-start(bf16[384,768]{1,0:T(8,128)(2,1)S(1)} %get-tuple-element.287), channel_id=1, source_target_pairs={{0,4},{8,0},{16,8},{24,16},{28,24},{20,28},{12,20},{4,12},{1,5},{9... | collective-permute-start | bytes 1769480 | tf_op jit(solution)/shard_map/ppermute | solution.py:987
  393.1 20.2 %collective-permute-start.53 = (bf16[216,768]{1,0:T(8,128)(2,1)}, bf16[216,768]{1,0:T(8,128)(2,1)S(1)}, u32[]{:S(2)}, u32[]{:S(2)}) collective-permute-start(bf16[216,768]{1,0:T(8,128)(2,1)} %collective-permute-done.45.refs_6_), channel_id=1, source_target_pairs={{0,8},{8,16},{16,24},{24,28},{28,20},{20,12},{12,4},{4,0},{1,9},{9... | collective-permute-start | bytes 995336 | tf_op jit(solution)/shard_map/ppermute | solution.py:987
  394.5 18.8 %collective-permute-start.54 = (bf16[216,768]{1,0:T(8,128)(2,1)}, bf16[216,768]{1,0:T(8,128)(2,1)S(1)}, u32[]{:S(2)}, u32[]{:S(2)}) collective-permute-start(bf16[216,768]{1,0:T(8,128)(2,1)} %collective-permute-done.46.refs_2_), channel_id=1, source_target_pairs={{0,4},{8,0},{16,8},{24,16},{28,24},{20,28},{12,20},{4,12},{1,5},{9... | collective-permute-start | bytes 995336 | tf_op jit(solution)/shard_map/ppermute | solution.py:987
  (104 other events, 1177.1 us)
Sparse Core Ops, SparseCore 0:
  78.0 49.3 all-gather.2
  185.4 110.1 reduce-scatter.1

commit v5 on v4

--- a/solution.py
+++ b/solution.py
@@ -902,7 +902,8 @@
     tail = whole[3 * rows : 3 * rows + TAIL_ROWS, :]
     each = logit_ref.shape[0]
     two_ref[...] = tail[0:1, :rows]
-    rms_ref[...] = jnp.sqrt(tail[1:4, 0:1] * (1.0 / entries))
+    squares = jnp.concatenate([tail[n : n + 1, 0:1] for n in range(1, 4)], axis=1)
+    rms_ref[...] = jnp.sqrt(squares * (1.0 / entries))
     logit_ref[...] = tail[4 : 4 + each, :heads]
     weight_ref[...] = tail[4 + each : 4 + 2 * each, :heads]
 
@@ -911,7 +912,7 @@
     count = len(pieces)
     rows, width = wq.shape
     ins = [*pieces, wq, wk, wv, gain]
-    shapes = [(rows, width)] * 3 + [(1, rows), (1, rows), (each, heads), (each, heads), (3, 1)]
+    shapes = [(rows, width)] * 3 + [(1, rows), (1, rows), (each, heads), (each, heads), (1, 3)]
     fixed = lambda i, sc: (0, 0)
     return pl.pallas_call(
         functools.partial(finish_kernel, entries, heads),
@@ -1246,30 +1247,30 @@
         )
 
     last = count // 2
+    far = parts(count - 1, 1, dk)
+    dk, far, *moved = tie(dk, far, *moved)
+    leaving.finish(*moved)
+    up, down = far_start(far[0])
+    moved = leaving.start()
     total = -(-(3 * per + TAIL_ROWS) // (8 * count)) * 8 * count
-    dk, *moved = tie(dk, *moved)
-    leaving.finish(*moved)
-    moved = leaving.start()
     keep, send = weight_grads(
         scalars, wt_count, total, dk, dv, dq, xg, gain_one, r_logit, r_weight, grad_gain_two, squares
     )
-    send, dk, *moved = tie(send, dk, *moved)
+    up, down, keep, send, summed, dk, *moved = tie(up, down, keep, send, summed, dk, *moved)
     leaving.finish(*moved)
+    up, down = far_end(up, down)
     near = lax.ppermute(send, "wt", swaps(wt_count, 1))
-    far = parts(count - 1, 1, dk)
-    near, far, summed, *moved = tie(near, far, summed, *leaving.start())
+    ffn_far = lax.ppermute(summed[:, width:], "wt", swaps(wt_count, 2))
+    pair = parts(2 * (last - 1) - 1, 2, dk)
+    near, ffn_far, pair, *moved = tie(near, ffn_far, pair, *leaving.start())
     leaving.finish(*moved)
-    ffn_far = lax.ppermute(summed[:, width:], "wt", swaps(wt_count, 2))
-    up, down = far_start(far[0])
     over = lax.ppermute(add(keep[1], near[1]), "wt", swaps(wt_count, 2))
-    pair = parts(2 * (last - 1) - 1, 2, dk)
-    up, down, pair, ffn_far = tie(up, down, pair, ffn_far)
-    up, down = far_end(up, down)
     spread = Spreading(add(summed[:, :width], ffn_far), count)
 
     turn = None
     for k in range(last - 1, 0, -1):
-        up, down = ring_both(add(up, pair[1]), add(down, pair[0]))
+        up, down, dk = tie(add(up, pair[1]), add(down, pair[0]), dk)
+        up, down = ring_both(up, down)
         streams = [s for s in (spread, leaving) if not s.done]
         moved = [stream.start() for stream in streams]
         after = parts(2 * (k - 1) - 1, 2, dk) if k > 1 else parts(0, 1, dk)
@@ -1277,9 +1278,10 @@
             up, down, pair, moved, over = tie(up, down, after, moved, over)
             turn = Turning(add(keep[0], near[0], over).reshape(count, -1, width), me)
         else:
-            if not turn.done:
-                after, *both = tie(after, *turn.start())
-                turn.finish(*both)
+            for _ in range(2):
+                if not turn.done:
+                    after, *both = tie(after, *turn.start())
+                    turn.finish(*both)
             both = [] if turn.done else turn.start()
             up, down, pair, moved, both = tie(up, down, after, moved, both)
             if both:
@@ -1297,18 +1299,24 @@
         second = jnp.where(offset == n, leaving.pieces[n], second)
     output_own = jnp.concatenate([out_low[:half], second], axis=0)
     places = ring_places(count, me, list(range(count))).astype(jnp.int32)
-    ffn_grads = None
+    ffn_grads = []
+
+    def unpacked():
+        return unpack(places, spread.ordered(), (w_out.shape, w_in.shape, w_output.shape))
+
     while not turn.done:
         moving = [] if spread.done else list(spread.start())
-        one, two, *moving = tie(*turn.start(), *moving)
+        if spread.done and not ffn_grads:
+            ffn_grads = unpacked()
+            one, two, ffn_grads = tie(*turn.start(), ffn_grads)
+        else:
+            one, two, *moving = tie(*turn.start(), *moving)
         turn.finish(one, two)
         if moving:
             spread.finish(*moving)
-        elif ffn_grads is None:
-            ffn_grads = unpack(places, spread.ordered(), (w_out.shape, w_in.shape, w_output.shape))
-            turn_start = list(turn.start())
-            one, two, *ffn_grads = tie(*turn_start, *ffn_grads)
-            turn.finish(one, two)
+    while not spread.done:
+        spread.finish(*tie(*spread.start()))
+    ffn_grads = ffn_grads or unpacked()
     grad_out, grad_in, grad_o = ffn_grads
     entries = float(rows * width) * (count * wt_count)
     grad_q, grad_k, grad_v, gain_grad, gain_two_grad, logit_grad, weight_grad, rms = finish_grads(

time: 461 us -> 458 us (level)
  other arithmetic: 36.7 us -> 29.3 us
    ppermute x24, starting transfers between devices: 38.4 us -> 20.7 us  [ring_both(): lax.ppermute(up, 'ctx', ring(count, 1))]
    ppermute x24, starting transfers between devices: 13.3 us -> 26.5 us  [ring_both(): lax.ppermute(down, 'ctx', ring(count, -1))]
    ppermute x24, waiting for transfers between devices: 37.6 us -> 44.3 us  [ring_both(): lax.ppermute(up, 'ctx', ring(count, 1))]
    convert_element_type x11, other arithmetic: 25 us -> 19 us  [add(): return sum((v.astype(F32) for v in values)).astype(BF16)]
  transfers between devices with their start and end apart: 69 -> 69, of which waited for: 22 -> 20; matrix products, arithmetic and copies ran while one was open for 10% -> 10% of each run, Pallas kernels for 48% -> 49%
where the time goes in v5:
time: 458 us; the launch traced here: 452 us
  Pallas kernels  250 us (55%)
  waiting for transfers between devices  73.5 us (16%)
  starting transfers between devices  56.9 us (12%)
  other arithmetic  29.3 us (6%)
  local copies, waits for them, and re-layouts  21.5 us (5%)
  between operations  20 us (4%)
    pallas_call x1, Pallas kernels, back(): pl.pallas_call(functools.partial(back_kernel, count, heads, base, group,...  83.7 us
    pallas_call x1, Pallas kernels, attend(): pl.pallas_call(functools.partial(attend_kernel, count, heads, group), gri...  44.8 us
    ppermute x24, waiting for transfers between devices, ring_both(): lax.ppermute(up, 'ctx', ring(count, 1))  44.3 us
    pallas_call x5, Pallas kernels, token_parts(): pl.pallas_call(functools.partial(token_kernel, count, first), grid_spec=p...  35.8 us
    ppermute x24, starting transfers between devices, ring_both(): lax.ppermute(down, 'ctx', ring(count, -1))  26.5 us
    pallas_call x1, Pallas kernels, ffn(): pl.pallas_call(functools.partial(ffn_kernel, wt_count), grid_spec=pltpu.P...  24.1 us
    pallas_call x3, Pallas kernels, project(): pl.pallas_call(functools.partial(project_kernel, batch, shares), grid_spe...  23.3 us
    ppermute x24, starting transfers between devices, ring_both(): lax.ppermute(up, 'ctx', ring(count, 1))  20.7 us
  transfers between devices with their start and end apart: 69, of which 20 were waited for; matrix products, arithmetic and copies ran while one was open for 10% of the time, Pallas kernels for 49%

profile of v5, /device:TPU:0, one launch (start us, length us, event | category | flops | bytes accessed | tf_op | source)
XLA Modules:
  0.0 451.5 jit_solution(100583261664663272)
XLA Ops:
  25.4 5.2 %collective-permute-done.2.refs_6_ = bf16[208,1536]{1,0:T(8,128)(2,1)} collective-permute-done((bf16[208,1536]{1,0:T(8,128)(2,1)S(1)}, bf16[208,1536]{1,0:T(8,128)(2,1)}, u32[]{:S(2)}, u32[]{:S(2)}) %collective-permute-start.2) | collective-permute-done | bytes 639008 | tf_op jit(solution)/shard_map/ppermute | solution.py:1010
  34.5 7.2 %collective-permute-done.7.refs_2_ = bf16[192,1536]{1,0:T(8,128)(2,1)S(1)} collective-permute-done((bf16[192,1536]{1,0:T(8,128)(2,1)S(1)}, bf16[192,1536]{1,0:T(8,128)(2,1)S(1)}, u32[]{:S(2)}, u32[]{:S(2)}) %collective-permute-start.7) | collective-permute-done | bytes 589856 | tf_op jit(solution)/shard_map/ppermute | solution.py:1010
  43.4 3.5 collective-permute-done.3.refs_0_
  52.6 8.9 %shard_map.327 = (bf16[8,384,768]{2,1,0:T(8,128)(2,1)}, bf16[8,384,768]{2,1,0:T(8,128)(2,1)}, bf16[8,384,768]{2,1,0:T(8,128)(2,1)}, bf16[768,1536]{1,0:T(8,128)(2,1)}) custom-call(s32[30]{0:T(128)} %concatenate.55.sc, bf16[384,768]{1,0:T(8,128)(2,1)} %bitcast.110, bf16[384,768]{1,0:T(8,128)(2,1)} %collective-permute-done.refs_1_, ...), custom_call_target="tpu_custom_call" | custom-call | flops 2717908992 | bytes 7077888 | tf_op jit(solution)/shard_map/pallas_call | solution.py:93
  70.2 6.5 %shard_map.328 = (bf16[8,384,768]{2,1,0:T(8,128)(2,1)}, bf16[8,384,768]{2,1,0:T(8,128)(2,1)}, bf16[8,384,768]{2,1,0:T(8,128)(2,1)}) custom-call(s32[30]{0:T(128)} %concatenate.55.sc, bf16[384,768]{1,0:T(8,128)(2,1)} %collective-permute-done.3.refs_0_, ...), custom_call_target="tpu_custom_call", output_to_operand_aliasing={{0}: (5, {}), {1}: (6, {}), {2}: (7, {})} | custom-call | flops 1811939328 | bytes 4718592 | tf_op jit(solution)/shard_map/pallas_call | solution.py:93
  78.6 7.9 %shard_map.329 = (bf16[8,384,768]{2,1,0:T(8,128)(2,1)}, bf16[8,384,768]{2,1,0:T(8,128)(2,1)}, bf16[8,384,768]{2,1,0:T(8,128)(2,1)}) custom-call(s32[30]{0:T(128)} %concatenate.55.sc, bf16[384,768]{1,0:T(8,128)(2,1)} %copy-done.5, bf16[384,768]{1,0:T(8,128)(2,1)} %copy-done.6, ...), custom_call_target="tpu_custom_call", output_to_operand_aliasing={{0}: (6, {}), {1}: (7, {}), {2}: (8, {})} | custom-call | flops 2717908992 | bytes 7077888 | tf_op jit(solution)/shard_map/pallas_call | solution.py:93
  88.5 4.4 shard_map.330
  93.8 44.8 %shard_map.331 = (bf16[2,192,768]{2,1,0:T(8,128)(2,1)}, bf16[2,768,2304]{2,1,0:T(8,128)(2,1)}, f32[2,1,2304]{2,1,0:T(1,128)}) custom-call(s32[30]{0:T(128)} %concatenate.55.sc, bf16[2,192,768]{2,1,0:T(8,128)(2,1)} %get-tuple-element.197.q_ref, bf16[8,384,768]{2,1,0:T(8,128)(2,1)} %get-tuple-element.198.k_ref, bf16[8,384,768]{2,1,0:T(8,128)(2,1)} %get-tuple-element.199.v_ref, ...), custom_call_target="tpu_custom_call" | custom-call | flops 24461180928 | bytes 14155776 | tf_op jit(solution)/shard_map/pallas_call | solution.py:260
  143.4 24.1 %shard_map.332 = (bf16[384,768]{1,0:T(8,128)(2,1)}, f32[384,768]{1,0:T(8,128)}, bf16[384,768]{1,0:T(8,128)(2,1)}, bf16[1728,1536]{1,0:T(8,128)(2,1)}, bf16[1728,...) custom-call(s32[30]{0:T(128)} %concatenate.55.sc, bf16[384,768]{1,0:T(8,128)(2,1)} %bitcast.115, ...), custom_call_target="tpu_custom_call" | custom-call | flops 10418651136 | bytes 14155776 | tf_op jit(solution)/shard_map/pallas_call | solution.py:681
  171.7 5.2 %shard_map.333 = (f32[12,128]{1,0:T(8,128)}, f32[2,1,2304]{2,1,0:T(1,128)}) custom-call(bf16[2,192,768]{2,1,0:T(8,128)(2,1)} %bitcast.105, bf16[2,768,2304]{2,1,0:T(8,128)(2,1)} %get-tuple-element.213.t_ref, f32[12,2304]{1,0:T(8,128)} %reshape.112.spread_ref), custom_call_target="tpu_custom_call" | custom-call | flops 7077888 | bytes 7077888 | tf_op jit(solution)/shard_map/pallas_call | solution.py:341
  176.9 7.9 %add_convert_fusion = bf16[1728,1536]{1,0:T(8,128)(2,1)} fusion(bf16[1728,1536]{1,0:T(8,128)(2,1)} %collective-permute-done.23, bf16[1728,1536]{1,0:T(8,128)(2,1)} %get-tuple-element.210), kind=kLoop, calls=%fused_computation | loop fusion | flops 10616832 | bytes 15925248 | tf_op jit(solution)/shard_map/convert_element_type | solution.py:1026
  188.5 83.7 %shard_map.334 = (bf16[8,384,768]{2,1,0:T(8,128)(2,1)}, bf16[8,384,768]{2,1,0:T(8,128)(2,1)}, bf16[2,192,768]{2,1,0:T(8,128)(2,1)}, f32[12,128]{1,0:T(8,128)}) custom-call(s32[30]{0:T(128)} %concatenate.55.sc, bf16[2,192,768]{2,1,0:T(8,128)(2,1)} %get-tuple-element.197.q_ref, bf16[2,192,768]{2,1,0:T(8,128)(2,1)} %bitcast.106, ...), custom_call_target="tpu_custom_call" | custom-call | flops 61152952320 | bytes 23592960 | tf_op jit(solution)/shard_map/pallas_call | solution.py:452
  272.2 5.9 %shard_map.335 = bf16[1,384,768]{2,1,0:T(8,128)(2,1)} custom-call(s32[30]{0:T(128)} %concatenate.55.sc, bf16[8,384,768]{2,1,0:T(8,128)(2,1)} %get-tuple-element.271.dk_ref, bf16[8,384,768]{2,1,0:T(8,128)(2,1)} %get-tuple-element.219.dv_ref, bf16[2,192,768]{2,1,0:T(8,128)(2,1)} %get-tuple-element.220.dq_ref, bf16[8,384,768]{2,1,0:T(8,128)(2,1)} %get-tuple-element.190.x_ref, ...), custom_call_target="tpu_custom_call" | custom-call | flops 905969664 | bytes 2359296 | tf_op jit(solution)/shard_map/pallas_call | solution.py:868
  283.5 20.1 %shard_map.336 = (bf16[2,640,768]{2,1,0:T(8,128)(2,1)}, bf16[2,640,768]{2,1,0:T(8,128)(2,1)}) custom-call(s32[30]{0:T(128)} %concatenate.55.sc, bf16[8,384,768]{2,1,0:T(8,128)(2,1)} %get-tuple-element.271.dk_ref, bf16[8,384,768]{2,1,0:T(8,128)(2,1)} %get-tuple-element.219.dv_ref, bf16[2,192,768]{2,1,0:T(8,128)(2,1)} %get-tuple-element.220.dq_ref, ...), custom_call_target="tpu_custom_call" | custom-call | flops 7247757312 | bytes 23592960 | tf_op jit(solution)/shard_map/pallas_call | solution.py:806
  309.8 7.5 %shard_map.337 = bf16[2,384,768]{2,1,0:T(8,128)(2,1)} custom-call(s32[30]{0:T(128)} %concatenate.55.sc, bf16[8,384,768]{2,1,0:T(8,128)(2,1)} %get-tuple-element.271.dk_ref, bf16[8,384,768]{2,1,0:T(8,128)(2,1)} %get-tuple-element.219.dv_ref, bf16[2,192,768]{2,1,0:T(8,128)(2,1)} %get-tuple-element.220.dq_ref, bf16[8,384,768]{2,1,0:T(8,128)(2,1)} %get-tuple-element.190.x_ref, ...), custom_call_target="tpu_custom_call" | custom-call | flops 1811939328 | bytes 4718592 | tf_op jit(solution)/shard_map/pallas_call | solution.py:868
  324.9 8.5 %shard_map.338 = bf16[2,384,768]{2,1,0:T(8,128)(2,1)} custom-call(s32[30]{0:T(128)} %concatenate.55.sc, bf16[8,384,768]{2,1,0:T(8,128)(2,1)} %get-tuple-element.271.dk_ref, bf16[8,384,768]{2,1,0:T(8,128)(2,1)} %get-tuple-element.219.dv_ref, bf16[2,192,768]{2,1,0:T(8,128)(2,1)} %get-tuple-element.220.dq_ref, bf16[8,384,768]{2,1,0:T(8,128)(2,1)} %get-tuple-element.190.x_ref, ...), custom_call_target="tpu_custom_call" | custom-call | flops 1811939328 | bytes 4718592 | tf_op jit(solution)/shard_map/pallas_call | solution.py:868
  333.4 9.3 %collective-permute-done.38.refs_7_ = bf16[216,768]{1,0:T(8,128)(2,1)} collective-permute-done((bf16[216,768]{1,0:T(8,128)(2,1)S(1)}, bf16[216,768]{1,0:T(8,128)(2,1)}, u32[]{:S(2)}, u32[]{:S(2)}) %collective-permute-start.38) | collective-permute-done | bytes 331808 | tf_op jit(solution)/shard_map/ppermute | solution.py:988
  348.9 7.5 %shard_map.339 = bf16[2,384,768]{2,1,0:T(8,128)(2,1)} custom-call(s32[30]{0:T(128)} %concatenate.55.sc, bf16[8,384,768]{2,1,0:T(8,128)(2,1)} %get-tuple-element.271.dk_ref, bf16[8,384,768]{2,1,0:T(8,128)(2,1)} %get-tuple-element.219.dv_ref, bf16[2,192,768]{2,1,0:T(8,128)(2,1)} %get-tuple-element.220.dq_ref, bf16[8,384,768]{2,1,0:T(8,128)(2,1)} %get-tuple-element.190.x_ref, ...), custom_call_target="tpu_custom_call" | custom-call | flops 1811939328 | bytes 4718592 | tf_op jit(solution)/shard_map/pallas_call | solution.py:868
  367.4 15.4 %collective-permute-done.49 = bf16[80,768]{1,0:T(8,128)(2,1)S(1)} collective-permute-done((bf16[80,768]{1,0:T(8,128)(2,1)S(1)}, bf16[80,768]{1,0:T(8,128)(2,1)S(1)}, u32[]{:S(2)}, u32[]{:S(2)}) %collective-permute-start.49) | collective-permute-done | bytes 122912 | tf_op jit(solution)/shard_map/ppermute | solution.py:988
  383.0 5.1 %collective-permute-done.50 = bf16[80,768]{1,0:T(8,128)(2,1)} collective-permute-done((bf16[80,768]{1,0:T(8,128)(2,1)}, bf16[80,768]{1,0:T(8,128)(2,1)}, u32[]{:S(2)}, u32[]{:S(2)}) %collective-permute-start.50) | collective-permute-done | bytes 122912 | tf_op jit(solution)/shard_map/ppermute | solution.py:988
  394.8 6.6 %shard_map.340 = bf16[1,384,768]{2,1,0:T(8,128)(2,1)} custom-call(s32[30]{0:T(128)} %concatenate.55.sc, bf16[8,384,768]{2,1,0:T(8,128)(2,1)} %get-tuple-element.271.dk_ref, bf16[8,384,768]{2,1,0:T(8,128)(2,1)} %get-tuple-element.219.dv_ref, bf16[2,192,768]{2,1,0:T(8,128)(2,1)} %get-tuple-element.220.dq_ref, bf16[8,384,768]{2,1,0:T(8,128)(2,1)} %get-tuple-element.190.x_ref, ...), custom_call_target="tpu_custom_call" | custom-call | flops 905969664 | bytes 2359296 | tf_op jit(solution)/shard_map/pallas_call | solution.py:868
  406.1 4.5 collective-permute-done.55.refs_7_
  434.6 5.2 %shard_map.341 = (f32[768,768]{1,0:T(8,128)}, f32[192,3072]{1,0:T(8,128)}, f32[192,768]{1,0:T(8,128)}) custom-call(s32[8]{0:T(128)} %compare_select_fusion.sc, bf16[216,768]{1,0:T(8,128)(2,1)} %copy-done.9, bf16[216,768]{1,0:T(8,128)(2,1)} %collective-permute-done.39.refs_1_, bf16[216,768]{1,0:T(8,128)(2,1)} %collective-permute-done.48.refs_2_, ...), custom_call_target="tpu_custom_call" | custom-call | bytes 7962624 | tf_op jit(solution)/shard_map/pallas_call | solution.py:953
  440.5 3.7 shard_map.342
  (310 shorter events, 123.3 us)
Async XLA Ops:
  7.2 134.4 %all-gather.3.cloned.1.call-start = ((), (), s32[]{:S(2)}) async-start(), calls=%async_computation.2 | async-start | bytes 2654208 | tf_op jit(solution)/shard_map/all_gather | solution.py:1214
  15.1 26.6 %collective-permute-start.5 = (bf16[208,1536]{1,0:T(8,128)(2,1)S(1)}, bf16[208,1536]{1,0:T(8,128)(2,1)}, u32[]{:S(2)}, u32[]{:S(2)}) collective-permute-start(bf16[208,1536]{1,0:T(8,128)(2,1)S(1)} %pad_maximum_fusion.refs_4_), channel_id=1, source_target_pairs={{0,1},{1,0},{2,3},{3,2},{4,5},{5,4},{6,7},{7,6},{8,9},{9,8},{10,11... | collective-permute-start | bytes 1916936 | tf_op jit(solution)/shard_map/ppermute | solution.py:1007
  15.2 26.5 %collective-permute-start.7 = (bf16[192,1536]{1,0:T(8,128)(2,1)S(1)}, bf16[192,1536]{1,0:T(8,128)(2,1)S(1)}, u32[]{:S(2)}, u32[]{:S(2)}) collective-permute-start(bf16[192,1536]{1,0:T(8,128)(2,1)S(1)} %constant_dynamic-update-slice_fusion.refs_0_), channel_id=1, source_target_pairs={{0,2},{1,3},{2,0},{3,1},{4,6},{5,7},{6,4},{7,5},{8,10},{9,11},{10,... | collective-permute-start | bytes 1769480 | tf_op jit(solution)/shard_map/ppermute | solution.py:1010
  41.7 19.9 %collective-permute-start.10 = (bf16[192,1536]{1,0:T(8,128)(2,1)S(1)}, bf16[192,1536]{1,0:T(8,128)(2,1)}, u32[]{:S(2)}, u32[]{:S(2)}) collective-permute-start(bf16[192,1536]{1,0:T(8,128)(2,1)S(1)} %constant_dynamic-update-slice_fusion.refs_0_), channel_id=1, source_target_pairs={{0,1},{1,0},{2,3},{3,2},{4,5},{5,4},{6,7},{7,6},{8,9},{9,8},{10,11... | collective-permute-start | bytes 1769480 | tf_op jit(solution)/shard_map/ppermute | solution.py:1007
  65.7 20.9 %collective-permute-start.17 = (bf16[192,1536]{1,0:T(8,128)(2,1)S(1)}, bf16[192,1536]{1,0:T(8,128)(2,1)}, u32[]{:S(2)}, u32[]{:S(2)}) collective-permute-start(bf16[192,1536]{1,0:T(8,128)(2,1)S(1)} %copy-done.24), channel_id=1, source_target_pairs={{0,2},{1,3},{2,0},{3,1},{4,6},{5,7},{6,4},{7,5},{8,10},{9,11},{10,... | collective-permute-start | bytes 1769480 | tf_op jit(solution)/shard_map/ppermute | solution.py:1010
  77.9 225.8 %reduce-scatter.2.cloned.1.call-start = ((), (), s32[]{:S(2)}) async-start(), calls=%async_computation.1 | async-start | bytes 5971968 | tf_op jit(solution)/shard_map/reduce_scatter | solution.py:1236
  93.0 45.6 %collective-permute-start.20 = (bf16[768,768]{1,0:T(8,128)(2,1)S(1)}, bf16[768,768]{1,0:T(8,128)(2,1)}, u32[]{:S(2)}, u32[]{:S(2)}) collective-permute-start(bf16[768,768]{1,0:T(8,128)(2,1)S(1)} %copy-done.51), channel_id=1, source_target_pairs={{0,2},{1,3},{2,0},{3,1},{4,6},{5,7},{6,4},{7,5},{8,10},{9,11},{10,... | collective-permute-start | bytes 3538952 | tf_op jit(solution)/shard_map/ppermute | solution.py:1210
  93.6 49.8 %collective-permute-start.21 = (bf16[768,768]{1,0:T(8,128)(2,1)S(1)}, bf16[768,768]{1,0:T(8,128)(2,1)}, u32[]{:S(2)}, u32[]{:S(2)}) collective-permute-start(bf16[768,768]{1,0:T(8,128)(2,1)S(1)} %copy-done.51), channel_id=1, source_target_pairs={{0,1},{1,0},{2,3},{3,2},{4,5},{5,4},{6,7},{7,6},{8,9},{9,8},{10,11... | collective-permute-start | bytes 3538952 | tf_op jit(solution)/shard_map/ppermute | solution.py:1211
  186.5 91.6 %collective-permute-start.26 = (bf16[192,768]{1,0:T(8,128)(2,1)S(1)}, bf16[192,768]{1,0:T(8,128)(2,1)S(1)}, u32[]{:S(2)}, u32[]{:S(2)}) collective-permute-start(bf16[192,768]{1,0:T(8,128)(2,1)S(1)} %collective-permute-done.24), channel_id=1, source_target_pairs={{0,8},{8,16},{16,24},{24,28},{28,20},{20,12},{12,4},{4,0},{1,9},{9... | collective-permute-start | bytes 884744 | tf_op jit(solution)/shard_map/ppermute | solution.py:988
  187.7 90.4 %collective-permute-start.27 = (bf16[192,768]{1,0:T(8,128)(2,1)S(1)}, bf16[192,768]{1,0:T(8,128)(2,1)S(1)}, u32[]{:S(2)}, u32[]{:S(2)}) collective-permute-start(bf16[192,768]{1,0:T(8,128)(2,1)S(1)} %collective-permute-done.25), channel_id=1, source_target_pairs={{0,4},{8,0},{16,8},{24,16},{28,24},{20,28},{12,20},{4,12},{1,5},{9... | collective-permute-start | bytes 884744 | tf_op jit(solution)/shard_map/ppermute | solution.py:988
  279.4 24.2 %collective-permute-start.28 = (bf16[192,768]{1,0:T(8,128)(2,1)S(1)}, bf16[192,768]{1,0:T(8,128)(2,1)S(1)}, u32[]{:S(2)}, u32[]{:S(2)}) collective-permute-start(bf16[192,768]{1,0:T(8,128)(2,1)S(1)} %get-tuple-element.330), channel_id=1, source_target_pairs={{0,8},{8,16},{16,24},{24,28},{28,20},{20,12},{12,4},{4,0},{1,9},{9... | collective-permute-start | bytes 884744 | tf_op jit(solution)/shard_map/ppermute | solution.py:988
  279.5 24.2 %collective-permute-start.29 = (bf16[192,768]{1,0:T(8,128)(2,1)S(1)}, bf16[192,768]{1,0:T(8,128)(2,1)S(1)}, u32[]{:S(2)}, u32[]{:S(2)}) collective-permute-start(bf16[192,768]{1,0:T(8,128)(2,1)S(1)} %get-tuple-element.329), channel_id=1, source_target_pairs={{0,4},{8,0},{16,8},{24,16},{28,24},{20,28},{12,20},{4,12},{1,5},{9... | collective-permute-start | bytes 884744 | tf_op jit(solution)/shard_map/ppermute | solution.py:988
  281.5 22.2 %collective-permute-start.30 = (bf16[192,768]{1,0:T(8,128)(2,1)S(1)}, bf16[192,768]{1,0:T(8,128)(2,1)S(1)}, u32[]{:S(2)}, u32[]{:S(2)}) collective-permute-start(bf16[192,768]{1,0:T(8,128)(2,1)S(1)} %collective-permute-done.26), channel_id=1, source_target_pairs={{0,8},{8,16},{16,24},{24,28},{28,20},{20,12},{12,4},{4,0},{1,9},{9... | collective-permute-start | bytes 884744 | tf_op jit(solution)/shard_map/ppermute | solution.py:988
  281.6 22.1 %collective-permute-start.31 = (bf16[192,768]{1,0:T(8,128)(2,1)S(1)}, bf16[192,768]{1,0:T(8,128)(2,1)S(1)}, u32[]{:S(2)}, u32[]{:S(2)}) collective-permute-start(bf16[192,768]{1,0:T(8,128)(2,1)S(1)} %collective-permute-done.27), channel_id=1, source_target_pairs={{0,4},{8,0},{16,8},{24,16},{28,24},{20,28},{12,20},{4,12},{1,5},{9... | collective-permute-start | bytes 884744 | tf_op jit(solution)/shard_map/ppermute | solution.py:988
  318.9 24.5 %collective-permute-start.40 = (bf16[640,768]{1,0:T(8,128)(2,1)S(1)}, bf16[640,768]{1,0:T(8,128)(2,1)}, u32[]{:S(2)}, u32[]{:S(2)}) collective-permute-start(bf16[640,768]{1,0:T(8,128)(2,1)S(1)} %fusion.8), channel_id=1, source_target_pairs={{0,2},{1,3},{2,0},{3,1},{4,6},{5,7},{6,4},{7,5},{8,10},{9,11},{10,... | collective-permute-start | bytes 2949128 | tf_op jit(solution)/shard_map/ppermute | solution.py:1267
  320.7 22.7 %collective-permute-start.36 = (bf16[384,768]{1,0:T(8,128)(2,1)}, bf16[384,768]{1,0:T(8,128)(2,1)}, u32[]{:S(2)}, u32[]{:S(2)}) collective-permute-start(bf16[384,768]{1,0:T(8,128)(2,1)} %get-tuple-element.245), channel_id=1, source_target_pairs={{0,8},{8,16},{16,24},{24,28},{28,20},{20,12},{12,4},{4,0},{1,9},{9... | collective-permute-start | bytes 1769480 | tf_op jit(solution)/shard_map/ppermute | solution.py:988
  321.4 22.0 %collective-permute-start.37 = (bf16[384,768]{1,0:T(8,128)(2,1)}, bf16[384,768]{1,0:T(8,128)(2,1)}, u32[]{:S(2)}, u32[]{:S(2)}) collective-permute-start(bf16[384,768]{1,0:T(8,128)(2,1)} %get-tuple-element.246), channel_id=1, source_target_pairs={{0,4},{8,0},{16,8},{24,16},{28,24},{20,28},{12,20},{4,12},{1,5},{9... | collective-permute-start | bytes 1769480 | tf_op jit(solution)/shard_map/ppermute | solution.py:988
  322.8 19.8 %collective-permute-start.38 = (bf16[216,768]{1,0:T(8,128)(2,1)S(1)}, bf16[216,768]{1,0:T(8,128)(2,1)}, u32[]{:S(2)}, u32[]{:S(2)}) collective-permute-start(bf16[216,768]{1,0:T(8,128)(2,1)S(1)} %add_convert_fusion.2.refs_0_), channel_id=1, source_target_pairs={{0,8},{8,16},{16,24},{24,28},{28,20},{20,12},{12,4},{4,0},{1,9},{9... | collective-permute-start | bytes 995336 | tf_op jit(solution)/shard_map/ppermute | solution.py:988
  359.1 28.9 %collective-permute-start.41 = (bf16[384,768]{1,0:T(8,128)(2,1)S(1)}, bf16[384,768]{1,0:T(8,128)(2,1)}, u32[]{:S(2)}, u32[]{:S(2)}) collective-permute-start(bf16[384,768]{1,0:T(8,128)(2,1)S(1)} %get-tuple-element.254), channel_id=1, source_target_pairs={{0,8},{8,16},{16,24},{24,28},{28,20},{20,12},{12,4},{4,0},{1,9},{9... | collective-permute-start | bytes 1769480 | tf_op jit(solution)/shard_map/ppermute | solution.py:988
  359.1 28.9 %collective-permute-start.42 = (bf16[384,768]{1,0:T(8,128)(2,1)S(1)}, bf16[384,768]{1,0:T(8,128)(2,1)}, u32[]{:S(2)}, u32[]{:S(2)}) collective-permute-start(bf16[384,768]{1,0:T(8,128)(2,1)S(1)} %get-tuple-element.255), channel_id=1, source_target_pairs={{0,4},{8,0},{16,8},{24,16},{28,24},{20,28},{12,20},{4,12},{1,5},{9... | collective-permute-start | bytes 1769480 | tf_op jit(solution)/shard_map/ppermute | solution.py:988
  361.2 26.9 %collective-permute-start.47 = (bf16[216,768]{1,0:T(8,128)(2,1)}, bf16[216,768]{1,0:T(8,128)(2,1)}, u32[]{:S(2)}, u32[]{:S(2)}) collective-permute-start(bf16[216,768]{1,0:T(8,128)(2,1)} %collective-permute-done.38.refs_7_), channel_id=1, source_target_pairs={{0,8},{8,16},{16,24},{24,28},{28,20},{20,12},{12,4},{4,0},{1,9},{9... | collective-permute-start | bytes 995336 | tf_op jit(solution)/shard_map/ppermute | solution.py:988
  363.7 24.4 %collective-permute-start.48 = (bf16[216,768]{1,0:T(8,128)(2,1)}, bf16[216,768]{1,0:T(8,128)(2,1)}, u32[]{:S(2)}, u32[]{:S(2)}) collective-permute-start(bf16[216,768]{1,0:T(8,128)(2,1)} %collective-permute-done.39.refs_1_), channel_id=1, source_target_pairs={{0,4},{8,0},{16,8},{24,16},{28,24},{20,28},{12,20},{4,12},{1,5},{9... | collective-permute-start | bytes 995336 | tf_op jit(solution)/shard_map/ppermute | solution.py:988
  392.7 30.3 %collective-permute-start.51 = (bf16[384,768]{1,0:T(8,128)(2,1)S(1)}, bf16[384,768]{1,0:T(8,128)(2,1)}, u32[]{:S(2)}, u32[]{:S(2)}) collective-permute-start(bf16[384,768]{1,0:T(8,128)(2,1)S(1)} %get-tuple-element.269), channel_id=1, source_target_pairs={{0,8},{8,16},{16,24},{24,28},{28,20},{20,12},{12,4},{4,0},{1,9},{9... | collective-permute-start | bytes 1769480 | tf_op jit(solution)/shard_map/ppermute | solution.py:988
  392.9 30.1 %collective-permute-start.52 = (bf16[384,768]{1,0:T(8,128)(2,1)S(1)}, bf16[384,768]{1,0:T(8,128)(2,1)}, u32[]{:S(2)}, u32[]{:S(2)}) collective-permute-start(bf16[384,768]{1,0:T(8,128)(2,1)S(1)} %get-tuple-element.270), channel_id=1, source_target_pairs={{0,4},{8,0},{16,8},{24,16},{28,24},{20,28},{12,20},{4,12},{1,5},{9... | collective-permute-start | bytes 1769480 | tf_op jit(solution)/shard_map/ppermute | solution.py:988
  (99 other events, 1152.4 us)
Sparse Core Ops, SparseCore 0:
  78.0 49.3 all-gather.2
  184.9 108.9 reduce-scatter.1
